TPU v7x, 128 devices: a whole 4x4x4 slice. The times are simulated.
128 devices in a mesh: pts: 128 (over x, z, y, core).
Axes of the slice: x: 4, y: 4, z: 4, core: 2. Of those that a mesh axis runs over, the one named last changes fastest.
Arguments:
- positions: float32 [3, 1048576], P(None, 'pts'), as said below
- noise: float32 [1048576], P('pts'), may hold values from 1 to 4
- right_side: float32 [32, 1048576], P(None, 'pts')
- pairs: int32 [2, 131072], P(None, 'pts'), may hold values from 0 to 8191, as said below
- counts: int32 [128], P('pts'), may hold values from 64 to 1024, as said below
Outputs:
- solution_field: float32 [32, 1048576], P(None, 'pts')
- residual: float32 [32, 1048576], P(None, 'pts')
Inputs may be any that keep to these rules, and one draw needn't show every extreme that they name: `pairs`: device d's slots are d * 1024 to (d + 1) * 1024 - 1. In every slot the row block is one of the 64 blocks device d holds. In a used slot the column block lies 0 to 15 blocks after the row block; used slots come in non-decreasing order of row block, every block's pair with itself is used, and no pair is used twice. Unused slots name a block of device d twice. counts[d] is the number of used slots of device d; some device uses all 1024. `positions`: points of two blocks that no used slot pairs are one unit or more apart.
All inputs are finite; a program needn't handle non-finite values.
Results may differ from a plain program's by a relative error of at most 0.0004.
Values sent between devices are 32-bit elements; how exact they have to be, the bound alone decides.
A program may use at most 64 MiB of HBM per device.

v0:
```python
import math

import jax
import jax.numpy as jnp
from jax import lax
from jax.sharding import PartitionSpec as P

BLK = 128
REACH = 15
ITERS = 2


def passed_along(shard, axis, by):
    count = lax.axis_size(axis)
    pairs = [(i, i + by) for i in range(count) if 0 <= i + by < count]
    return lax.ppermute(shard, axis, pairs)


def wendland(left, right):
    total = jnp.zeros((left.shape[0], left.shape[2], right.shape[2]), jnp.float32)
    for coord in range(3):
        delta = left[:, coord, :, None] - right[:, coord, None, :]
        total = total + delta * delta
    dist = jnp.sqrt(total)
    reach = jnp.maximum(1.0 - dist, 0.0)
    return reach * reach * (reach * reach) * (4.0 * dist + 1.0)


def tile_products(pos_blocks, val_blocks, rows, cols, live):
    kern = wendland(jnp.take(pos_blocks, rows, axis=0), jnp.take(pos_blocks, cols, axis=0))
    front = jnp.einsum(
        "gij,gfj->gfi", kern, jnp.take(val_blocks, cols, axis=0), precision=lax.Precision.HIGHEST
    )
    back = jnp.einsum(
        "gij,gfi->gfj", kern, jnp.take(val_blocks, rows, axis=0), precision=lax.Precision.HIGHEST
    )
    keep = live.astype(jnp.float32)
    cross = keep * (rows != cols).astype(jnp.float32)
    return (front * keep[:, None, None], back * cross[:, None, None])


def spread(terms, slots, places_count):
    places = (slots[:, None] == jnp.arange(places_count, dtype=jnp.int32)[None, :]).astype(
        jnp.float32
    )
    flat = terms.reshape(terms.shape[0], -1)
    summed = jnp.dot(places.T, flat, precision=lax.Precision.HIGH)
    return summed.reshape((places_count,) + terms.shape[1:])


def to_blocks(field):
    return field.reshape(field.shape[0], field.shape[1] // BLK, BLK).transpose(1, 0, 2)


def frame_sums(left, right):
    return jnp.sum(left * right, axis=(0, 2))


def squares(residual):
    return lax.psum(frame_sums(residual, residual), "pts")


def body(positions, noise, right_side, pairs, counts):
    nblocks = positions.shape[1] // BLK
    slots_dev = pairs.shape[1]
    group = math.gcd(slots_dev, 128)
    base = lax.axis_index("pts") * nblocks
    count = counts[0]
    own_pos = to_blocks(positions)
    noise_blocks = noise.reshape(nblocks, BLK)[:, None, :]
    lanes = jnp.arange(group, dtype=jnp.int32)
    next_pos = passed_along(positions[:, : REACH * BLK], "pts", -1)
    ext_pos = jnp.concatenate([own_pos, to_blocks(next_pos)], axis=0)
    extent = nblocks + REACH
    local = jnp.clip(pairs - base, 0, extent - 1)
    right_blocks = to_blocks(right_side)
    solution_field = jnp.zeros_like(right_blocks)
    residual = right_blocks
    direction = right_blocks
    norm_now = squares(residual)
    for step_index in range(ITERS):
        following = passed_along(direction[:REACH], "pts", -1)
        ext_vals = jnp.concatenate([direction, following], axis=0)

        def step(index, total):
            chosen = lax.dynamic_slice_in_dim(local, index * group, group, 1)
            rows, cols = (chosen[0], chosen[1])
            live = index * group + lanes < count
            front, back = tile_products(ext_pos, ext_vals, rows, cols, live)
            terms = jnp.concatenate([front, back], axis=0)
            return total + spread(terms, jnp.concatenate([rows, cols]), extent)

        start = jnp.zeros((extent,) + direction.shape[1:], jnp.float32)
        total = lax.fori_loop(0, slots_dev // group, step, start)
        returned = passed_along(total[nblocks:], "pts", 1)
        padded = jnp.concatenate(
            [returned, jnp.zeros((nblocks - REACH,) + direction.shape[1:], jnp.float32)], axis=0
        )
        image = total[:nblocks] + padded + noise_blocks * direction
        curve = lax.psum(frame_sums(direction, image), "pts")
        alpha = norm_now / curve
        solution_field = solution_field + alpha[None, :, None] * direction
        residual = residual - alpha[None, :, None] * image
        norm_next = squares(residual)
        direction = residual + (norm_next / norm_now)[None, :, None] * direction
        norm_now = norm_next
    width = right_side.shape[1]
    frames = right_side.shape[0]
    solution_out = solution_field.transpose(1, 0, 2).reshape(frames, width)
    residual_out = residual.transpose(1, 0, 2).reshape(frames, width)
    return (solution_out, residual_out)


def solution(mesh):
    in_specs = (P(None, "pts"), P("pts"), P(None, "pts"), P(None, "pts"), P("pts"))
    out_specs = (P(None, "pts"), P(None, "pts"))
    return jax.shard_map(body, mesh=mesh, in_specs=in_specs, out_specs=out_specs, check_vma=False)
```

profile of v0, /device:TPU:1, one launch (start us, length us, event | category | flops | bytes accessed | tf_op | source)
XLA Modules:
  0.0 1274.5 jit_solution(8502156105347741004)
XLA Ops:
  12.9 492.7 %while.28 = (s32[]{:T(128)}, f32[79,32,128]{2,0,1:T(8,128)S(1)}, s32[2,1024]{1,0:T(2,128)S(1)}, f32[79,32,128]{2,1,0:T(8,128)S(1)}, f32[79,3,128]{2,1,0:T(4,128)...) while((s32[]{:T(128)}, f32[79,32,128]{2,0,1:T(8,128)S(1)}, ...), condition=%wide.region_3.6_spmd.clone, body=%wide.region_2.5_spmd.clone.sunk | while | flops 2174468096 | bytes 60284864 | solution.py:94
  17.9 21.0 %fusion.119 = f32[128,32,128]{2,1,0:T(8,128)} fusion(f32[128,128]{1,0:T(8,128)S(1)} %bitcast.178, f32[128,128]{1,0:T(8,128)S(1)} %bitcast.190, f32[128,128]{1,0:T(8,128)S(1)} %bitcast.180, f32[128,128]{1,0:T(8,128)S(1)} %bitcast.192, f32[128,128]{1,0:T(8,128)S(1)} %bitcast.176, f32[128,128]{1,0:T(8,128)S(1)} %bitcast.188, ...), kind=kOutput, calls=%fused_computation.35.clone.1 | convolution fusion | flops 837812224 | bytes 4588160 | tf_op jit(solution)/shard_map/while/body/eval_jaxpr/gij,gfj->gfi/dot_general | solution.py:31
  41.0 17.5 %fusion.118 = f32[128,32,128]{2,1,0:T(8,128)S(1)} fusion(f32[128,128]{1,0:T(8,128)S(1)} %bitcast.179, f32[128,128]{1,0:T(8,128)S(1)} %bitcast.191, f32[128,128]{1,0:T(8,128)S(1)} %bitcast.181, f32[128,128]{1,0:T(8,128)S(1)} %bitcast.193, f32[128,128]{1,0:T(8,128)S(1)} %bitcast.177, f32[128,128]{1,0:T(8,128)S(1)} %bitcast.189, ...), kind=kOutput, calls=%fused_computation.36.clone.1 | convolution fusion | flops 837812224 | bytes 4588160 | tf_op jit(solution)/shard_map/while/body/eval_jaxpr/gij,gfi->gfj/dot_general | solution.py:34
  79.5 21.0 %fusion.119 = f32[128,32,128]{2,1,0:T(8,128)} fusion(f32[128,128]{1,0:T(8,128)S(1)} %bitcast.178, f32[128,128]{1,0:T(8,128)S(1)} %bitcast.190, f32[128,128]{1,0:T(8,128)S(1)} %bitcast.180, f32[128,128]{1,0:T(8,128)S(1)} %bitcast.192, f32[128,128]{1,0:T(8,128)S(1)} %bitcast.176, f32[128,128]{1,0:T(8,128)S(1)} %bitcast.188, ...), kind=kOutput, calls=%fused_computation.35.clone.1 | convolution fusion | flops 837812224 | bytes 4588160 | tf_op jit(solution)/shard_map/while/body/eval_jaxpr/gij,gfj->gfi/dot_general | solution.py:31
  102.6 17.5 %fusion.118 = f32[128,32,128]{2,1,0:T(8,128)S(1)} fusion(f32[128,128]{1,0:T(8,128)S(1)} %bitcast.179, f32[128,128]{1,0:T(8,128)S(1)} %bitcast.191, f32[128,128]{1,0:T(8,128)S(1)} %bitcast.181, f32[128,128]{1,0:T(8,128)S(1)} %bitcast.193, f32[128,128]{1,0:T(8,128)S(1)} %bitcast.177, f32[128,128]{1,0:T(8,128)S(1)} %bitcast.189, ...), kind=kOutput, calls=%fused_computation.36.clone.1 | convolution fusion | flops 837812224 | bytes 4588160 | tf_op jit(solution)/shard_map/while/body/eval_jaxpr/gij,gfi->gfj/dot_general | solution.py:34
  120.6 5.7 copy.26
  141.0 21.0 %fusion.119 = f32[128,32,128]{2,1,0:T(8,128)} fusion(f32[128,128]{1,0:T(8,128)S(1)} %bitcast.178, f32[128,128]{1,0:T(8,128)S(1)} %bitcast.190, f32[128,128]{1,0:T(8,128)S(1)} %bitcast.180, f32[128,128]{1,0:T(8,128)S(1)} %bitcast.192, f32[128,128]{1,0:T(8,128)S(1)} %bitcast.176, f32[128,128]{1,0:T(8,128)S(1)} %bitcast.188, ...), kind=kOutput, calls=%fused_computation.35.clone.1 | convolution fusion | flops 837812224 | bytes 4588160 | tf_op jit(solution)/shard_map/while/body/eval_jaxpr/gij,gfj->gfi/dot_general | solution.py:31
  164.2 17.5 %fusion.118 = f32[128,32,128]{2,1,0:T(8,128)S(1)} fusion(f32[128,128]{1,0:T(8,128)S(1)} %bitcast.179, f32[128,128]{1,0:T(8,128)S(1)} %bitcast.191, f32[128,128]{1,0:T(8,128)S(1)} %bitcast.181, f32[128,128]{1,0:T(8,128)S(1)} %bitcast.193, f32[128,128]{1,0:T(8,128)S(1)} %bitcast.177, f32[128,128]{1,0:T(8,128)S(1)} %bitcast.189, ...), kind=kOutput, calls=%fused_computation.36.clone.1 | convolution fusion | flops 837812224 | bytes 4588160 | tf_op jit(solution)/shard_map/while/body/eval_jaxpr/gij,gfi->gfj/dot_general | solution.py:34
  182.2 5.7 copy.26
  202.6 21.0 %fusion.119 = f32[128,32,128]{2,1,0:T(8,128)} fusion(f32[128,128]{1,0:T(8,128)S(1)} %bitcast.178, f32[128,128]{1,0:T(8,128)S(1)} %bitcast.190, f32[128,128]{1,0:T(8,128)S(1)} %bitcast.180, f32[128,128]{1,0:T(8,128)S(1)} %bitcast.192, f32[128,128]{1,0:T(8,128)S(1)} %bitcast.176, f32[128,128]{1,0:T(8,128)S(1)} %bitcast.188, ...), kind=kOutput, calls=%fused_computation.35.clone.1 | convolution fusion | flops 837812224 | bytes 4588160 | tf_op jit(solution)/shard_map/while/body/eval_jaxpr/gij,gfj->gfi/dot_general | solution.py:31
  225.8 17.5 %fusion.118 = f32[128,32,128]{2,1,0:T(8,128)S(1)} fusion(f32[128,128]{1,0:T(8,128)S(1)} %bitcast.179, f32[128,128]{1,0:T(8,128)S(1)} %bitcast.191, f32[128,128]{1,0:T(8,128)S(1)} %bitcast.181, f32[128,128]{1,0:T(8,128)S(1)} %bitcast.193, f32[128,128]{1,0:T(8,128)S(1)} %bitcast.177, f32[128,128]{1,0:T(8,128)S(1)} %bitcast.189, ...), kind=kOutput, calls=%fused_computation.36.clone.1 | convolution fusion | flops 837812224 | bytes 4588160 | tf_op jit(solution)/shard_map/while/body/eval_jaxpr/gij,gfi->gfj/dot_general | solution.py:34
  243.7 5.7 copy.26
  264.2 21.0 %fusion.119 = f32[128,32,128]{2,1,0:T(8,128)} fusion(f32[128,128]{1,0:T(8,128)S(1)} %bitcast.178, f32[128,128]{1,0:T(8,128)S(1)} %bitcast.190, f32[128,128]{1,0:T(8,128)S(1)} %bitcast.180, f32[128,128]{1,0:T(8,128)S(1)} %bitcast.192, f32[128,128]{1,0:T(8,128)S(1)} %bitcast.176, f32[128,128]{1,0:T(8,128)S(1)} %bitcast.188, ...), kind=kOutput, calls=%fused_computation.35.clone.1 | convolution fusion | flops 837812224 | bytes 4588160 | tf_op jit(solution)/shard_map/while/body/eval_jaxpr/gij,gfj->gfi/dot_general | solution.py:31
  287.3 17.5 %fusion.118 = f32[128,32,128]{2,1,0:T(8,128)S(1)} fusion(f32[128,128]{1,0:T(8,128)S(1)} %bitcast.179, f32[128,128]{1,0:T(8,128)S(1)} %bitcast.191, f32[128,128]{1,0:T(8,128)S(1)} %bitcast.181, f32[128,128]{1,0:T(8,128)S(1)} %bitcast.193, f32[128,128]{1,0:T(8,128)S(1)} %bitcast.177, f32[128,128]{1,0:T(8,128)S(1)} %bitcast.189, ...), kind=kOutput, calls=%fused_computation.36.clone.1 | convolution fusion | flops 837812224 | bytes 4588160 | tf_op jit(solution)/shard_map/while/body/eval_jaxpr/gij,gfi->gfj/dot_general | solution.py:34
  325.8 21.0 %fusion.119 = f32[128,32,128]{2,1,0:T(8,128)} fusion(f32[128,128]{1,0:T(8,128)S(1)} %bitcast.178, f32[128,128]{1,0:T(8,128)S(1)} %bitcast.190, f32[128,128]{1,0:T(8,128)S(1)} %bitcast.180, f32[128,128]{1,0:T(8,128)S(1)} %bitcast.192, f32[128,128]{1,0:T(8,128)S(1)} %bitcast.176, f32[128,128]{1,0:T(8,128)S(1)} %bitcast.188, ...), kind=kOutput, calls=%fused_computation.35.clone.1 | convolution fusion | flops 837812224 | bytes 4588160 | tf_op jit(solution)/shard_map/while/body/eval_jaxpr/gij,gfj->gfi/dot_general | solution.py:31
  348.9 17.5 %fusion.118 = f32[128,32,128]{2,1,0:T(8,128)S(1)} fusion(f32[128,128]{1,0:T(8,128)S(1)} %bitcast.179, f32[128,128]{1,0:T(8,128)S(1)} %bitcast.191, f32[128,128]{1,0:T(8,128)S(1)} %bitcast.181, f32[128,128]{1,0:T(8,128)S(1)} %bitcast.193, f32[128,128]{1,0:T(8,128)S(1)} %bitcast.177, f32[128,128]{1,0:T(8,128)S(1)} %bitcast.189, ...), kind=kOutput, calls=%fused_computation.36.clone.1 | convolution fusion | flops 837812224 | bytes 4588160 | tf_op jit(solution)/shard_map/while/body/eval_jaxpr/gij,gfi->gfj/dot_general | solution.py:34
  387.4 21.0 %fusion.119 = f32[128,32,128]{2,1,0:T(8,128)} fusion(f32[128,128]{1,0:T(8,128)S(1)} %bitcast.178, f32[128,128]{1,0:T(8,128)S(1)} %bitcast.190, f32[128,128]{1,0:T(8,128)S(1)} %bitcast.180, f32[128,128]{1,0:T(8,128)S(1)} %bitcast.192, f32[128,128]{1,0:T(8,128)S(1)} %bitcast.176, f32[128,128]{1,0:T(8,128)S(1)} %bitcast.188, ...), kind=kOutput, calls=%fused_computation.35.clone.1 | convolution fusion | flops 837812224 | bytes 4588160 | tf_op jit(solution)/shard_map/while/body/eval_jaxpr/gij,gfj->gfi/dot_general | solution.py:31
  410.5 17.5 %fusion.118 = f32[128,32,128]{2,1,0:T(8,128)S(1)} fusion(f32[128,128]{1,0:T(8,128)S(1)} %bitcast.179, f32[128,128]{1,0:T(8,128)S(1)} %bitcast.191, f32[128,128]{1,0:T(8,128)S(1)} %bitcast.181, f32[128,128]{1,0:T(8,128)S(1)} %bitcast.193, f32[128,128]{1,0:T(8,128)S(1)} %bitcast.177, f32[128,128]{1,0:T(8,128)S(1)} %bitcast.189, ...), kind=kOutput, calls=%fused_computation.36.clone.1 | convolution fusion | flops 837812224 | bytes 4588160 | tf_op jit(solution)/shard_map/while/body/eval_jaxpr/gij,gfi->gfj/dot_general | solution.py:34
  449.0 21.0 %fusion.119 = f32[128,32,128]{2,1,0:T(8,128)} fusion(f32[128,128]{1,0:T(8,128)S(1)} %bitcast.178, f32[128,128]{1,0:T(8,128)S(1)} %bitcast.190, f32[128,128]{1,0:T(8,128)S(1)} %bitcast.180, f32[128,128]{1,0:T(8,128)S(1)} %bitcast.192, f32[128,128]{1,0:T(8,128)S(1)} %bitcast.176, f32[128,128]{1,0:T(8,128)S(1)} %bitcast.188, ...), kind=kOutput, calls=%fused_computation.35.clone.1 | convolution fusion | flops 837812224 | bytes 4588160 | tf_op jit(solution)/shard_map/while/body/eval_jaxpr/gij,gfj->gfi/dot_general | solution.py:31
  472.1 17.5 %fusion.118 = f32[128,32,128]{2,1,0:T(8,128)S(1)} fusion(f32[128,128]{1,0:T(8,128)S(1)} %bitcast.179, f32[128,128]{1,0:T(8,128)S(1)} %bitcast.191, f32[128,128]{1,0:T(8,128)S(1)} %bitcast.181, f32[128,128]{1,0:T(8,128)S(1)} %bitcast.193, f32[128,128]{1,0:T(8,128)S(1)} %bitcast.177, f32[128,128]{1,0:T(8,128)S(1)} %bitcast.189, ...), kind=kOutput, calls=%fused_computation.36.clone.1 | convolution fusion | flops 837812224 | bytes 4588160 | tf_op jit(solution)/shard_map/while/body/eval_jaxpr/gij,gfi->gfj/dot_general | solution.py:34
  512.7 73.7 %all-reduce.2 = (f32[32]{0:T(128)S(1)}, f32[32]{0:T(128)S(1)}) all-reduce(f32[32]{0:T(128)S(1)} %get-tuple-element.313, f32[32]{0:T(128)S(1)} %get-tuple-element.312), channel_id=1, replica_groups=mesh['pts'=128] {'pts'}, use_global_device_ids=true, to_apply=%region_1.2 | all-reduce | flops 64 | bytes 512 | tf_op jit(solution)/shard_map/psum | solution.py:60
  588.2 64.1 %psum.30 = f32[32]{0:T(128)S(1)} all-reduce(f32[32]{0:T(128)S(1)} %multiply_reduce_fusion.1), channel_id=1, replica_groups=mesh['pts'=128] {'pts'}, use_global_device_ids=true, to_apply=%region_7.10 | all-reduce | flops 32 | bytes 256 | tf_op jit(solution)/shard_map/psum | solution.py:60
  663.1 529.7 %while.29 = (s32[]{:T(128)}, f32[79,32,128]{2,0,1:T(8,128)}, s32[2,1024]{1,0:T(2,128)}, f32[79,32,128]{2,1,0:T(8,128)S(1)}, f32[79,3,128]{2,1,0:T(4,128)S(1)}, /...) while((s32[]{:T(128)}, f32[79,32,128]{2,0,1:T(8,128)}, s32[2,1024]{1,0:T(2,128)}, ...), condition=%wide.region_9.12_spmd.clone, body=%wide.region_8.11_spmd.clone.sunk | while | flops 2174468096 | bytes 60310604 | solution.py:94
  671.6 21.0 %fusion.127 = f32[128,32,128]{2,1,0:T(8,128)} fusion(f32[128,128]{1,0:T(8,128)S(1)} %bitcast.184, f32[128,128]{1,0:T(8,128)S(1)} %bitcast.196, f32[128,128]{1,0:T(8,128)S(1)} %bitcast.186, f32[128,128]{1,0:T(8,128)S(1)} %bitcast.198, f32[128,128]{1,0:T(8,128)S(1)} %bitcast.182, f32[128,128]{1,0:T(8,128)S(1)} %bitcast.194, ...), kind=kOutput, calls=%fused_computation.93.clone.1 | convolution fusion | flops 837812224 | bytes 4588160 | tf_op jit(solution)/shard_map/while/body/eval_jaxpr/gij,gfj->gfi/dot_general | solution.py:31
  695.0 17.5 %fusion.126 = f32[128,32,128]{2,1,0:T(8,128)S(1)} fusion(f32[128,128]{1,0:T(8,128)S(1)} %bitcast.185, f32[128,128]{1,0:T(8,128)S(1)} %bitcast.197, f32[128,128]{1,0:T(8,128)S(1)} %bitcast.187, f32[128,128]{1,0:T(8,128)S(1)} %bitcast.199, f32[128,128]{1,0:T(8,128)S(1)} %bitcast.183, f32[128,128]{1,0:T(8,128)S(1)} %bitcast.195, ...), kind=kOutput, calls=%fused_computation.94.clone.1 | convolution fusion | flops 837812224 | bytes 4588160 | tf_op jit(solution)/shard_map/while/body/eval_jaxpr/gij,gfi->gfj/dot_general | solution.py:34
  712.9 5.8 copy.28
  737.4 21.0 %fusion.127 = f32[128,32,128]{2,1,0:T(8,128)} fusion(f32[128,128]{1,0:T(8,128)S(1)} %bitcast.184, f32[128,128]{1,0:T(8,128)S(1)} %bitcast.196, f32[128,128]{1,0:T(8,128)S(1)} %bitcast.186, f32[128,128]{1,0:T(8,128)S(1)} %bitcast.198, f32[128,128]{1,0:T(8,128)S(1)} %bitcast.182, f32[128,128]{1,0:T(8,128)S(1)} %bitcast.194, ...), kind=kOutput, calls=%fused_computation.93.clone.1 | convolution fusion | flops 837812224 | bytes 4588160 | tf_op jit(solution)/shard_map/while/body/eval_jaxpr/gij,gfj->gfi/dot_general | solution.py:31
  760.8 17.5 %fusion.126 = f32[128,32,128]{2,1,0:T(8,128)S(1)} fusion(f32[128,128]{1,0:T(8,128)S(1)} %bitcast.185, f32[128,128]{1,0:T(8,128)S(1)} %bitcast.197, f32[128,128]{1,0:T(8,128)S(1)} %bitcast.187, f32[128,128]{1,0:T(8,128)S(1)} %bitcast.199, f32[128,128]{1,0:T(8,128)S(1)} %bitcast.183, f32[128,128]{1,0:T(8,128)S(1)} %bitcast.195, ...), kind=kOutput, calls=%fused_computation.94.clone.1 | convolution fusion | flops 837812224 | bytes 4588160 | tf_op jit(solution)/shard_map/while/body/eval_jaxpr/gij,gfi->gfj/dot_general | solution.py:34
  778.8 5.8 copy.28
  803.7 21.0 %fusion.127 = f32[128,32,128]{2,1,0:T(8,128)} fusion(f32[128,128]{1,0:T(8,128)S(1)} %bitcast.184, f32[128,128]{1,0:T(8,128)S(1)} %bitcast.196, f32[128,128]{1,0:T(8,128)S(1)} %bitcast.186, f32[128,128]{1,0:T(8,128)S(1)} %bitcast.198, f32[128,128]{1,0:T(8,128)S(1)} %bitcast.182, f32[128,128]{1,0:T(8,128)S(1)} %bitcast.194, ...), kind=kOutput, calls=%fused_computation.93.clone.1 | convolution fusion | flops 837812224 | bytes 4588160 | tf_op jit(solution)/shard_map/while/body/eval_jaxpr/gij,gfj->gfi/dot_general | solution.py:31
  827.1 17.5 %fusion.126 = f32[128,32,128]{2,1,0:T(8,128)S(1)} fusion(f32[128,128]{1,0:T(8,128)S(1)} %bitcast.185, f32[128,128]{1,0:T(8,128)S(1)} %bitcast.197, f32[128,128]{1,0:T(8,128)S(1)} %bitcast.187, f32[128,128]{1,0:T(8,128)S(1)} %bitcast.199, f32[128,128]{1,0:T(8,128)S(1)} %bitcast.183, f32[128,128]{1,0:T(8,128)S(1)} %bitcast.195, ...), kind=kOutput, calls=%fused_computation.94.clone.1 | convolution fusion | flops 837812224 | bytes 4588160 | tf_op jit(solution)/shard_map/while/body/eval_jaxpr/gij,gfi->gfj/dot_general | solution.py:34
  845.1 5.8 copy.28
  869.9 21.0 %fusion.127 = f32[128,32,128]{2,1,0:T(8,128)} fusion(f32[128,128]{1,0:T(8,128)S(1)} %bitcast.184, f32[128,128]{1,0:T(8,128)S(1)} %bitcast.196, f32[128,128]{1,0:T(8,128)S(1)} %bitcast.186, f32[128,128]{1,0:T(8,128)S(1)} %bitcast.198, f32[128,128]{1,0:T(8,128)S(1)} %bitcast.182, f32[128,128]{1,0:T(8,128)S(1)} %bitcast.194, ...), kind=kOutput, calls=%fused_computation.93.clone.1 | convolution fusion | flops 837812224 | bytes 4588160 | tf_op jit(solution)/shard_map/while/body/eval_jaxpr/gij,gfj->gfi/dot_general | solution.py:31
  893.3 17.5 %fusion.126 = f32[128,32,128]{2,1,0:T(8,128)S(1)} fusion(f32[128,128]{1,0:T(8,128)S(1)} %bitcast.185, f32[128,128]{1,0:T(8,128)S(1)} %bitcast.197, f32[128,128]{1,0:T(8,128)S(1)} %bitcast.187, f32[128,128]{1,0:T(8,128)S(1)} %bitcast.199, f32[128,128]{1,0:T(8,128)S(1)} %bitcast.183, f32[128,128]{1,0:T(8,128)S(1)} %bitcast.195, ...), kind=kOutput, calls=%fused_computation.94.clone.1 | convolution fusion | flops 837812224 | bytes 4588160 | tf_op jit(solution)/shard_map/while/body/eval_jaxpr/gij,gfi->gfj/dot_general | solution.py:34
  911.3 5.8 copy.28
  936.2 21.0 %fusion.127 = f32[128,32,128]{2,1,0:T(8,128)} fusion(f32[128,128]{1,0:T(8,128)S(1)} %bitcast.184, f32[128,128]{1,0:T(8,128)S(1)} %bitcast.196, f32[128,128]{1,0:T(8,128)S(1)} %bitcast.186, f32[128,128]{1,0:T(8,128)S(1)} %bitcast.198, f32[128,128]{1,0:T(8,128)S(1)} %bitcast.182, f32[128,128]{1,0:T(8,128)S(1)} %bitcast.194, ...), kind=kOutput, calls=%fused_computation.93.clone.1 | convolution fusion | flops 837812224 | bytes 4588160 | tf_op jit(solution)/shard_map/while/body/eval_jaxpr/gij,gfj->gfi/dot_general | solution.py:31
  959.6 17.5 %fusion.126 = f32[128,32,128]{2,1,0:T(8,128)S(1)} fusion(f32[128,128]{1,0:T(8,128)S(1)} %bitcast.185, f32[128,128]{1,0:T(8,128)S(1)} %bitcast.197, f32[128,128]{1,0:T(8,128)S(1)} %bitcast.187, f32[128,128]{1,0:T(8,128)S(1)} %bitcast.199, f32[128,128]{1,0:T(8,128)S(1)} %bitcast.183, f32[128,128]{1,0:T(8,128)S(1)} %bitcast.195, ...), kind=kOutput, calls=%fused_computation.94.clone.1 | convolution fusion | flops 837812224 | bytes 4588160 | tf_op jit(solution)/shard_map/while/body/eval_jaxpr/gij,gfi->gfj/dot_general | solution.py:34
  977.5 5.8 copy.28
  1002.4 21.0 %fusion.127 = f32[128,32,128]{2,1,0:T(8,128)} fusion(f32[128,128]{1,0:T(8,128)S(1)} %bitcast.184, f32[128,128]{1,0:T(8,128)S(1)} %bitcast.196, f32[128,128]{1,0:T(8,128)S(1)} %bitcast.186, f32[128,128]{1,0:T(8,128)S(1)} %bitcast.198, f32[128,128]{1,0:T(8,128)S(1)} %bitcast.182, f32[128,128]{1,0:T(8,128)S(1)} %bitcast.194, ...), kind=kOutput, calls=%fused_computation.93.clone.1 | convolution fusion | flops 837812224 | bytes 4588160 | tf_op jit(solution)/shard_map/while/body/eval_jaxpr/gij,gfj->gfi/dot_general | solution.py:31
  1025.8 17.5 %fusion.126 = f32[128,32,128]{2,1,0:T(8,128)S(1)} fusion(f32[128,128]{1,0:T(8,128)S(1)} %bitcast.185, f32[128,128]{1,0:T(8,128)S(1)} %bitcast.197, f32[128,128]{1,0:T(8,128)S(1)} %bitcast.187, f32[128,128]{1,0:T(8,128)S(1)} %bitcast.199, f32[128,128]{1,0:T(8,128)S(1)} %bitcast.183, f32[128,128]{1,0:T(8,128)S(1)} %bitcast.195, ...), kind=kOutput, calls=%fused_computation.94.clone.1 | convolution fusion | flops 837812224 | bytes 4588160 | tf_op jit(solution)/shard_map/while/body/eval_jaxpr/gij,gfi->gfj/dot_general | solution.py:34
  1043.8 5.8 copy.28
  1068.6 21.0 %fusion.127 = f32[128,32,128]{2,1,0:T(8,128)} fusion(f32[128,128]{1,0:T(8,128)S(1)} %bitcast.184, f32[128,128]{1,0:T(8,128)S(1)} %bitcast.196, f32[128,128]{1,0:T(8,128)S(1)} %bitcast.186, f32[128,128]{1,0:T(8,128)S(1)} %bitcast.198, f32[128,128]{1,0:T(8,128)S(1)} %bitcast.182, f32[128,128]{1,0:T(8,128)S(1)} %bitcast.194, ...), kind=kOutput, calls=%fused_computation.93.clone.1 | convolution fusion | flops 837812224 | bytes 4588160 | tf_op jit(solution)/shard_map/while/body/eval_jaxpr/gij,gfj->gfi/dot_general | solution.py:31
  1092.0 17.5 %fusion.126 = f32[128,32,128]{2,1,0:T(8,128)S(1)} fusion(f32[128,128]{1,0:T(8,128)S(1)} %bitcast.185, f32[128,128]{1,0:T(8,128)S(1)} %bitcast.197, f32[128,128]{1,0:T(8,128)S(1)} %bitcast.187, f32[128,128]{1,0:T(8,128)S(1)} %bitcast.199, f32[128,128]{1,0:T(8,128)S(1)} %bitcast.183, f32[128,128]{1,0:T(8,128)S(1)} %bitcast.195, ...), kind=kOutput, calls=%fused_computation.94.clone.1 | convolution fusion | flops 837812224 | bytes 4588160 | tf_op jit(solution)/shard_map/while/body/eval_jaxpr/gij,gfi->gfj/dot_general | solution.py:34
  1110.0 5.8 copy.28
  1134.9 21.0 %fusion.127 = f32[128,32,128]{2,1,0:T(8,128)} fusion(f32[128,128]{1,0:T(8,128)S(1)} %bitcast.184, f32[128,128]{1,0:T(8,128)S(1)} %bitcast.196, f32[128,128]{1,0:T(8,128)S(1)} %bitcast.186, f32[128,128]{1,0:T(8,128)S(1)} %bitcast.198, f32[128,128]{1,0:T(8,128)S(1)} %bitcast.182, f32[128,128]{1,0:T(8,128)S(1)} %bitcast.194, ...), kind=kOutput, calls=%fused_computation.93.clone.1 | convolution fusion | flops 837812224 | bytes 4588160 | tf_op jit(solution)/shard_map/while/body/eval_jaxpr/gij,gfj->gfi/dot_general | solution.py:31
  1158.3 17.5 %fusion.126 = f32[128,32,128]{2,1,0:T(8,128)S(1)} fusion(f32[128,128]{1,0:T(8,128)S(1)} %bitcast.185, f32[128,128]{1,0:T(8,128)S(1)} %bitcast.197, f32[128,128]{1,0:T(8,128)S(1)} %bitcast.187, f32[128,128]{1,0:T(8,128)S(1)} %bitcast.199, f32[128,128]{1,0:T(8,128)S(1)} %bitcast.183, f32[128,128]{1,0:T(8,128)S(1)} %bitcast.195, ...), kind=kOutput, calls=%fused_computation.94.clone.1 | convolution fusion | flops 837812224 | bytes 4588160 | tf_op jit(solution)/shard_map/while/body/eval_jaxpr/gij,gfi->gfj/dot_general | solution.py:34
  1176.3 5.8 copy.28
  1200.8 68.1 %psum.31 = f32[32]{0:T(128)S(1)} all-reduce(f32[32]{0:T(128)S(1)} %multiply_reduce_fusion), channel_id=1, replica_groups=mesh['pts'=128] {'pts'}, use_global_device_ids=true, to_apply=%region_11.14 | all-reduce | flops 32 | bytes 256 | tf_op jit(solution)/shard_map/psum | solution.py:100
  (444 shorter events, 385.5 us)
Async XLA Ops:
  2.0 10.3 copy-start.4
  2.1 10.2 collective-permute-start
  6.2 5.2 collective-permute-start.1
  12.9 498.1 %copy-start.9 = (f32[8192]{0:T(1024)S(1)}, f32[8192]{0:T(1024)}, u32[]{:S(2)}) copy-start(f32[8192]{0:T(1024)} %param.14) | copy-start | bytes 98308
  41.0 17.5 %copy-start.2 = (f32[128,32,128]{2,1,0:T(8,128)S(1)}, f32[128,32,128]{2,1,0:T(8,128)}, u32[]{:S(2)}) copy-start(f32[128,32,128]{2,1,0:T(8,128)} %fusion.119) | copy-start | bytes 6291460 | tf_op jit(solution)/shard_map/while
  102.6 17.5 %copy-start.2 = (f32[128,32,128]{2,1,0:T(8,128)S(1)}, f32[128,32,128]{2,1,0:T(8,128)}, u32[]{:S(2)}) copy-start(f32[128,32,128]{2,1,0:T(8,128)} %fusion.119) | copy-start | bytes 6291460 | tf_op jit(solution)/shard_map/while
  164.2 17.5 %copy-start.2 = (f32[128,32,128]{2,1,0:T(8,128)S(1)}, f32[128,32,128]{2,1,0:T(8,128)}, u32[]{:S(2)}) copy-start(f32[128,32,128]{2,1,0:T(8,128)} %fusion.119) | copy-start | bytes 6291460 | tf_op jit(solution)/shard_map/while
  225.8 17.5 %copy-start.2 = (f32[128,32,128]{2,1,0:T(8,128)S(1)}, f32[128,32,128]{2,1,0:T(8,128)}, u32[]{:S(2)}) copy-start(f32[128,32,128]{2,1,0:T(8,128)} %fusion.119) | copy-start | bytes 6291460 | tf_op jit(solution)/shard_map/while
  287.3 17.5 %copy-start.2 = (f32[128,32,128]{2,1,0:T(8,128)S(1)}, f32[128,32,128]{2,1,0:T(8,128)}, u32[]{:S(2)}) copy-start(f32[128,32,128]{2,1,0:T(8,128)} %fusion.119) | copy-start | bytes 6291460 | tf_op jit(solution)/shard_map/while
  348.9 17.5 %copy-start.2 = (f32[128,32,128]{2,1,0:T(8,128)S(1)}, f32[128,32,128]{2,1,0:T(8,128)}, u32[]{:S(2)}) copy-start(f32[128,32,128]{2,1,0:T(8,128)} %fusion.119) | copy-start | bytes 6291460 | tf_op jit(solution)/shard_map/while
  410.5 17.5 %copy-start.2 = (f32[128,32,128]{2,1,0:T(8,128)S(1)}, f32[128,32,128]{2,1,0:T(8,128)}, u32[]{:S(2)}) copy-start(f32[128,32,128]{2,1,0:T(8,128)} %fusion.119) | copy-start | bytes 6291460 | tf_op jit(solution)/shard_map/while
  472.1 17.5 %copy-start.2 = (f32[128,32,128]{2,1,0:T(8,128)S(1)}, f32[128,32,128]{2,1,0:T(8,128)}, u32[]{:S(2)}) copy-start(f32[128,32,128]{2,1,0:T(8,128)} %fusion.119) | copy-start | bytes 6291460 | tf_op jit(solution)/shard_map/while
  505.6 147.0 %copy-start = (f32[79,32,128]{2,0,1:T(8,128)}, f32[79,32,128]{2,0,1:T(8,128)S(1)}, u32[]{:S(2)}) copy-start(f32[79,32,128]{2,0,1:T(8,128)S(1)} %get-tuple-element.252) | copy-start | bytes 3883012
  505.6 147.0 %copy-start.15 = (s32[2,1024]{1,0:T(2,128)}, s32[2,1024]{1,0:T(2,128)S(1)}, u32[]{:S(2)}) copy-start(s32[2,1024]{1,0:T(2,128)S(1)} %get-tuple-element.587) | copy-start | bytes 24580
  505.6 146.7 %copy-start.5 = (f32[4,8,64,128]{3,2,1,0:T(8,128)S(1)}, f32[4,8,64,128]{3,2,1,0:T(8,128)}, u32[]{:S(2)}) copy-start(f32[4,8,64,128]{3,2,1,0:T(8,128)} %copy-done.4) | copy-start | bytes 3145732
  505.6 5.4 collective-permute-start.2
  511.0 141.7 %copy-start.7 = (f32[15,32,128]{2,0,1:T(8,128)}, f32[15,32,128]{2,0,1:T(8,128)S(1)}, u32[]{:S(2)}) copy-start(f32[15,32,128]{2,0,1:T(8,128)S(1)} %collective-permute-done.2) | copy-start | bytes 737284
  586.4 76.2 %copy-start.16 = (f32[32]{0:T(128)}, f32[32]{0:T(128)S(1)}, u32[]{:S(2)}) copy-start(f32[32]{0:T(128)S(1)} %div.9) | copy-start | bytes 388
  652.3 10.8 copy-start.17
  653.6 7.7 collective-permute-start.3
  663.0 606.6 %copy-start.1 = (f32[79,32,128]{2,0,1:T(8,128)S(1)}, f32[79,32,128]{2,0,1:T(8,128)}, u32[]{:S(2)}) copy-start(f32[79,32,128]{2,0,1:T(8,128)} %copy-done) | copy-start | bytes 3883012
  663.0 606.6 %copy-start.8 = (f32[15,32,128]{2,0,1:T(8,128)S(1)}, f32[15,32,128]{2,0,1:T(8,128)}, u32[]{:S(2)}) copy-start(f32[15,32,128]{2,0,1:T(8,128)} %copy-done.7) | copy-start | bytes 737284
  667.7 3.9 copy-start.14
  695.0 17.5 %copy-start.3 = (f32[128,32,128]{2,1,0:T(8,128)S(1)}, f32[128,32,128]{2,1,0:T(8,128)}, u32[]{:S(2)}) copy-start(f32[128,32,128]{2,1,0:T(8,128)} %fusion.127) | copy-start | bytes 6291460 | tf_op jit(solution)/shard_map/while
  718.7 5.6 copy-start.11
  733.5 3.9 copy-start.14
  760.8 17.5 %copy-start.3 = (f32[128,32,128]{2,1,0:T(8,128)S(1)}, f32[128,32,128]{2,1,0:T(8,128)}, u32[]{:S(2)}) copy-start(f32[128,32,128]{2,1,0:T(8,128)} %fusion.127) | copy-start | bytes 6291460 | tf_op jit(solution)/shard_map/while
  784.6 5.6 copy-start.11
  799.8 3.9 copy-start.14
  827.1 17.5 %copy-start.3 = (f32[128,32,128]{2,1,0:T(8,128)S(1)}, f32[128,32,128]{2,1,0:T(8,128)}, u32[]{:S(2)}) copy-start(f32[128,32,128]{2,1,0:T(8,128)} %fusion.127) | copy-start | bytes 6291460 | tf_op jit(solution)/shard_map/while
  850.8 5.6 copy-start.11
  866.1 3.9 copy-start.14
  893.3 17.5 %copy-start.3 = (f32[128,32,128]{2,1,0:T(8,128)S(1)}, f32[128,32,128]{2,1,0:T(8,128)}, u32[]{:S(2)}) copy-start(f32[128,32,128]{2,1,0:T(8,128)} %fusion.127) | copy-start | bytes 6291460 | tf_op jit(solution)/shard_map/while
  917.1 5.6 copy-start.11
  932.3 3.9 copy-start.14
  959.6 17.5 %copy-start.3 = (f32[128,32,128]{2,1,0:T(8,128)S(1)}, f32[128,32,128]{2,1,0:T(8,128)}, u32[]{:S(2)}) copy-start(f32[128,32,128]{2,1,0:T(8,128)} %fusion.127) | copy-start | bytes 6291460 | tf_op jit(solution)/shard_map/while
  983.3 5.6 copy-start.11
  998.5 3.9 copy-start.14
  1023.4 2.4 copy-start.13
  1025.8 17.5 %copy-start.3 = (f32[128,32,128]{2,1,0:T(8,128)S(1)}, f32[128,32,128]{2,1,0:T(8,128)}, u32[]{:S(2)}) copy-start(f32[128,32,128]{2,1,0:T(8,128)} %fusion.127) | copy-start | bytes 6291460 | tf_op jit(solution)/shard_map/while
  1049.5 5.6 copy-start.11
  1064.8 3.9 copy-start.14
  1092.0 17.5 %copy-start.3 = (f32[128,32,128]{2,1,0:T(8,128)S(1)}, f32[128,32,128]{2,1,0:T(8,128)}, u32[]{:S(2)}) copy-start(f32[128,32,128]{2,1,0:T(8,128)} %fusion.127) | copy-start | bytes 6291460 | tf_op jit(solution)/shard_map/while
  1115.8 5.6 copy-start.11
  1131.0 3.9 copy-start.14
  1158.3 17.5 %copy-start.3 = (f32[128,32,128]{2,1,0:T(8,128)S(1)}, f32[128,32,128]{2,1,0:T(8,128)}, u32[]{:S(2)}) copy-start(f32[128,32,128]{2,1,0:T(8,128)} %fusion.127) | copy-start | bytes 6291460 | tf_op jit(solution)/shard_map/while
  1182.1 5.6 copy-start.11
  1193.7 5.2 collective-permute-start.4
  (24 other events, 28.3 us)
where the time goes:
time: 1280 us; the launch traced here: 1270 us
  matrix products  689 us (54%)
  local copies, waits for them, and re-layouts  295 us (23%)
  blocking collectives  206 us (16%)
  other arithmetic  55.4 us (4%)
  waiting for transfers between devices  13.9 us (1%)
    dot_general x16, matrix products, tile_products(): jnp.einsum('gij,gfj->gfi', kern, jnp.take(val_blocks, cols, axis=0), prec...  337 us
    dot_general x16, matrix products, tile_products(): jnp.einsum('gij,gfi->gfj', kern, jnp.take(val_blocks, rows, axis=0), prec...  280 us
    psum x2, blocking collectives, squares(): return lax.psum(frame_sums(residual, residual), 'pts')  138 us
    while x128, local copies, waits for them, and re-layouts  92.3 us
    dot_general x16, local copies, waits for them, and re-layouts, spread(): summed = jnp.dot(places.T, flat, precision=lax.Precision.HIGH)  90.1 us
    dot_general x16, matrix products, spread(): summed = jnp.dot(places.T, flat, precision=lax.Precision.HIGH)  72.6 us
    psum x1, blocking collectives, body(): curve = lax.psum(frame_sums(direction, image), 'pts')  68.1 us
    gather x16, local copies, waits for them, and re-layouts, tile_products(): jnp.take(val_blocks, rows, axis=0)  35.6 us
  transfers between devices with their start and end apart: 5, of which 4 were waited for; matrix products, arithmetic and copies ran while one was open for 0% of the time, Pallas kernels for 0%

commit v1 on v0

v1 whole, which is shorter than its diff:
```python
import functools

import jax
import jax.numpy as jnp
from jax import lax
from jax.experimental import pallas as pl
from jax.experimental.pallas import tpu as pltpu
from jax.sharding import PartitionSpec as P

SUP = 256
HALO = 8
FRAMES = 32
TINY = 1e-36
MESH = pl.DeviceIdType.MESH
VMEM = pl.BlockSpec(memory_space=pltpu.VMEM)
SMEM = pl.BlockSpec(memory_space=pltpu.SMEM)
GROUP = 8


def f32(shape):
    return jax.ShapeDtypeStruct(shape, jnp.float32)


def dot(left, right, dim):
    return lax.dot_general(
        left, right, (((1,), (dim,)), ((), ())), preferred_element_type=jnp.float32
    )


def lanes(index, width=SUP):
    return pl.ds(pl.multiple_of(index * width, width), width)


def spread_rows(pos_ref, rows_ref, rows):
    def step(a, _):
        turned = jnp.transpose(pos_ref[:, lanes(a)])
        for c in range(3):
            rows_ref[a, c] = jnp.broadcast_to(turned[:, c : c + 1], (SUP, 128))
        return 0

    lax.fori_loop(0, rows, step, 0)


def split(values):
    high = values.astype(jnp.bfloat16)
    low = (values - high.astype(jnp.float32)).astype(jnp.bfloat16)
    return jnp.concatenate([high, low], axis=0)


def sweep(span_ref, pos_ref, rows_ref, vals_ref, tiles, out_ref, rows):
    total = span_ref[rows]

    def following(a, c):
        last = c >= a + span_ref[a]
        a_next = jnp.minimum(jnp.where(last, a + 1, a), rows - 1)
        return a_next, jnp.where(last, a_next, c + 1)

    def kernel_rows(a, c, into, part, parts):
        high_ref, low_ref = into
        step = 16
        for i in range(part * SUP // parts, (part + 1) * SUP // parts, step):
            for h in range(2):
                dist2 = None
                for axis in range(3):
                    col = pos_ref[axis : axis + 1, pl.ds(pl.multiple_of(c * SUP + h * 128, 128), 128)]
                    diff = rows_ref[a, axis, i : i + step, :] - col
                    dist2 = diff * diff if axis == 0 else dist2 + diff * diff
                dist2 = jnp.maximum(dist2, TINY)
                reach = jnp.maximum(1.0 - dist2 * lax.rsqrt(dist2), 0.0)
                square = reach * reach
                kern = square * square * (1.25 - reach)
                high = kern.astype(jnp.bfloat16)
                low = (kern - high.astype(jnp.float32)).astype(jnp.bfloat16)
                high_ref[i : i + step, h * 128 : (h + 1) * 128] = high
                low_ref[i : i + step, h * 128 : (h + 1) * 128] = low

    def both(now, then, tiles_now, tiles_then, valid):
        a, c = now
        high_ref, low_ref = tiles_now
        row_vals, col_vals = vals_ref[a], vals_ref[c]
        kernel_rows(*then, tiles_then, 0, 4)
        front = dot(col_vals, high_ref[...], 1)
        kernel_rows(*then, tiles_then, 1, 4)
        front += dot(col_vals, low_ref[...], 1)
        kernel_rows(*then, tiles_then, 2, 4)
        back = dot(row_vals, high_ref[...], 0)
        kernel_rows(*then, tiles_then, 3, 4)
        back += dot(row_vals, low_ref[...], 0)
        front = (front[:FRAMES] + front[FRAMES:]) * 4.0
        back = (back[:FRAMES] + back[FRAMES:]) * 4.0
        out_ref[:, lanes(a)] += jnp.where(valid, front, 0.0)
        out_ref[:, lanes(c)] += jnp.where(valid & (a != c), back, 0.0)

    def step(i, now):
        then = following(*now)
        both(now, then, tiles[0], tiles[1], True)
        later = following(*then)
        both(then, later, tiles[1], tiles[0], 2 * i + 1 < total)
        return later

    kernel_rows(0, 0, tiles[0], 0, 1)
    lax.fori_loop(0, (total + 1) // 2, step, (jnp.int32(0), jnp.int32(0)))


def lane_totals(quantities):
    stacked = jnp.concatenate(quantities + [jnp.zeros_like(quantities[0])] * (4 - len(quantities)), axis=0)
    return jnp.broadcast_to(jnp.sum(jnp.transpose(stacked), axis=0, keepdims=True), (8, 128))


def frame_columns(totals):
    turned = jnp.transpose(jnp.broadcast_to(totals, (128, 128)))
    return [turned[i * FRAMES : (i + 1) * FRAMES] for i in range(4)]


def wide(column):
    return jnp.concatenate([column, column], axis=1)


def fold(values):
    return values[:, :128] + values[:, 128:]


def first_kernel(span_ref, pos_ref, noise_ref, own_ref, halo_ref, out_ref, sums_ref, rows_ref, vals_ref, *tiles):
    rows = own_ref.shape[1] // SUP
    spread_rows(pos_ref, rows_ref, rows)
    zero = jnp.zeros((FRAMES, 128), jnp.float32)

    def begin(a, norm):
        values = own_ref[:, lanes(a)]
        vals_ref[a] = split(values)
        out_ref[:, lanes(a)] = noise_ref[:, lanes(a)] * values
        return norm + fold(values * values)

    norm = lax.fori_loop(0, rows, begin, zero)

    def begin_halo(a, _):
        vals_ref[rows + a] = split(halo_ref[:, lanes(a)])
        out_ref[:, lanes(rows + a)] = jnp.zeros((FRAMES, SUP), jnp.float32)
        return 0

    lax.fori_loop(0, HALO, begin_halo, 0)
    sweep(span_ref, pos_ref, rows_ref, vals_ref, (tiles[:2], tiles[2:]), out_ref, rows)
    curve = lax.fori_loop(0, rows, lambda a, s: s + fold(own_ref[:, lanes(a)] * out_ref[:, lanes(a)]), zero)
    curve = lax.fori_loop(
        0, HALO, lambda a, s: s + fold(halo_ref[:, lanes(a)] * out_ref[:, lanes(rows + a)]), curve
    )
    sums_ref[...] = lane_totals([norm, curve])


def second_kernel(
    span_ref, pos_ref, noise_ref, own_ref, halo_ref, image_ref, left_ref, right_ref, first_ref,
    out_ref, sums_ref, rows_ref, vals_ref, resid_ref, *tiles
):
    rows = own_ref.shape[1] // SUP
    spread_rows(pos_ref, rows_ref, rows)
    norm_before, curve_before = frame_columns(first_ref[0:1])[:2]
    alpha = wide(norm_before / curve_before)
    zero = jnp.zeros((FRAMES, 128), jnp.float32)

    def begin(a, image, values, sums):
        residual = values - alpha * image
        vals_ref[a] = split(residual)
        resid_ref[:, lanes(a)] = residual
        out_ref[:, lanes(a)] = noise_ref[:, lanes(a)] * residual
        return (sums[0] + fold(residual * residual), sums[1] + fold(residual * image))

    def begin_first(a, sums):
        return begin(a, image_ref[:, lanes(a)] + left_ref[:, lanes(a)], own_ref[:, lanes(a)], sums)

    def begin_rest(a, sums):
        return begin(a, image_ref[:, lanes(a)], own_ref[:, lanes(a)], sums)

    sums = lax.fori_loop(0, HALO, begin_first, (zero, zero))
    norm, cross = lax.fori_loop(HALO, rows, begin_rest, sums)

    def begin_halo(a, _):
        image = image_ref[:, lanes(rows + a)] + right_ref[:, lanes(a)]
        residual = halo_ref[:, lanes(a)] - alpha * image
        vals_ref[rows + a] = split(residual)
        resid_ref[:, lanes(rows + a)] = residual
        out_ref[:, lanes(rows + a)] = jnp.zeros((FRAMES, SUP), jnp.float32)
        return 0

    lax.fori_loop(0, HALO, begin_halo, 0)
    sweep(span_ref, pos_ref, rows_ref, vals_ref, (tiles[:2], tiles[2:]), out_ref, rows)
    curve = lax.fori_loop(
        0, rows + HALO, lambda a, s: s + fold(resid_ref[:, lanes(a)] * out_ref[:, lanes(a)]), zero
    )
    sums_ref[...] = lane_totals([norm, curve, cross])


def apply_call(kernel, operands, rows, with_residual):
    extent = (rows + HALO) * SUP
    scratch = [
        pltpu.VMEM((rows, 3, SUP, 128), jnp.float32),
        pltpu.VMEM((rows + HALO, 2 * FRAMES, SUP), jnp.bfloat16),
    ]
    if with_residual:
        scratch.append(pltpu.VMEM((FRAMES, extent), jnp.float32))
    scratch += [pltpu.VMEM((SUP, SUP), jnp.bfloat16)] * 4
    return pl.pallas_call(
        kernel,
        out_shape=(f32((FRAMES, extent)), f32((8, 128))),
        in_specs=[SMEM] + [VMEM] * (len(operands) - 1),
        out_specs=(VMEM, VMEM),
        scratch_shapes=scratch,
        compiler_params=pltpu.CompilerParams(vmem_limit_bytes=44 * 2**20),
    )(*operands)


def exchange_kernel(both_ways, rows, part_ref, sums_ref, *refs):
    if both_ways:
        left_out, right_out, total_out, left_buf, right_buf, near, far, mine, edge_sems, near_sems, far_sems = refs
    else:
        left_out, total_out, left_buf, near, far, mine, edge_sems, near_sems, far_sems = refs
    size = lax.axis_size("pts")
    me = lax.axis_index("pts")
    groups = size // GROUP
    spot, group = lax.rem(me, GROUP), me // GROUP
    right, left = lax.rem(me + 1, size), lax.rem(me + size - 1, size)
    near_peers = [group * GROUP + lax.rem(spot + k, GROUP) for k in range(1, GROUP)]
    far_peers = [lax.rem(group + k, groups) * GROUP + spot for k in range(1, groups)]
    barrier = pltpu.get_barrier_semaphore()
    peers = near_peers + far_peers + [left, right]
    for peer in peers:
        pl.semaphore_signal(barrier, inc=1, device_id=(peer,), device_id_type=MESH)
    pl.semaphore_wait(barrier, len(peers))

    def send(src, dst, sems, index, peer):
        copy = pltpu.make_async_remote_copy(
            src_ref=src, dst_ref=dst, send_sem=sems.at[0, index], recv_sem=sems.at[1, index],
            device_id=(peer,), device_id_type=MESH,
        )
        copy.start()
        return copy

    near_copies = [send(sums_ref, near.at[k], near_sems, k, near_peers[k - 1]) for k in range(1, GROUP)]
    width = HALO * SUP
    edges = [send(part_ref.at[:, pl.ds(rows * SUP, width)], left_buf, edge_sems, 0, right)]
    if both_ways:
        edges.append(send(part_ref.at[:, pl.ds(0, width)], right_buf, edge_sems, 1, left))
    for copy in near_copies:
        copy.wait()
    total = sums_ref[...]
    for k in range(1, GROUP):
        total = total + near[k]
    mine[...] = total
    far_copies = [send(mine, far.at[k], far_sems, k, far_peers[k - 1]) for k in range(1, groups)]
    for copy in far_copies:
        copy.wait()
    for k in range(1, groups):
        total = total + far[k]
    total_out[...] = total
    for copy in edges:
        copy.wait()
    left_out[...] = left_buf[...]
    if both_ways:
        right_out[...] = right_buf[...]


def exchange(part, sums, rows, both_ways, collective_id):
    edge = f32((FRAMES, HALO * SUP))
    edges = 2 if both_ways else 1
    groups = lax.axis_size("pts") // GROUP
    return pl.pallas_call(
        functools.partial(exchange_kernel, both_ways, rows),
        out_shape=(edge,) * edges + (f32((8, 128)),),
        in_specs=[VMEM, VMEM],
        out_specs=(VMEM,) * (edges + 1),
        scratch_shapes=[pltpu.VMEM(edge.shape, jnp.float32)] * edges
        + [
            pltpu.VMEM((GROUP, 8, 128), jnp.float32),
            pltpu.VMEM((groups, 8, 128), jnp.float32),
            pltpu.VMEM((8, 128), jnp.float32),
            pltpu.SemaphoreType.DMA((2, edges)),
            pltpu.SemaphoreType.DMA((2, GROUP)),
            pltpu.SemaphoreType.DMA((2, groups)),
        ],
        compiler_params=pltpu.CompilerParams(
            collective_id=collective_id, has_side_effects=True, vmem_limit_bytes=16 * 2**20
        ),
    )(part, sums)


def last_kernel(own_ref, image_ref, left_ref, part_ref, left2_ref, first_ref, second_ref, field_ref, resid_ref):
    norm0, curve0 = frame_columns(first_ref[0:1])[:2]
    norm1, curve1, cross1 = frame_columns(second_ref[0:1])[:3]
    beta = norm1 / norm0
    alpha0 = wide(norm0 / curve0)
    alpha1 = wide(norm1 / (curve1 + 2.0 * beta * cross1 + beta * beta * curve0))
    beta = wide(beta)
    edge = (pl.program_id(0) == 0).astype(jnp.float32)

    def step(a, _):
        at = lanes(a)
        first = own_ref[:, at]
        image = image_ref[:, at] + edge * left_ref[:, at]
        residual = first - alpha0 * image
        direction = residual + beta * first
        image_next = part_ref[:, at] + edge * left2_ref[:, at] + beta * image
        field_ref[:, at] = alpha0 * first + alpha1 * direction
        resid_ref[:, at] = residual - alpha1 * image_next
        return 0

    lax.fori_loop(0, HALO, step, 0)


def last(own, image, left, part, left2, first, second):
    width = HALO * SUP
    steps = own.shape[1] // width
    moving = pl.BlockSpec((FRAMES, width), lambda i: (0, i))
    fixed = pl.BlockSpec((FRAMES, width), lambda i: (0, 0))
    small = pl.BlockSpec((8, 128), lambda i: (0, 0))
    return pl.pallas_call(
        last_kernel,
        grid=(steps,),
        out_shape=(f32(own.shape), f32(own.shape)),
        in_specs=[moving, moving, fixed, moving, fixed, small, small],
        out_specs=(moving, moving),
    )(own, image, left, part, left2, first, second)


def spans(positions, rows):
    boxed = positions.reshape(3, rows + HALO, SUP)
    low, high = jnp.min(boxed, axis=2), jnp.max(boxed, axis=2)
    alone = lax.axis_index("pts") == lax.axis_size("pts") - 1
    limit = jnp.where(alone, rows, rows + HALO)
    index = jnp.arange(rows, dtype=jnp.int32)
    span = jnp.zeros((rows,), jnp.int32)
    for k in range(1, HALO + 1):
        gap = jnp.maximum(jnp.maximum(low[:, k : k + rows] - high[:, :rows], low[:, :rows] - high[:, k : k + rows]), 0.0)
        near = (jnp.sum(gap * gap, axis=0) < 1.0) & (index + k < limit)
        span = jnp.where(near, k, span)
    return jnp.concatenate([span, jnp.sum(span + 1, keepdims=True)])


def body(positions, noise, right_side, pairs, counts):
    rows = positions.shape[1] // SUP
    width = HALO * SUP
    size = lax.axis_size("pts")
    back = [(i + 1, i) for i in range(size - 1)]
    edge_pos = lax.ppermute(positions[:, :width], "pts", back)
    halo = lax.ppermute(right_side[:, :width], "pts", back)
    pos = jnp.concatenate([positions, edge_pos], axis=1)
    span = spans(pos, rows)
    pos = jnp.concatenate([pos, jnp.zeros((5, pos.shape[1]), jnp.float32)], axis=0)
    noise = noise.reshape(1, -1)
    image, sums = apply_call(first_kernel, (span, pos, noise, right_side, halo), rows, False)
    left, right, first = exchange(image, sums, rows, True, 0)
    part, sums = apply_call(
        second_kernel, (span, pos, noise, right_side, halo, image, left, right, first), rows, True
    )
    left2, second = exchange(part, sums, rows, False, 1)
    return last(right_side, image, left, part, left2, first, second)


def solution(mesh):
    in_specs = (P(None, "pts"), P("pts"), P(None, "pts"), P(None, "pts"), P("pts"))
    out_specs = (P(None, "pts"), P(None, "pts"))
    return jax.shard_map(body, mesh=mesh, in_specs=in_specs, out_specs=out_specs, check_vma=False)
```

time: 1280 us -> 184 us (0.14)
  matrix products: 689 us -> 0 us
  local copies, waits for them, and re-layouts: 295 us -> 5.19 us
  blocking collectives: 206 us -> 0 us
  Pallas kernels: 0 us -> 168 us
  other arithmetic: 55.4 us -> 1.68 us
    dot_general x48 -> x0, matrix products: 689 us -> none  [the longest x16 337 us: tile_products(): jnp.einsum('gij,gfj->gfi', kern, jnp.take(val_blocks, cols, axis=0), prec...]
    psum x3 -> x0, blocking collectives: 206 us -> none  [the longest x2 138 us: squares(): return lax.psum(frame_sums(residual, residual), 'pts')]
    pallas_call x0 -> x5, Pallas kernels: none -> 168 us  [the longest x2 94.9 us: apply_call(): pl.pallas_call(kernel, out_shape=(f32((FRAMES, extent)), f32((8, 128))),...]
    gather x64 -> x0, local copies, waits for them, and re-layouts: 95.1 us -> none  [the longest x16 35.6 us: tile_products(): jnp.take(val_blocks, rows, axis=0)]
    while x128 -> x0, local copies, waits for them, and re-layouts: 92.3 us -> none
    dot_general x16 -> x0, local copies, waits for them, and re-layouts: 90.1 us -> none  [spread(): summed = jnp.dot(places.T, flat, precision=lax.Precision.HIGH)]
    mul x16 -> x0, other arithmetic: 16 us -> none  [tile_products(): cross = keep * (rows != cols).astype(jnp.float32)]
  transfers between devices with their start and end apart: 5 -> 2, of which waited for: 4 -> 1; matrix products, arithmetic and copies ran while one was open for 0% -> 2% of each run, Pallas kernels for 0% -> 0%
where the time goes in v1:
time: 184 us
  Pallas kernels  168 us (91%)
  starting transfers between devices  5.24 us (3%)
  local copies, waits for them, and re-layouts  5.19 us (3%)
  waiting for transfers between devices  3.07 us (2%)
    pallas_call x2, Pallas kernels, apply_call(): pl.pallas_call(kernel, out_shape=(f32((FRAMES, extent)), f32((8, 128))),...  94.9 us
    pallas_call x2, Pallas kernels, exchange(): pl.pallas_call(functools.partial(exchange_kernel, both_ways, rows), out_s...  68.1 us
    pallas_call x1, Pallas kernels, last(): pl.pallas_call(last_kernel, grid=(steps,), out_shape=(f32(own.shape), f32...  4.67 us
  transfers between devices with their start and end apart: 2, of which 1 were waited for; matrix products, arithmetic and copies ran while one was open for 2% of the time, Pallas kernels for 0%

profile of v1, /device:TPU:1, one launch (start us, length us, event | category | flops | bytes accessed | tf_op | source)
XLA Modules:
  0.0 183.6 jit_solution(5236402688853148169)
XLA Ops:
  0.6 0.0 copy-start.1
  0.6 0.0 copy-start.5
  0.7 0.9 slice.74
  1.5 3.3 %collective-permute-start = (f32[3,2048]{1,0:T(4,128)S(1)}, f32[3,2048]{1,0:T(4,128)S(1)}, u32[]{:S(2)}, u32[]{:S(2)}) collective-permute-start(f32[3,2048]{1,0:T(4,128)S(1)} %slice.74), channel_id=1, source_target_pairs={{1,0},{2,1},{3,2},{4,3},{5,4},{6,5},{7,6},{8,7},{9,8},{10,9},{11,1... | collective-permute-start | bytes 73736 | tf_op jit(solution)/shard_map/ppermute | solution.py:342
  4.8 1.0 slice.93
  5.8 1.9 %collective-permute-start.1 = (f32[32,2048]{1,0:T(8,128)S(1)}, f32[32,2048]{1,0:T(8,128)S(1)}, u32[]{:S(2)}, u32[]{:S(2)}) collective-permute-start(f32[32,2048]{1,0:T(8,128)S(1)} %slice.93), channel_id=1, source_target_pairs={{1,0},{2,1},{3,2},{4,3},{5,4},{6,5},{7,6},{8,7},{9,8},{10,9},{11,1... | collective-permute-start | bytes 786440 | tf_op jit(solution)/shard_map/ppermute | solution.py:343
  7.7 0.9 constant_dynamic-update-slice_fusion.1
  8.7 0.0 collective-permute-done
  8.7 0.1 bitcast_reduce_fusion.1
  8.8 0.1 multiply_reduce_fusion
  8.9 0.1 multiply_reduce_fusion.3
  9.1 0.6 add_reduce_fusion
  9.7 0.7 pad_add_fusion.span_ref
  10.4 3.1 %collective-permute-done.1.halo_ref = f32[32,2048]{1,0:T(8,128)S(1)} collective-permute-done((f32[32,2048]{1,0:T(8,128)S(1)}, f32[32,2048]{1,0:T(8,128)S(1)}, u32[]{:S(2)}, u32[]{:S(2)}) %collective-permute-start.1) | collective-permute-done | bytes 262176 | tf_op jit(solution)/shard_map/ppermute | solution.py:343
  13.5 0.0 copy-done.1
  13.5 0.0 copy-done.5
  13.5 47.3 %shard_map.50 = (f32[32,10240]{1,0:T(8,128)S(1)}, f32[8,128]{1,0:T(8,128)S(1)}) custom-call(s32[33]{0:T(128)S(1)} %pad_add_fusion.span_ref, f32[8,10240]{1,0:T(8,128)S(1)} %concatenate.11.pos_ref, f32[1,8192]{1,0:T(1,128)S(1)} %bitcast.6, f32[32,8192]{1,0:T(8,128)S(1)} %copy-done.1, f32[32,2048]{1,0:T(8,128)S(1)} %collective-permute-done.1.halo_ref), custom_call_target="tpu_custom_call" | custom-call | tf_op jit(solution)/shard_map/pallas_call | solution.py:201
  60.8 0.0 copy-start
  60.8 35.2 %shard_map.51 = (f32[32,2048]{1,0:T(8,128)S(1)}, f32[32,2048]{1,0:T(8,128)S(1)}, f32[8,128]{1,0:T(8,128)S(1)}) custom-call(f32[32,10240]{1,0:T(8,128)S(1)} %get-tuple-element.11.part_ref.image_ref, f32[8,128]{1,0:T(8,128)S(1)} %get-tuple-element.12.sums_ref), custom_call_target="tpu_custom_call" | custom-call | tf_op jit(solution)/shard_map/pallas_call | solution.py:265
  96.0 0.0 copy-start.3
  96.0 0.0 copy-start.6
  96.0 47.6 %shard_map.52 = (f32[32,10240]{1,0:T(8,128)S(1)}, f32[8,128]{1,0:T(8,128)S(1)}) custom-call(s32[33]{0:T(128)S(1)} %pad_add_fusion.span_ref, f32[8,10240]{1,0:T(8,128)S(1)} %concatenate.11.pos_ref, f32[1,8192]{1,0:T(1,128)S(1)} %bitcast.7, f32[32,8192]{1,0:T(8,128)S(1)} %copy-done.1, f32[32,2048]{1,0:T(8,128)S(1)} %collective-permute-done.1.halo_ref, ...), custom_call_target="tpu_custom_call" | custom-call | tf_op jit(solution)/shard_map/pallas_call | solution.py:201
  143.6 0.0 copy-done
  143.6 0.0 copy-done.3
  143.6 0.0 copy-done.6
  143.6 32.9 %shard_map.53 = (f32[32,2048]{1,0:T(8,128)S(1)}, f32[8,128]{1,0:T(8,128)S(1)}) custom-call(f32[32,10240]{1,0:T(8,128)S(1)} %get-tuple-element.16.part_ref, f32[8,128]{1,0:T(8,128)S(1)} %get-tuple-element.17.sums_ref), custom_call_target="tpu_custom_call" | custom-call | tf_op jit(solution)/shard_map/pallas_call | solution.py:265
  176.6 0.0 copy-start.2
  176.6 1.1 copy-done.2
  177.7 0.0 copy-start.4
  177.7 0.7 copy-done.4
  178.4 0.0 copy-start.7
  178.4 0.6 copy-done.7
  179.0 4.7 %shard_map.54 = (f32[32,8192]{1,0:T(8,128)}, f32[32,8192]{1,0:T(8,128)}) custom-call(f32[32,8192]{1,0:T(8,128)} %own_ref.5, f32[32,10240]{1,0:T(8,128)} %copy-done, f32[32,2048]{1,0:T(8,128)} %copy-done.3, f32[32,10240]{1,0:T(8,128)} %copy-done.2, f32[32,2048]{1,0:T(8,128)} %copy-done.4, f32[8,128]{1,0:T(8,128)} %copy-done.6, f32[8,128]{1,0:T(8,128)} %copy-done.7), custom_call_target="tpu_custom_call" | custom-call | tf_op jit(solution)/shard_map/pallas_call | solution.py:314
  (2 shorter events, 0.0 us)
Async XLA Ops:
  0.6 12.9 %copy-start.1 = (f32[32,8192]{1,0:T(8,128)S(1)}, f32[32,8192]{1,0:T(8,128)}, u32[]{:S(2)}) copy-start(f32[32,8192]{1,0:T(8,128)} %own_ref.5) | copy-start | bytes 3145732
  0.6 12.9 %copy-start.5 = (f32[8192]{0:T(1024)S(1)}, f32[8192]{0:T(1024)}, u32[]{:S(2)}) copy-start(f32[8192]{0:T(1024)} %param.6) | copy-start | bytes 98308
  1.5 7.2 %collective-permute-start = (f32[3,2048]{1,0:T(4,128)S(1)}, f32[3,2048]{1,0:T(4,128)S(1)}, u32[]{:S(2)}, u32[]{:S(2)}) collective-permute-start(f32[3,2048]{1,0:T(4,128)S(1)} %slice.74), channel_id=1, source_target_pairs={{1,0},{2,1},{3,2},{4,3},{5,4},{6,5},{7,6},{8,7},{9,8},{10,9},{11,1... | collective-permute-start | bytes 73736 | tf_op jit(solution)/shard_map/ppermute | solution.py:342
  5.8 7.7 %collective-permute-start.1 = (f32[32,2048]{1,0:T(8,128)S(1)}, f32[32,2048]{1,0:T(8,128)S(1)}, u32[]{:S(2)}, u32[]{:S(2)}) collective-permute-start(f32[32,2048]{1,0:T(8,128)S(1)} %slice.93), channel_id=1, source_target_pairs={{1,0},{2,1},{3,2},{4,3},{5,4},{6,5},{7,6},{8,7},{9,8},{10,9},{11,1... | collective-permute-start | bytes 786440 | tf_op jit(solution)/shard_map/ppermute | solution.py:343
  60.8 82.8 %copy-start = (f32[32,10240]{1,0:T(8,128)}, f32[32,10240]{1,0:T(8,128)S(1)}, u32[]{:S(2)}) copy-start(f32[32,10240]{1,0:T(8,128)S(1)} %get-tuple-element.11.part_ref.image_ref) | copy-start | bytes 3932164
  96.0 47.6 %copy-start.3 = (f32[32,2048]{1,0:T(8,128)}, f32[32,2048]{1,0:T(8,128)S(1)}, u32[]{:S(2)}) copy-start(f32[32,2048]{1,0:T(8,128)S(1)} %get-tuple-element.13.left_ref) | copy-start | bytes 786436
  96.0 47.6 %copy-start.6 = (f32[8,128]{1,0:T(8,128)}, f32[8,128]{1,0:T(8,128)S(1)}, u32[]{:S(2)}) copy-start(f32[8,128]{1,0:T(8,128)S(1)} %get-tuple-element.15.first_ref) | copy-start | bytes 12292
  176.6 1.1 copy-start.2
  177.7 0.7 copy-start.4
  178.4 0.6 copy-start.7

commit v2 on v1

v2 whole, which is shorter than its diff:
```python
import functools

import jax
import jax.numpy as jnp
from jax import lax
from jax.experimental import pallas as pl
from jax.experimental.pallas import tpu as pltpu
from jax.sharding import PartitionSpec as P

SUP = 256
HALO = 8
FRAMES = 32
TINY = 1e-36
MESH = pl.DeviceIdType.MESH
VMEM = pl.BlockSpec(memory_space=pltpu.VMEM)
ANY = pl.BlockSpec(memory_space=pl.ANY)
SMEM = pl.BlockSpec(memory_space=pltpu.SMEM)
BATCH = 8
TILES = (BATCH, 2, SUP, SUP)
KEPT = 17
GROUP = 8


def f32(shape):
    return jax.ShapeDtypeStruct(shape, jnp.float32)


def dot(left, right, dim):
    return lax.dot_general(
        left, right, (((1,), (dim,)), ((), ())), preferred_element_type=jnp.float32
    )


def lanes(index, width=SUP):
    return pl.ds(pl.multiple_of(index * width, width), width)


def spread_rows(pos_ref, rows_ref, rows):
    row = lax.broadcasted_iota(jnp.int32, (32, 3 * 128), 0)
    lane = lax.broadcasted_iota(jnp.int32, (32, 3 * 128), 1)
    ones = ((row & 7) == (lane >> 7)).astype(jnp.float32).astype(jnp.bfloat16)

    def step(a, _):
        rest = pos_ref[:, lanes(a)]
        terms = []
        for _ in range(3):
            term = rest.astype(jnp.bfloat16).astype(jnp.float32)
            terms.append(term)
            rest = rest - term
        terms = jnp.concatenate(terms + [jnp.zeros_like(rest)], axis=0).astype(jnp.bfloat16)
        wide_rows = lax.dot_general(terms, ones, (((0,), (0,)), ((), ())), preferred_element_type=jnp.float32)
        for c in range(3):
            rows_ref[a, c] = wide_rows[:, c * 128 : (c + 1) * 128]
        return 0

    lax.fori_loop(0, rows, step, 0, unroll=4)


def split(values):
    values = 4.0 * values
    high = values.astype(jnp.bfloat16)
    low = (values - high.astype(jnp.float32)).astype(jnp.bfloat16)
    return jnp.concatenate([high, low], axis=0)


def follower(span_ref, base, rows):
    def following(a, c):
        last = c >= a + span_ref[a - base]
        a_next = jnp.minimum(jnp.where(last, a + 1, a), base + rows - 1)
        return a_next, jnp.where(last, a_next, c + 1)

    return following


def kernel_tile(pos_ref, rows_ref, a, c, store):
    highs, lows = [], []
    step = 16
    for i in range(0, SUP, step):
        pair = []
        for h in range(2):
            dist2 = None
            for axis in range(3):
                col = pos_ref[axis : axis + 1, pl.ds(pl.multiple_of(c * SUP + h * 128, 128), 128)]
                diff = rows_ref[a, axis, i : i + step, :] - col
                dist2 = diff * diff if axis == 0 else dist2 + diff * diff
            dist2 = jnp.maximum(dist2, TINY)
            reach = jnp.maximum(1.0 - dist2 * lax.rsqrt(dist2), 0.0)
            square = reach * reach
            kern = square * square * (1.25 - reach)
            high = kern.astype(jnp.bfloat16)
            pair.append((high, (kern - high.astype(jnp.float32)).astype(jnp.bfloat16)))
        highs.append(jnp.concatenate([p[0] for p in pair], axis=1))
        lows.append(jnp.concatenate([p[1] for p in pair], axis=1))
        store(i, step, highs[-1], lows[-1])
    return jnp.concatenate(highs, axis=0), jnp.concatenate(lows, axis=0)


def products(vals_ref, out_ref, base, a, c, high, low, valid):
    row_vals, col_vals = vals_ref[a - base], vals_ref[c - base]
    front = dot(col_vals, high, 1) + dot(col_vals, low, 1)
    back = dot(row_vals, high, 0) + dot(row_vals, low, 0)
    unused = out_ref.shape[1] // SUP - 1
    out_ref[:, lanes(jnp.where(valid, a, unused))] += front[:FRAMES] + front[FRAMES:]
    out_ref[:, lanes(jnp.where(valid & (a != c), c, unused))] += back[:FRAMES] + back[FRAMES:]


def group_count(total):
    return (total + BATCH - 1) // BATCH


def sweep(span_ref, pos_ref, rows_ref, vals_ref, out_ref, base, rows, keep_ref, stage_ref, sems):
    total = span_ref[rows]
    groups = group_count(total)
    kept = jnp.minimum(groups, keep_ref.shape[0])
    following = follower(span_ref, base, rows)

    def save(g):
        slot = lax.rem(g, 2)
        return pltpu.make_async_copy(stage_ref.at[slot], keep_ref.at[g], sems.at[slot])

    def step(g, now):
        slot = lax.rem(g, 2)

        @pl.when((g >= 2) & (g - 2 < kept))
        def _():
            save(g - 2).wait()

        for u in range(BATCH):
            a, c = now

            def store(i, step, high, low):
                stage_ref[slot, u, 0, i : i + step, :] = high
                stage_ref[slot, u, 1, i : i + step, :] = low

            high, low = kernel_tile(pos_ref, rows_ref, a - base, c - base, store)
            products(vals_ref, out_ref, base, a, c, high, low, BATCH * g + u < total)
            now = following(a, c)

        @pl.when(g < kept)
        def _():
            save(g).start()

        return now

    lax.fori_loop(0, groups, step, (jnp.int32(base), jnp.int32(base)))
    for k in (2, 1):
        g = groups - k

        @pl.when((g >= 0) & (g < kept))
        def _():
            save(g).wait()


def loader(kept, groups, keeps, stage_ref, sems):
    def load(g, do):
        slot = lax.rem(g, 2)

        @pl.when(g < kept)
        def _():
            do(pltpu.make_async_copy(keeps[0].at[g], stage_ref.at[slot], sems.at[slot]))

        @pl.when((g >= kept) & (g < groups))
        def _():
            do(pltpu.make_async_copy(keeps[1].at[g - kept], stage_ref.at[slot], sems.at[slot]))

    return load


def first_load(spans, counts, keeps, stage_ref, sems):
    kept = jnp.minimum(group_count(spans[0][counts[0]]), keeps[0].shape[0])
    groups = kept + group_count(spans[1][counts[1]])
    loader(kept, groups, keeps, stage_ref, sems)(jnp.int32(0), lambda copy: copy.start())


def sweep_again(spans, bases, counts, keeps, pos_ref, rows_ref, vals_ref, out_ref, stage_ref, sems):
    totals = [span[rows] for span, rows in zip(spans, counts)]
    kept = jnp.minimum(group_count(totals[0]), keeps[0].shape[0])
    groups = kept + group_count(totals[1])
    followers = [follower(*part) for part in zip(spans, bases, counts)]

    load = loader(kept, groups, keeps, stage_ref, sems)

    def part(index, first, end, now):
        def step(g, now):
            slot = lax.rem(g, 2)
            load(g + 1, lambda copy: copy.start())
            load(g, lambda copy: copy.wait())
            for u in range(BATCH):
                a, c = now
                valid = BATCH * (g - first) + u < totals[index]
                products(vals_ref, out_ref, 0, a, c, stage_ref[slot, u, 0], stage_ref[slot, u, 1], valid)
                now = followers[index](a, c)
            return now

        return lax.fori_loop(first, end, step, (jnp.int32(now), jnp.int32(now)))

    reached = part(0, 0, kept, bases[0])
    part(1, kept, groups, bases[1])

    @pl.when(BATCH * kept < totals[0])
    def _():
        spread_rows(pos_ref, rows_ref, counts[0])

        def step(t, now):
            a, c = now
            high, low = kernel_tile(pos_ref, rows_ref, a, c, lambda *_: None)
            products(vals_ref, out_ref, 0, a, c, high, low, True)
            return followers[0](a, c)

        lax.fori_loop(BATCH * kept, totals[0], step, reached)


def lane_totals(quantities):
    stacked = jnp.concatenate(quantities + [jnp.zeros_like(quantities[0])] * (4 - len(quantities)), axis=0)
    return jnp.broadcast_to(jnp.sum(jnp.transpose(stacked), axis=0, keepdims=True), (8, 128))


def frame_columns(totals):
    turned = jnp.transpose(jnp.broadcast_to(totals, (128, 128)))
    return [turned[i * FRAMES : (i + 1) * FRAMES] for i in range(4)]


def wide(column):
    return jnp.concatenate([column, column], axis=1)


def fold(values):
    return values[:, :128] + values[:, 128:]


def zeros():
    return jnp.zeros((FRAMES, 128), jnp.float32)


def loop(low, high, step, start):
    return lax.fori_loop(low, high, step, start, unroll=4)


def inner_kernel(span_ref, pos_ref, noise_ref, own_ref, out_ref, norm_ref, keep_ref, rows_ref, vals_ref, stage_ref, sems):
    rows = own_ref.shape[1] // SUP
    spread_rows(pos_ref, rows_ref, rows - HALO)

    def begin(a, norm):
        values = own_ref[:, lanes(a)]
        vals_ref[a] = split(values)
        out_ref[:, lanes(a)] = noise_ref[:, lanes(a)] * values
        return norm + fold(values * values)

    norm_ref[...] = loop(0, rows, begin, zeros())
    sweep(span_ref, pos_ref, rows_ref, vals_ref, out_ref, 0, rows - HALO, keep_ref, stage_ref, sems)


def outer_kernel(
    span_ref, pos_ref, own_ref, halo_ref, norm_ref, begun_ref, out_ref, sums_ref, keep_ref, rows_ref, vals_ref, stage_ref, sems
):
    rows = own_ref.shape[1] // SUP
    base = rows - HALO
    spread_rows(pos_ref, rows_ref, HALO)

    def begin(a, _):
        vals_ref[a] = split(own_ref[:, lanes(base + a)])
        vals_ref[HALO + a] = split(halo_ref[:, lanes(a)])
        out_ref[:, lanes(rows + a)] = jnp.zeros((FRAMES, SUP), jnp.float32)
        return 0

    def resume(a, _):
        out_ref[:, lanes(a)] = begun_ref[:, lanes(a)]
        return 0

    loop(0, rows, resume, 0)
    loop(0, HALO, begin, 0)
    sweep(span_ref, pos_ref, rows_ref, vals_ref, out_ref, base, HALO, keep_ref, stage_ref, sems)
    curve = loop(0, rows, lambda a, s: s + fold(own_ref[:, lanes(a)] * out_ref[:, lanes(a)]), zeros())
    curve = loop(0, HALO, lambda a, s: s + fold(halo_ref[:, lanes(a)] * out_ref[:, lanes(rows + a)]), curve)
    sums_ref[...] = lane_totals([norm_ref[...], curve])


def second_kernel(
    span_ref, outer_ref, pos_ref, noise_ref, own_ref, halo_ref, image_ref, left_ref, right_ref, first_ref, keep_ref, keep2_ref,
    out_ref, sums_ref, rows_ref, vals_ref, resid_ref, stage_ref, sems
):
    rows = own_ref.shape[1] // SUP
    spans, bases, counts = (span_ref, outer_ref), (0, rows - HALO), (rows - HALO, HALO)
    keeps = (keep_ref, keep2_ref)
    first_load(spans, counts, keeps, stage_ref, sems)
    norm_before, curve_before = frame_columns(first_ref[0:1])[:2]
    alpha = wide(norm_before / curve_before)

    def begin(a, image, values, sums):
        residual = values - alpha * image
        vals_ref[a] = split(residual)
        resid_ref[:, lanes(a)] = residual
        out_ref[:, lanes(a)] = noise_ref[:, lanes(a)] * residual
        return (sums[0] + fold(residual * residual), sums[1] + fold(residual * image))

    def begin_first(a, sums):
        return begin(a, image_ref[:, lanes(a)] + left_ref[:, lanes(a)], own_ref[:, lanes(a)], sums)

    def begin_rest(a, sums):
        return begin(a, image_ref[:, lanes(a)], own_ref[:, lanes(a)], sums)

    sums = loop(0, HALO, begin_first, (zeros(), zeros()))
    norm, cross = loop(HALO, rows, begin_rest, sums)

    def begin_halo(a, _):
        image = image_ref[:, lanes(rows + a)] + right_ref[:, lanes(a)]
        residual = halo_ref[:, lanes(a)] - alpha * image
        vals_ref[rows + a] = split(residual)
        resid_ref[:, lanes(rows + a)] = residual
        out_ref[:, lanes(rows + a)] = jnp.zeros((FRAMES, SUP), jnp.float32)
        return 0

    loop(0, HALO, begin_halo, 0)
    sweep_again(spans, bases, counts, keeps, pos_ref, rows_ref, vals_ref, out_ref, stage_ref, sems)
    curve = loop(0, rows + HALO, lambda a, s: s + fold(resid_ref[:, lanes(a)] * out_ref[:, lanes(a)]), zeros())
    sums_ref[...] = lane_totals([norm, curve, cross])


def field_scratch(rows_held, vals_held):
    return [
        pltpu.VMEM((rows_held, 3, SUP, 128), jnp.float32),
        pltpu.VMEM((vals_held, 2 * FRAMES, SUP), jnp.bfloat16),
    ]


def stage_scratch():
    return [pltpu.VMEM((2,) + TILES, jnp.bfloat16), pltpu.SemaphoreType.DMA((2,))]


def local_call(kernel, operands, out_shape, scratch, smalls, anys=0, any_outs=0):
    plain = len(operands) - smalls - anys
    return pl.pallas_call(
        kernel,
        out_shape=out_shape,
        in_specs=[SMEM] * smalls + [VMEM] * plain + [ANY] * anys,
        out_specs=(VMEM,) * (len(out_shape) - any_outs) + (ANY,) * any_outs,
        scratch_shapes=scratch,
        compiler_params=pltpu.CompilerParams(vmem_limit_bytes=44 * 2**20),
    )(*operands)


def exchange_kernel(both_ways, rows, part_ref, sums_ref, *refs):
    if both_ways:
        left_out, right_out, total_out, left_buf, right_buf, near, far, mine, edge_sems, near_sems, far_sems = refs
    else:
        left_out, total_out, left_buf, near, far, mine, edge_sems, near_sems, far_sems = refs
    size = lax.axis_size("pts")
    me = lax.axis_index("pts")
    groups = size // GROUP
    spot, group = lax.rem(me, GROUP), me // GROUP
    right, left = lax.rem(me + 1, size), lax.rem(me + size - 1, size)
    near_peers = [group * GROUP + lax.rem(spot + k, GROUP) for k in range(1, GROUP)]
    far_peers = [lax.rem(group + k, groups) * GROUP + spot for k in range(1, groups)]
    barrier = pltpu.get_barrier_semaphore()
    peers = near_peers + far_peers + [left, right]
    for peer in peers:
        pl.semaphore_signal(barrier, inc=1, device_id=(peer,), device_id_type=MESH)
    pl.semaphore_wait(barrier, len(peers))

    def send(src, dst, sems, index, peer):
        copy = pltpu.make_async_remote_copy(
            src_ref=src, dst_ref=dst, send_sem=sems.at[0, index], recv_sem=sems.at[1, index],
            device_id=(peer,), device_id_type=MESH,
        )
        copy.start()
        return copy

    near_copies = [send(sums_ref, near.at[k], near_sems, k, near_peers[k - 1]) for k in range(1, GROUP)]
    width = HALO * SUP
    edges = [send(part_ref.at[:, pl.ds(rows * SUP, width)], left_buf, edge_sems, 0, right)]
    if both_ways:
        edges.append(send(part_ref.at[:, pl.ds(0, width)], right_buf, edge_sems, 1, left))
    for copy in near_copies:
        copy.wait()
    total = sums_ref[...]
    for k in range(1, GROUP):
        total = total + near[k]
    mine[...] = total
    far_copies = [send(mine, far.at[k], far_sems, k, far_peers[k - 1]) for k in range(1, groups)]
    for copy in far_copies:
        copy.wait()
    for k in range(1, groups):
        total = total + far[k]
    total_out[...] = total
    for copy in edges:
        copy.wait()
    left_out[...] = left_buf[...]
    if both_ways:
        right_out[...] = right_buf[...]


def exchange(part, sums, rows, both_ways, collective_id):
    edge = f32((FRAMES, HALO * SUP))
    edges = 2 if both_ways else 1
    groups = lax.axis_size("pts") // GROUP
    return pl.pallas_call(
        functools.partial(exchange_kernel, both_ways, rows),
        out_shape=(edge,) * edges + (f32((8, 128)),),
        in_specs=[VMEM, VMEM],
        out_specs=(VMEM,) * (edges + 1),
        scratch_shapes=[pltpu.VMEM(edge.shape, jnp.float32)] * edges
        + [
            pltpu.VMEM((GROUP, 8, 128), jnp.float32),
            pltpu.VMEM((groups, 8, 128), jnp.float32),
            pltpu.VMEM((8, 128), jnp.float32),
            pltpu.SemaphoreType.DMA((2, edges)),
            pltpu.SemaphoreType.DMA((2, GROUP)),
            pltpu.SemaphoreType.DMA((2, groups)),
        ],
        compiler_params=pltpu.CompilerParams(
            collective_id=collective_id, has_side_effects=True, vmem_limit_bytes=16 * 2**20
        ),
    )(part, sums)


def last_kernel(
    own_ref, image_ref, left_ref, part_ref, left2_ref, first_ref, second_ref, field_out, resid_out, field_ref, resid_ref, sems
):
    norm0, curve0 = frame_columns(first_ref[0:1])[:2]
    norm1, curve1, cross1 = frame_columns(second_ref[0:1])[:3]
    beta = norm1 / norm0
    alpha0 = wide(norm0 / curve0)
    alpha1 = wide(norm1 / (curve1 + 2.0 * beta * cross1 + beta * beta * curve0))
    beta = wide(beta)
    width = HALO * SUP
    copies = []
    for part in range(own_ref.shape[1] // width):
        def step(a, _):
            at = lanes(part * HALO + a)
            first, image, image_next = own_ref[:, at], image_ref[:, at], part_ref[:, at]
            if part == 0:
                image = image + left_ref[:, at]
                image_next = image_next + left2_ref[:, at]
            residual = first - alpha0 * image
            direction = residual + beta * first
            field_ref[:, at] = alpha0 * first + alpha1 * direction
            resid_ref[:, at] = residual - alpha1 * (image_next + beta * image)
            return 0

        loop(0, HALO, step, 0)
        at = pl.ds(part * width, width)
        for index, (src, dst) in enumerate(((field_ref, field_out), (resid_ref, resid_out))):
            copies.append(pltpu.make_async_copy(src.at[:, at], dst.at[:, at], sems.at[index, part]))
            copies[-1].start()
    for copy in copies:
        copy.wait()


def spans(positions, rows, limit):
    extent = positions.shape[1] // SUP
    boxed = positions.reshape(3, extent, SUP)
    low, high = jnp.min(boxed, axis=2), jnp.max(boxed, axis=2)
    index = jnp.arange(rows, dtype=jnp.int32)
    span = jnp.zeros((rows,), jnp.int32)
    for k in range(1, HALO + 1):
        ahead = slice(k, k + rows)
        gap = jnp.maximum(jnp.maximum(low[:, ahead] - high[:, :rows], low[:, :rows] - high[:, ahead]), 0.0)
        near = (jnp.sum(gap * gap, axis=0) < 1.0) & (index + k < limit)
        span = jnp.where(near, k, span)
    return jnp.concatenate([span, jnp.sum(span + 1, keepdims=True)])


def padded(positions):
    return jnp.concatenate([positions, jnp.zeros((5, positions.shape[1]), jnp.float32)], axis=0)


def body(positions, noise, right_side, pairs, counts):
    rows = positions.shape[1] // SUP
    inner = rows - HALO
    width = HALO * SUP
    size = lax.axis_size("pts")
    back = [(i + 1, i) for i in range(size - 1)]
    edge_pos = lax.ppermute(positions[:, :width], "pts", back)
    halo = lax.ppermute(right_side[:, :width], "pts", back)
    pos = padded(positions)
    noise = noise.reshape(1, -1)
    field = f32((FRAMES, (rows + HALO + 1) * SUP))
    small = f32((FRAMES, 128))
    span = spans(positions, inner, rows)
    image, norm, keep = local_call(
        inner_kernel, (span, pos, noise, right_side),
        (field, small, jax.ShapeDtypeStruct((KEPT,) + TILES, jnp.bfloat16)),
        field_scratch(inner, rows) + stage_scratch(), 1, any_outs=1,
    )
    outer_pos = jnp.concatenate([positions[:, inner * SUP :], edge_pos], axis=1)
    alone = lax.axis_index("pts") == size - 1
    outer_span = spans(outer_pos, HALO, jnp.where(alone, HALO, 2 * HALO))
    steps = -(-HALO * (HALO + 1) // BATCH)
    image, sums, keep2 = local_call(
        outer_kernel, (outer_span, padded(outer_pos), right_side, halo, norm, image),
        (field, f32((8, 128)), jax.ShapeDtypeStruct((steps,) + TILES, jnp.bfloat16)),
        field_scratch(HALO, 2 * HALO) + stage_scratch(), 1, any_outs=1,
    )
    left, right, first = exchange(image, sums, rows, True, 0)
    part, sums = local_call(
        second_kernel,
        (span, outer_span, pos, noise, right_side, halo, image, left, right, first, keep, keep2),
        (field, f32((8, 128))),
        field_scratch(inner, rows + HALO) + [pltpu.VMEM((FRAMES, (rows + HALO) * SUP), jnp.float32)] + stage_scratch(),
        2, anys=2,
    )
    left2, second = exchange(part, sums, rows, False, 1)
    parts = rows // HALO
    return local_call(
        last_kernel, (right_side, image, left, part, left2, first, second),
        (f32(right_side.shape), f32(right_side.shape)),
        [pltpu.VMEM(right_side.shape, jnp.float32)] * 2 + [pltpu.SemaphoreType.DMA((2, parts))], 0, any_outs=2,
    )


def solution(mesh):
    in_specs = (P(None, "pts"), P("pts"), P(None, "pts"), P(None, "pts"), P("pts"))
    out_specs = (P(None, "pts"), P(None, "pts"))
    return jax.shard_map(body, mesh=mesh, in_specs=in_specs, out_specs=out_specs, check_vma=False)
```

time: 184 us -> 109 us (0.59)
  Pallas kernels: 168 us -> 94.8 us
  waiting for transfers between devices: 3.07 us -> 0.01 us
  other arithmetic: 1.68 us -> 4.25 us
    pallas_call x3 -> x4, Pallas kernels: 99.6 us -> 55.8 us  [local_call(): pl.pallas_call(kernel, out_shape=out_shape, in_specs=[SMEM] * smalls + [V...]
    pallas_call x2, Pallas kernels: 68.1 us -> 39 us  [exchange(): pl.pallas_call(functools.partial(exchange_kernel, both_ways, rows), out_s...]
    ppermute x1, waiting for transfers between devices: 3.07 us -> 0.01 us  [body(): halo = lax.ppermute(right_side[:, :width], 'pts', back)]
    unnamed x17 -> x4, local copies, waits for them, and re-layouts: 3.33 us -> 0.76 us
  transfers between devices with their start and end apart: 2 -> 2, of which waited for: 1 -> 0; matrix products, arithmetic and copies ran while one was open for 2% -> 6% of each run, Pallas kernels for 0% -> 22%
where the time goes in v2:
time: 109 us
  Pallas kernels  94.8 us (87%)
  starting transfers between devices  5.25 us (5%)
  other arithmetic  4.25 us (4%)
  local copies, waits for them, and re-layouts  3.55 us (3%)
    pallas_call x4, Pallas kernels, local_call(): pl.pallas_call(kernel, out_shape=out_shape, in_specs=[SMEM] * smalls + [V...  55.8 us
    pallas_call x2, Pallas kernels, exchange(): pl.pallas_call(functools.partial(exchange_kernel, both_ways, rows), out_s...  39 us
    ppermute x1, starting transfers between devices, body(): edge_pos = lax.ppermute(positions[:, :width], 'pts', back)  3.33 us
  transfers between devices with their start and end apart: 2, of which 0 were waited for; matrix products, arithmetic and copies ran while one was open for 6% of the time, Pallas kernels for 22%

profile of v2, /device:TPU:1, one launch (start us, length us, event | category | flops | bytes accessed | tf_op | source)
XLA Modules:
  0.0 108.6 jit_solution(1479150465609923906)
XLA Ops:
  0.6 0.0 copy-start
  0.6 0.9 fusion
  1.5 3.3 %collective-permute-start = (f32[3,2048]{1,0:T(4,128)S(1)}, f32[3,2048]{1,0:T(4,128)S(1)}, u32[]{:S(2)}, u32[]{:S(2)}) collective-permute-start(f32[3,2048]{1,0:T(4,128)S(1)} %get-tuple-element.53), channel_id=1, source_target_pairs={{1,0},{2,1},{3,2},{4,3},{5,4},{6,5},{7,6},{8,7},{9,8},{10,9},{11,1... | collective-permute-start | bytes 73736 | tf_op jit(solution)/shard_map/ppermute | solution.py:473
  4.9 1.0 slice.165
  5.8 1.9 %collective-permute-start.1 = (f32[32,2048]{1,0:T(8,128)S(1)}, f32[32,2048]{1,0:T(8,128)S(1)}, u32[]{:S(2)}, u32[]{:S(2)}) collective-permute-start(f32[32,2048]{1,0:T(8,128)S(1)} %slice.165), channel_id=1, source_target_pairs={{1,0},{2,1},{3,2},{4,3},{5,4},{6,5},{7,6},{8,7},{9,8},{10,9},{11,1... | collective-permute-start | bytes 786440 | tf_op jit(solution)/shard_map/ppermute | solution.py:474
  7.8 1.0 bitcast_reduce_fusion.1
  8.8 0.1 multiply_reduce_fusion
  8.9 0.1 multiply_reduce_fusion.3
  9.0 0.6 add_reduce_fusion
  9.6 0.7 pad_add_fusion.1.span_ref
  10.3 0.9 concatenate.19.pos_ref
  11.3 0.0 copy-done
  11.3 0.0 copy-start.1
  11.3 0.7 copy-done.1
  12.0 24.3 %shard_map.50 = (f32[32,10496]{1,0:T(8,128)S(1)}, f32[32,128]{1,0:T(8,128)S(1)}, bf16[17,8,2,256,256]{4,3,2,1,0:T(8,128)(2,1)}) custom-call(s32[25]{0:T(128)S(1)} %pad_add_fusion.1.span_ref, f32[8,8192]{1,0:T(8,128)S(1)} %concatenate.19.pos_ref, f32[1,8192]{1,0:T(1,128)S(1)} %bitcast.11, f32[32,8192]{1,0:T(8,128)S(1)} %copy-done), custom_call_target="tpu_custom_call" | custom-call | tf_op jit(solution)/shard_map/pallas_call | solution.py:332
  36.4 0.0 collective-permute-done
  36.4 0.1 bitcast_reduce_fusion.3
  36.5 0.1 multiply_reduce_fusion.8
  36.6 0.1 multiply_reduce_fusion.11
  36.7 0.6 add_reduce_fusion.1
  37.4 0.7 pad_add_fusion.span_ref.outer_ref
  38.1 0.0 collective-permute-done.1.halo_ref
  38.1 8.4 %shard_map.51 = (f32[32,10496]{1,0:T(8,128)S(1)}, f32[8,128]{1,0:T(8,128)S(1)}, bf16[9,8,2,256,256]{4,3,2,1,0:T(8,128)(2,1)}) custom-call(s32[9]{0:T(128)S(1)} %pad_add_fusion.span_ref.outer_ref, f32[8,4096]{1,0:T(8,128)S(1)} %concatenate.17.pos_ref, f32[32,8192]{1,0:T(8,128)S(1)} %copy-done, f32[32,2048]{1,0:T(8,128)S(1)} %collective-permute-done.1.halo_ref, ...), custom_call_target="tpu_custom_call" | custom-call | tf_op jit(solution)/shard_map/pallas_call | solution.py:332
  46.5 24.8 %shard_map.52 = (f32[32,2048]{1,0:T(8,128)S(1)}, f32[32,2048]{1,0:T(8,128)S(1)}, f32[8,128]{1,0:T(8,128)S(1)}) custom-call(f32[32,10496]{1,0:T(8,128)S(1)} %get-tuple-element.17.part_ref.image_ref, f32[8,128]{1,0:T(8,128)S(1)} %get-tuple-element.18.sums_ref), custom_call_target="tpu_custom_call" | custom-call | tf_op jit(solution)/shard_map/pallas_call | solution.py:396
  71.4 21.4 %shard_map.53 = (f32[32,10496]{1,0:T(8,128)S(1)}, f32[8,128]{1,0:T(8,128)S(1)}) custom-call(s32[25]{0:T(128)S(1)} %pad_add_fusion.1.span_ref, s32[9]{0:T(128)S(1)} %pad_add_fusion.span_ref.outer_ref, f32[8,8192]{1,0:T(8,128)S(1)} %concatenate.19.pos_ref, f32[1,8192]{1,0:T(1,128)S(1)} %bitcast.12, f32[32,8192]{1,0:T(8,128)S(1)} %copy-done, ...), custom_call_target="tpu_custom_call" | custom-call | tf_op jit(solution)/shard_map/pallas_call | solution.py:332
  92.7 14.2 %shard_map.54 = (f32[32,2048]{1,0:T(8,128)S(1)}, f32[8,128]{1,0:T(8,128)S(1)}) custom-call(f32[32,10496]{1,0:T(8,128)S(1)} %get-tuple-element.24.part_ref, f32[8,128]{1,0:T(8,128)S(1)} %get-tuple-element.25.sums_ref), custom_call_target="tpu_custom_call" | custom-call | tf_op jit(solution)/shard_map/pallas_call | solution.py:396
  107.0 1.6 %shard_map.55 = (f32[32,8192]{1,0:T(8,128)}, f32[32,8192]{1,0:T(8,128)}) custom-call(f32[32,8192]{1,0:T(8,128)S(1)} %copy-done, f32[32,10496]{1,0:T(8,128)S(1)} %get-tuple-element.17.part_ref.image_ref, f32[32,2048]{1,0:T(8,128)S(1)} %get-tuple-element.19.left_ref, f32[32,10496]{1,0:T(8,128)S(1)} %get-tuple-element.24.part_ref, ...), custom_call_target="tpu_custom_call" | custom-call | tf_op jit(solution)/shard_map/pallas_call | solution.py:332
  (2 shorter events, 0.0 us)
Async XLA Ops:
  0.6 10.7 %copy-start = (f32[32,8192]{1,0:T(8,128)S(1)}, f32[32,8192]{1,0:T(8,128)}, u32[]{:S(2)}) copy-start(f32[32,8192]{1,0:T(8,128)} %own_ref.7) | copy-start | bytes 3145732
  1.5 34.8 %collective-permute-start = (f32[3,2048]{1,0:T(4,128)S(1)}, f32[3,2048]{1,0:T(4,128)S(1)}, u32[]{:S(2)}, u32[]{:S(2)}) collective-permute-start(f32[3,2048]{1,0:T(4,128)S(1)} %get-tuple-element.53), channel_id=1, source_target_pairs={{1,0},{2,1},{3,2},{4,3},{5,4},{6,5},{7,6},{8,7},{9,8},{10,9},{11,1... | collective-permute-start | bytes 73736 | tf_op jit(solution)/shard_map/ppermute | solution.py:473
  5.8 32.3 %collective-permute-start.1 = (f32[32,2048]{1,0:T(8,128)S(1)}, f32[32,2048]{1,0:T(8,128)S(1)}, u32[]{:S(2)}, u32[]{:S(2)}) collective-permute-start(f32[32,2048]{1,0:T(8,128)S(1)} %slice.165), channel_id=1, source_target_pairs={{1,0},{2,1},{3,2},{4,3},{5,4},{6,5},{7,6},{8,7},{9,8},{10,9},{11,1... | collective-permute-start | bytes 786440 | tf_op jit(solution)/shard_map/ppermute | solution.py:474
  11.3 0.8 copy-start.1

commit v3 on v2

--- a/solution.py
+++ b/solution.py
@@ -15,9 +15,11 @@
 VMEM = pl.BlockSpec(memory_space=pltpu.VMEM)
 ANY = pl.BlockSpec(memory_space=pl.ANY)
 SMEM = pl.BlockSpec(memory_space=pltpu.SMEM)
+AHEAD = 3
 BATCH = 8
-TILES = (BATCH, 2, SUP, SUP)
-KEPT = 17
+EIGHT = jnp.float8_e4m3fn
+UNIT = 8.0
+KERNEL = UNIT**5 / 4
 GROUP = 8
 
 
@@ -56,11 +58,17 @@
     lax.fori_loop(0, rows, step, 0, unroll=4)
 
 
-def split(values):
-    values = 4.0 * values
+def scale_of(peak):
+    peak = jnp.max(peak, axis=1, keepdims=True)
+    return jnp.broadcast_to(224.0 / jnp.maximum(peak, 1e-30), (FRAMES, SUP))
+
+
+def hold(vals_ref, a, values):
+    high_ref, low_ref = vals_ref
+    low_ref[a] = values.astype(EIGHT)
     high = values.astype(jnp.bfloat16)
     low = (values - high.astype(jnp.float32)).astype(jnp.bfloat16)
-    return jnp.concatenate([high, low], axis=0)
+    high_ref[a] = jnp.concatenate([high, low], axis=0)
 
 
 def follower(span_ref, base, rows):
@@ -72,9 +80,9 @@
     return following
 
 
-def kernel_tile(pos_ref, rows_ref, a, c, store):
+def kernel_tile(pos_ref, rows_ref, a, c, high_ref, low_ref):
     highs, lows = [], []
-    step = 16
+    step = 32
     for i in range(0, SUP, step):
         pair = []
         for h in range(2):
@@ -84,130 +92,113 @@
                 diff = rows_ref[a, axis, i : i + step, :] - col
                 dist2 = diff * diff if axis == 0 else dist2 + diff * diff
             dist2 = jnp.maximum(dist2, TINY)
-            reach = jnp.maximum(1.0 - dist2 * lax.rsqrt(dist2), 0.0)
+            reach = jnp.maximum(UNIT - dist2 * lax.rsqrt(dist2), 0.0)
             square = reach * reach
-            kern = square * square * (1.25 - reach)
+            kern = square * square * (1.25 * UNIT - reach)
             high = kern.astype(jnp.bfloat16)
-            pair.append((high, (kern - high.astype(jnp.float32)).astype(jnp.bfloat16)))
+            pair.append((high, (kern - high.astype(jnp.float32)).astype(EIGHT)))
         highs.append(jnp.concatenate([p[0] for p in pair], axis=1))
         lows.append(jnp.concatenate([p[1] for p in pair], axis=1))
-        store(i, step, highs[-1], lows[-1])
+        high_ref[i : i + step, :] = highs[-1]
+        low_ref[i : i + step, :] = lows[-1]
     return jnp.concatenate(highs, axis=0), jnp.concatenate(lows, axis=0)
 
 
 def products(vals_ref, out_ref, base, a, c, high, low, valid):
-    row_vals, col_vals = vals_ref[a - base], vals_ref[c - base]
-    front = dot(col_vals, high, 1) + dot(col_vals, low, 1)
-    back = dot(row_vals, high, 0) + dot(row_vals, low, 0)
+    high_ref, low_ref = vals_ref
+    front = dot(high_ref[c - base], high, 1)
+    front = front[:FRAMES] + front[FRAMES:] + dot(low_ref[c - base], low, 1)
+    back = dot(high_ref[a - base], high, 0)
+    back = back[:FRAMES] + back[FRAMES:] + dot(low_ref[a - base], low, 0)
     unused = out_ref.shape[1] // SUP - 1
-    out_ref[:, lanes(jnp.where(valid, a, unused))] += front[:FRAMES] + front[FRAMES:]
-    out_ref[:, lanes(jnp.where(valid & (a != c), c, unused))] += back[:FRAMES] + back[FRAMES:]
+    out_ref[:, lanes(jnp.where(valid, a, unused))] += front
+    out_ref[:, lanes(jnp.where(valid & (a != c), c, unused))] += back
 
 
 def group_count(total):
     return (total + BATCH - 1) // BATCH
 
 
-def sweep(span_ref, pos_ref, rows_ref, vals_ref, out_ref, base, rows, keep_ref, stage_ref, sems):
+def moves(tiles, keep, g, save):
+    slot = lax.rem(g, 2)
+    stages, sems = tiles
+    out = []
+    for index in range(2):
+        here, there = stages[index].at[slot], keep[index].at[g]
+        src, dst = (here, there) if save else (there, here)
+        out.append(pltpu.make_async_copy(src, dst, sems.at[index, slot]))
+    return out
+
+
+def sweep(span_ref, pos_ref, rows_ref, vals_ref, out_ref, base, rows, keep, tiles):
     total = span_ref[rows]
     groups = group_count(total)
-    kept = jnp.minimum(groups, keep_ref.shape[0])
     following = follower(span_ref, base, rows)
-
-    def save(g):
-        slot = lax.rem(g, 2)
-        return pltpu.make_async_copy(stage_ref.at[slot], keep_ref.at[g], sems.at[slot])
+    highs, lows = tiles[0]
 
     def step(g, now):
         slot = lax.rem(g, 2)
 
-        @pl.when((g >= 2) & (g - 2 < kept))
+        @pl.when(g >= 2)
         def _():
-            save(g - 2).wait()
+            for copy in moves(tiles, keep, g - 2, True):
+                copy.wait()
 
         for u in range(BATCH):
             a, c = now
-
-            def store(i, step, high, low):
-                stage_ref[slot, u, 0, i : i + step, :] = high
-                stage_ref[slot, u, 1, i : i + step, :] = low
-
-            high, low = kernel_tile(pos_ref, rows_ref, a - base, c - base, store)
+            high, low = kernel_tile(pos_ref, rows_ref, a - base, c - base, highs.at[slot, u], lows.at[slot, u])
             products(vals_ref, out_ref, base, a, c, high, low, BATCH * g + u < total)
             now = following(a, c)
-
-        @pl.when(g < kept)
-        def _():
-            save(g).start()
-
+        for copy in moves(tiles, keep, g, True):
+            copy.start()
         return now
 
     lax.fori_loop(0, groups, step, (jnp.int32(base), jnp.int32(base)))
     for k in (2, 1):
-        g = groups - k
-
-        @pl.when((g >= 0) & (g < kept))
+        @pl.when(groups >= k)
         def _():
-            save(g).wait()
-
-
-def loader(kept, groups, keeps, stage_ref, sems):
-    def load(g, do):
-        slot = lax.rem(g, 2)
-
-        @pl.when(g < kept)
+            for copy in moves(tiles, keep, groups - k, True):
+                copy.wait()
+
+
+def fetch(keeps, counts, tiles, g, start):
+    for part, (first, end) in enumerate(((0, counts[0]), (counts[0], counts[0] + counts[1]))):
+        @pl.when((g >= first) & (g < end))
         def _():
-            do(pltpu.make_async_copy(keeps[0].at[g], stage_ref.at[slot], sems.at[slot]))
-
-        @pl.when((g >= kept) & (g < groups))
-        def _():
-            do(pltpu.make_async_copy(keeps[1].at[g - kept], stage_ref.at[slot], sems.at[slot]))
-
-    return load
-
-
-def first_load(spans, counts, keeps, stage_ref, sems):
-    kept = jnp.minimum(group_count(spans[0][counts[0]]), keeps[0].shape[0])
-    groups = kept + group_count(spans[1][counts[1]])
-    loader(kept, groups, keeps, stage_ref, sems)(jnp.int32(0), lambda copy: copy.start())
-
-
-def sweep_again(spans, bases, counts, keeps, pos_ref, rows_ref, vals_ref, out_ref, stage_ref, sems):
-    totals = [span[rows] for span, rows in zip(spans, counts)]
-    kept = jnp.minimum(group_count(totals[0]), keeps[0].shape[0])
-    groups = kept + group_count(totals[1])
-    followers = [follower(*part) for part in zip(spans, bases, counts)]
-
-    load = loader(kept, groups, keeps, stage_ref, sems)
-
-    def part(index, first, end, now):
-        def step(g, now):
-            slot = lax.rem(g, 2)
-            load(g + 1, lambda copy: copy.start())
-            load(g, lambda copy: copy.wait())
+            slot = lax.rem(g, AHEAD + 1)
+            for index in range(2):
+                src, dst = keeps[2 * part + index].at[g - first], tiles[0][index].at[slot]
+                sem = tiles[1].at[index, slot]
+                copy = pltpu.make_async_copy(src, dst, sem)
+                if start:
+                    copy.start()
+                else:
+                    copy.wait()
+
+
+def sweep_again(spans, bases, rows, vals_ref, out_ref, keeps, tiles):
+    totals = [span[n] for span, n in zip(spans, rows)]
+    counts = [group_count(total) for total in totals]
+    highs, lows = tiles[0]
+    first = 0
+    for part in range(2):
+        following = follower(spans[part], bases[part], rows[part])
+
+        def step(g, now, first=first, total=totals[part], following=following):
+            slot = lax.rem(g, AHEAD + 1)
+            fetch(keeps, counts, tiles, g + AHEAD, True)
+            fetch(keeps, counts, tiles, g, False)
             for u in range(BATCH):
                 a, c = now
-                valid = BATCH * (g - first) + u < totals[index]
-                products(vals_ref, out_ref, 0, a, c, stage_ref[slot, u, 0], stage_ref[slot, u, 1], valid)
-                now = followers[index](a, c)
+                products(
+                    vals_ref, out_ref, 0, a, c, highs[slot, u], lows[slot, u], BATCH * (g - first) + u < total
+                )
+                now = following(a, c)
             return now
 
-        return lax.fori_loop(first, end, step, (jnp.int32(now), jnp.int32(now)))
-
-    reached = part(0, 0, kept, bases[0])
-    part(1, kept, groups, bases[1])
-
-    @pl.when(BATCH * kept < totals[0])
-    def _():
-        spread_rows(pos_ref, rows_ref, counts[0])
-
-        def step(t, now):
-            a, c = now
-            high, low = kernel_tile(pos_ref, rows_ref, a, c, lambda *_: None)
-            products(vals_ref, out_ref, 0, a, c, high, low, True)
-            return followers[0](a, c)
-
-        lax.fori_loop(BATCH * kept, totals[0], step, reached)
+        start = jnp.int32(bases[part])
+        lax.fori_loop(first, first + counts[part], step, (start, start))
+        first = first + counts[part]
 
 
 def lane_totals(quantities):
@@ -236,62 +227,107 @@
     return lax.fori_loop(low, high, step, start, unroll=4)
 
 
-def inner_kernel(span_ref, pos_ref, noise_ref, own_ref, out_ref, norm_ref, keep_ref, rows_ref, vals_ref, stage_ref, sems):
+def clear(out_ref, first, count):
+    def step(a, _):
+        out_ref[:, lanes(first + a)] = jnp.zeros((FRAMES, SUP), jnp.float32)
+        return 0
+
+    loop(0, count, step, 0)
+
+
+def larger(peak, values):
+    values = jnp.abs(values)
+    return jnp.maximum(peak, jnp.maximum(values[:, :128], values[:, 128:]))
+
+
+def inner_kernel(
+    span_ref, pos_ref, noise_ref, own_ref, out_ref, norm_ref, keep_high, keep_low, rows_ref, high_ref, low_ref, *stage
+):
     rows = own_ref.shape[1] // SUP
+    vals_ref, tiles = (high_ref, low_ref), (stage[:2], stage[2])
+    scale = scale_of(loop(0, rows, lambda a, peak: larger(peak, own_ref[:, lanes(a)]), zeros()))
     spread_rows(pos_ref, rows_ref, rows - HALO)
+    clear(out_ref, 0, rows)
 
     def begin(a, norm):
         values = own_ref[:, lanes(a)]
-        vals_ref[a] = split(values)
-        out_ref[:, lanes(a)] = noise_ref[:, lanes(a)] * values
+        hold(vals_ref, a, scale * values)
         return norm + fold(values * values)
 
     norm_ref[...] = loop(0, rows, begin, zeros())
-    sweep(span_ref, pos_ref, rows_ref, vals_ref, out_ref, 0, rows - HALO, keep_ref, stage_ref, sems)
+    sweep(span_ref, pos_ref, rows_ref, vals_ref, out_ref, 0, rows - HALO, (keep_high, keep_low), tiles)
+    inverse = 1.0 / (KERNEL * scale)
+
+    def finish(a, _):
+        at = lanes(a)
+        out_ref[:, at] = out_ref[:, at] * inverse + noise_ref[:, at] * own_ref[:, at]
+        return 0
+
+    loop(0, rows, finish, 0)
 
 
 def outer_kernel(
-    span_ref, pos_ref, own_ref, halo_ref, norm_ref, begun_ref, out_ref, sums_ref, keep_ref, rows_ref, vals_ref, stage_ref, sems
+    span_ref, pos_ref, own_ref, halo_ref, norm_ref, begun_ref, out_ref, sums_ref, keep_high, keep_low,
+    rows_ref, high_ref, low_ref, *stage
 ):
     rows = own_ref.shape[1] // SUP
     base = rows - HALO
+    vals_ref, tiles = (high_ref, low_ref), (stage[:2], stage[2])
+
+    def peaks(a, peak):
+        return larger(larger(peak, own_ref[:, lanes(base + a)]), halo_ref[:, lanes(a)])
+
+    scale = scale_of(loop(0, HALO, peaks, zeros()))
     spread_rows(pos_ref, rows_ref, HALO)
+    clear(out_ref, base, 2 * HALO)
 
     def begin(a, _):
-        vals_ref[a] = split(own_ref[:, lanes(base + a)])
-        vals_ref[HALO + a] = split(halo_ref[:, lanes(a)])
-        out_ref[:, lanes(rows + a)] = jnp.zeros((FRAMES, SUP), jnp.float32)
+        hold(vals_ref, a, scale * own_ref[:, lanes(base + a)])
+        hold(vals_ref, HALO + a, scale * halo_ref[:, lanes(a)])
         return 0
 
-    def resume(a, _):
-        out_ref[:, lanes(a)] = begun_ref[:, lanes(a)]
-        return 0
-
-    loop(0, rows, resume, 0)
     loop(0, HALO, begin, 0)
-    sweep(span_ref, pos_ref, rows_ref, vals_ref, out_ref, base, HALO, keep_ref, stage_ref, sems)
-    curve = loop(0, rows, lambda a, s: s + fold(own_ref[:, lanes(a)] * out_ref[:, lanes(a)]), zeros())
-    curve = loop(0, HALO, lambda a, s: s + fold(halo_ref[:, lanes(a)] * out_ref[:, lanes(rows + a)]), curve)
+    sweep(span_ref, pos_ref, rows_ref, vals_ref, out_ref, base, HALO, (keep_high, keep_low), tiles)
+    inverse = 1.0 / (KERNEL * scale)
+
+    def rest(a, curve):
+        at = lanes(a)
+        image = begun_ref[:, at]
+        out_ref[:, at] = image
+        return curve + fold(own_ref[:, at] * image)
+
+    def edge(a, curve):
+        at = lanes(base + a)
+        image = begun_ref[:, at] + out_ref[:, at] * inverse
+        out_ref[:, at] = image
+        curve = curve + fold(own_ref[:, at] * image)
+        at = lanes(rows + a)
+        image = out_ref[:, at] * inverse
+        out_ref[:, at] = image
+        return curve + fold(halo_ref[:, lanes(a)] * image)
+
+    curve = loop(0, HALO, edge, loop(0, base, rest, zeros()))
     sums_ref[...] = lane_totals([norm_ref[...], curve])
 
 
 def second_kernel(
-    span_ref, outer_ref, pos_ref, noise_ref, own_ref, halo_ref, image_ref, left_ref, right_ref, first_ref, keep_ref, keep2_ref,
-    out_ref, sums_ref, rows_ref, vals_ref, resid_ref, stage_ref, sems
+    span_ref, outer_ref, noise_ref, own_ref, halo_ref, image_ref, left_ref, right_ref, first_ref, *refs
 ):
+    keeps, (out_ref, sums_ref, high_ref, low_ref, resid_ref), stage = refs[:4], refs[4:9], refs[9:]
+    vals_ref, tiles = (high_ref, low_ref), (stage[:2], stage[2])
     rows = own_ref.shape[1] // SUP
     spans, bases, counts = (span_ref, outer_ref), (0, rows - HALO), (rows - HALO, HALO)
-    keeps = (keep_ref, keep2_ref)
-    first_load(spans, counts, keeps, stage_ref, sems)
+    for g in range(AHEAD):
+        fetch(keeps, [group_count(span[n]) for span, n in zip(spans, counts)], tiles, jnp.int32(g), True)
     norm_before, curve_before = frame_columns(first_ref[0:1])[:2]
     alpha = wide(norm_before / curve_before)
 
     def begin(a, image, values, sums):
         residual = values - alpha * image
-        vals_ref[a] = split(residual)
         resid_ref[:, lanes(a)] = residual
-        out_ref[:, lanes(a)] = noise_ref[:, lanes(a)] * residual
-        return (sums[0] + fold(residual * residual), sums[1] + fold(residual * image))
+        return (
+            sums[0] + fold(residual * residual), sums[1] + fold(residual * image), larger(sums[2], residual)
+        )
 
     def begin_first(a, sums):
         return begin(a, image_ref[:, lanes(a)] + left_ref[:, lanes(a)], own_ref[:, lanes(a)], sums)
@@ -299,32 +335,88 @@
     def begin_rest(a, sums):
         return begin(a, image_ref[:, lanes(a)], own_ref[:, lanes(a)], sums)
 
-    sums = loop(0, HALO, begin_first, (zeros(), zeros()))
-    norm, cross = loop(HALO, rows, begin_rest, sums)
-
-    def begin_halo(a, _):
+    sums = loop(0, HALO, begin_first, (zeros(), zeros(), zeros()))
+    norm, cross, peak = loop(HALO, rows, begin_rest, sums)
+
+    def begin_halo(a, peak):
         image = image_ref[:, lanes(rows + a)] + right_ref[:, lanes(a)]
         residual = halo_ref[:, lanes(a)] - alpha * image
-        vals_ref[rows + a] = split(residual)
         resid_ref[:, lanes(rows + a)] = residual
-        out_ref[:, lanes(rows + a)] = jnp.zeros((FRAMES, SUP), jnp.float32)
+        return larger(peak, residual)
+
+    scale = scale_of(loop(0, HALO, begin_halo, peak))
+
+    def ready(a, _):
+        hold(vals_ref, a, scale * resid_ref[:, lanes(a)])
         return 0
 
-    loop(0, HALO, begin_halo, 0)
-    sweep_again(spans, bases, counts, keeps, pos_ref, rows_ref, vals_ref, out_ref, stage_ref, sems)
-    curve = loop(0, rows + HALO, lambda a, s: s + fold(resid_ref[:, lanes(a)] * out_ref[:, lanes(a)]), zeros())
+    loop(0, rows + HALO, ready, 0)
+    clear(out_ref, 0, rows + HALO)
+    sweep_again(spans, bases, counts, vals_ref, out_ref, keeps, tiles)
+    inverse = 1.0 / (KERNEL * scale)
+
+    def finish(a, curve):
+        at = lanes(a)
+        image = out_ref[:, at] * inverse + noise_ref[:, at] * resid_ref[:, at]
+        out_ref[:, at] = image
+        return curve + fold(resid_ref[:, at] * image)
+
+    def finish_halo(a, curve):
+        at = lanes(rows + a)
+        image = out_ref[:, at] * inverse
+        out_ref[:, at] = image
+        return curve + fold(resid_ref[:, at] * image)
+
+    curve = loop(0, HALO, finish_halo, loop(0, rows, finish, zeros()))
     sums_ref[...] = lane_totals([norm, curve, cross])
 
 
-def field_scratch(rows_held, vals_held):
+def vals_scratch(count):
     return [
-        pltpu.VMEM((rows_held, 3, SUP, 128), jnp.float32),
-        pltpu.VMEM((vals_held, 2 * FRAMES, SUP), jnp.bfloat16),
+        pltpu.VMEM((count, 2 * FRAMES, SUP), jnp.bfloat16),
+        pltpu.VMEM((count, FRAMES, SUP), EIGHT),
     ]
 
 
-def stage_scratch():
-    return [pltpu.VMEM((2,) + TILES, jnp.bfloat16), pltpu.SemaphoreType.DMA((2,))]
+def stage_scratch(slots):
+    return [
+        pltpu.VMEM((slots, BATCH, SUP, SUP), jnp.bfloat16),
+        pltpu.VMEM((slots, BATCH, SUP, SUP), EIGHT),
+        pltpu.SemaphoreType.DMA((2, slots)),
+    ]
+
+
+def kept(rows):
+    steps = -(-rows * (HALO + 1) // BATCH)
+    shape = (steps, BATCH, SUP, SUP)
+    return jax.ShapeDtypeStruct(shape, jnp.bfloat16), jax.ShapeDtypeStruct(shape, EIGHT)
+
+
+def first_pass(span, outer_span, positions, edge_pos, noise, right_side, halo):
+    rows = positions.shape[1] // SUP
+    inner = rows - HALO
+    field = f32((FRAMES, (rows + HALO + 1) * SUP))
+    spread = pltpu.VMEM((inner, 3, SUP, 128), jnp.float32)
+    image, norm, *keep = local_call(
+        inner_kernel, (span, padded(positions), noise, right_side), (field, f32((FRAMES, 128))) + kept(inner),
+        [spread] + vals_scratch(rows) + stage_scratch(2), 1, any_outs=2,
+    )
+    outer_pos = padded(jnp.concatenate([positions[:, inner * SUP :], edge_pos], axis=1))
+    spread = pltpu.VMEM((HALO, 3, SUP, 128), jnp.float32)
+    image, sums, *keep_outer = local_call(
+        outer_kernel, (outer_span, outer_pos, right_side, halo, norm, image), (field, f32((8, 128))) + kept(HALO),
+        [spread] + vals_scratch(2 * HALO) + stage_scratch(2), 1, any_outs=2,
+    )
+    return image, sums, keep + keep_outer
+
+
+def second_pass(span, outer_span, noise, right_side, halo, image, left, right, first, keeps):
+    extent = right_side.shape[1] // SUP + HALO
+    return local_call(
+        second_kernel, (span, outer_span, noise, right_side, halo, image, left, right, first, *keeps),
+        (f32((FRAMES, (extent + 1) * SUP)), f32((8, 128))),
+        vals_scratch(extent) + [pltpu.VMEM((FRAMES, extent * SUP), jnp.float32)] + stage_scratch(AHEAD + 1), 2, anys=4,
+    )
 
 
 def local_call(kernel, operands, out_shape, scratch, smalls, anys=0, any_outs=0):
@@ -461,7 +553,7 @@
 
 
 def padded(positions):
-    return jnp.concatenate([positions, jnp.zeros((5, positions.shape[1]), jnp.float32)], axis=0)
+    return UNIT * jnp.concatenate([positions, jnp.zeros((5, positions.shape[1]), jnp.float32)], axis=0)
 
 
 def body(positions, noise, right_side, pairs, counts):
@@ -472,33 +564,13 @@
     back = [(i + 1, i) for i in range(size - 1)]
     edge_pos = lax.ppermute(positions[:, :width], "pts", back)
     halo = lax.ppermute(right_side[:, :width], "pts", back)
-    pos = padded(positions)
     noise = noise.reshape(1, -1)
-    field = f32((FRAMES, (rows + HALO + 1) * SUP))
-    small = f32((FRAMES, 128))
     span = spans(positions, inner, rows)
-    image, norm, keep = local_call(
-        inner_kernel, (span, pos, noise, right_side),
-        (field, small, jax.ShapeDtypeStruct((KEPT,) + TILES, jnp.bfloat16)),
-        field_scratch(inner, rows) + stage_scratch(), 1, any_outs=1,
-    )
     outer_pos = jnp.concatenate([positions[:, inner * SUP :], edge_pos], axis=1)
-    alone = lax.axis_index("pts") == size - 1
-    outer_span = spans(outer_pos, HALO, jnp.where(alone, HALO, 2 * HALO))
-    steps = -(-HALO * (HALO + 1) // BATCH)
-    image, sums, keep2 = local_call(
-        outer_kernel, (outer_span, padded(outer_pos), right_side, halo, norm, image),
-        (field, f32((8, 128)), jax.ShapeDtypeStruct((steps,) + TILES, jnp.bfloat16)),
-        field_scratch(HALO, 2 * HALO) + stage_scratch(), 1, any_outs=1,
-    )
+    outer_span = spans(outer_pos, HALO, jnp.where(lax.axis_index("pts") == size - 1, HALO, 2 * HALO))
+    image, sums, keeps = first_pass(span, outer_span, positions, edge_pos, noise, right_side, halo)
     left, right, first = exchange(image, sums, rows, True, 0)
-    part, sums = local_call(
-        second_kernel,
-        (span, outer_span, pos, noise, right_side, halo, image, left, right, first, keep, keep2),
-        (field, f32((8, 128))),
-        field_scratch(inner, rows + HALO) + [pltpu.VMEM((FRAMES, (rows + HALO) * SUP), jnp.float32)] + stage_scratch(),
-        2, anys=2,
-    )
+    part, sums = second_pass(span, outer_span, noise, right_side, halo, image, left, right, first, keeps)
     left2, second = exchange(part, sums, rows, False, 1)
     parts = rows // HALO
     return local_call(

time: 109 us -> 113 us (1.037)
  Pallas kernels: 94.8 us -> 96.4 us
  local copies, waits for them, and re-layouts: 3.55 us -> 5.06 us
    pallas_call x2, Pallas kernels: 39 us -> 43.4 us  [exchange(): pl.pallas_call(functools.partial(exchange_kernel, both_ways, rows), out_s...]
    pallas_call x4, Pallas kernels: 55.8 us -> 53 us  [local_call(): pl.pallas_call(kernel, out_shape=out_shape, in_specs=[SMEM] * smalls + [V...]
    unnamed x4 -> x8, local copies, waits for them, and re-layouts: 0.76 us -> 3.21 us
  transfers between devices with their start and end apart: 2 -> 2, of which waited for: 0 -> 0; matrix products, arithmetic and copies ran while one was open for 6% -> 5% of each run, Pallas kernels for 22% -> 23%
where the time goes in v3:
time: 113 us
  Pallas kernels  96.4 us (85%)
  starting transfers between devices  5.25 us (5%)
  other arithmetic  5.2 us (5%)
  local copies, waits for them, and re-layouts  5.06 us (4%)
    pallas_call x4, Pallas kernels, local_call(): pl.pallas_call(kernel, out_shape=out_shape, in_specs=[SMEM] * smalls + [V...  53 us
    pallas_call x2, Pallas kernels, exchange(): pl.pallas_call(functools.partial(exchange_kernel, both_ways, rows), out_s...  43.4 us
    ppermute x1, starting transfers between devices, body(): edge_pos = lax.ppermute(positions[:, :width], 'pts', back)  3.33 us
    unnamed x8, local copies, waits for them, and re-layouts  3.21 us
  transfers between devices with their start and end apart: 2, of which 0 were waited for; matrix products, arithmetic and copies ran while one was open for 5% of the time, Pallas kernels for 23%

profile of v3, /device:TPU:1, one launch (start us, length us, event | category | flops | bytes accessed | tf_op | source)
XLA Modules:
  0.0 112.7 jit_solution(12229172146361494861)
XLA Ops:
  0.6 0.0 copy-start.2
  0.6 0.9 fusion
  1.5 3.3 %collective-permute-start = (f32[3,2048]{1,0:T(4,128)S(1)}, f32[3,2048]{1,0:T(4,128)S(1)}, u32[]{:S(2)}, u32[]{:S(2)}) collective-permute-start(f32[3,2048]{1,0:T(4,128)S(1)} %get-tuple-element.57), channel_id=1, source_target_pairs={{1,0},{2,1},{3,2},{4,3},{5,4},{6,5},{7,6},{8,7},{9,8},{10,9},{11,1... | collective-permute-start | bytes 73736 | tf_op jit(solution)/shard_map/ppermute | solution.py:565
  4.9 1.0 slice.166
  5.8 1.9 %collective-permute-start.1 = (f32[32,2048]{1,0:T(8,128)S(1)}, f32[32,2048]{1,0:T(8,128)S(1)}, u32[]{:S(2)}, u32[]{:S(2)}) collective-permute-start(f32[32,2048]{1,0:T(8,128)S(1)} %slice.166), channel_id=1, source_target_pairs={{1,0},{2,1},{3,2},{4,3},{5,4},{6,5},{7,6},{8,7},{9,8},{10,9},{11,1... | collective-permute-start | bytes 786440 | tf_op jit(solution)/shard_map/ppermute | solution.py:566
  7.8 1.0 bitcast_reduce_fusion.1
  8.8 0.1 multiply_reduce_fusion
  8.9 0.1 multiply_reduce_fusion.3
  9.0 0.9 pad_multiply_fusion.pos_ref
  9.9 0.6 add_reduce_fusion
  10.6 0.7 pad_add_fusion.1.span_ref
  11.3 0.0 copy-start
  11.3 1.2 %copy-done = f32[32,8192]{1,0:T(8,128)S(1)} copy-done((f32[32,8192]{1,0:T(8,128)S(1)}, f32[32,8192]{1,0:T(8,128)}, u32[]{:S(2)}) %copy-start) | copy-done | bytes 1048600
  12.5 0.0 copy-start.3
  12.5 0.8 copy-done.3
  13.3 25.4 %shard_map.50 = (f32[32,10496]{1,0:T(8,128)S(1)}, f32[32,128]{1,0:T(8,128)S(1)}, bf16[27,8,256,256]{3,2,1,0:T(8,128)(2,1)}, f8e4m3fn[27,8,256,256]{3,2,1,0:T(32,128)(4,1)}) custom-call(s32[25]{0:T(128)S(1)} %pad_add_fusion.1.span_ref, f32[8,8192]{1,0:T(8,128)S(1)} %pad_multiply_fusion.pos_ref, f32[1,8192]{1,0:T(1,128)S(1)} %bitcast.11, f32[32,8192]{1,0:T(8,128)S(1)} %copy-done), custom_call_target="tpu_custom_call" | custom-call | tf_op jit(solution)/shard_map/pallas_call | solution.py:424
  38.7 0.0 collective-permute-done
  38.7 0.1 bitcast_reduce_fusion.3
  38.8 0.1 multiply_reduce_fusion.8
  38.9 0.1 multiply_reduce_fusion.11
  39.0 0.6 add_reduce_fusion.1
  39.7 0.7 pad_add_fusion.span_ref.outer_ref
  40.4 0.0 collective-permute-done.1.halo_ref
  40.4 0.0 copy-start.1
  40.4 1.2 %copy-done.1 = f32[32,8192]{1,0:T(8,128)S(1)} copy-done((f32[32,8192]{1,0:T(8,128)S(1)}, f32[32,8192]{1,0:T(8,128)}, u32[]{:S(2)}) %copy-start.1) | copy-done | bytes 1048600
  41.6 9.8 %shard_map.51 = (f32[32,10496]{1,0:T(8,128)S(1)}, f32[8,128]{1,0:T(8,128)S(1)}, bf16[9,8,256,256]{3,2,1,0:T(8,128)(2,1)}, f8e4m3fn[9,8,256,256]{3,2,1,0:T(32,128)(4,1)S(1)}) custom-call(s32[9]{0:T(128)S(1)} %pad_add_fusion.span_ref.outer_ref, f32[8,4096]{1,0:T(8,128)S(1)} %pad_multiply_fusion.1.pos_ref, f32[32,8192]{1,0:T(8,128)S(1)} %copy-done.1, ...), custom_call_target="tpu_custom_call" | custom-call | tf_op jit(solution)/shard_map/pallas_call | solution.py:424
  51.5 27.6 %shard_map.52 = (f32[32,2048]{1,0:T(8,128)S(1)}, f32[32,2048]{1,0:T(8,128)S(1)}, f32[8,128]{1,0:T(8,128)S(1)}) custom-call(f32[32,10496]{1,0:T(8,128)S(1)} %get-tuple-element.19.part_ref.image_ref, f32[8,128]{1,0:T(8,128)S(1)} %get-tuple-element.20.sums_ref), custom_call_target="tpu_custom_call" | custom-call | tf_op jit(solution)/shard_map/pallas_call | solution.py:488
  79.1 0.0 copy-done.2
  79.1 16.1 %shard_map.53 = (f32[32,10496]{1,0:T(8,128)S(1)}, f32[8,128]{1,0:T(8,128)S(1)}) custom-call(s32[25]{0:T(128)S(1)} %pad_add_fusion.1.span_ref, s32[9]{0:T(128)S(1)} %pad_add_fusion.span_ref.outer_ref, f32[1,8192]{1,0:T(1,128)S(1)} %bitcast.12, f32[32,8192]{1,0:T(8,128)S(1)} %copy-done.2, f32[32,2048]{1,0:T(8,128)S(1)} %collective-permute-done.1.halo_ref, ...), custom_call_target="tpu_custom_call" | custom-call | tf_op jit(solution)/shard_map/pallas_call | solution.py:424
  95.2 15.8 %shard_map.54 = (f32[32,2048]{1,0:T(8,128)S(1)}, f32[8,128]{1,0:T(8,128)S(1)}) custom-call(f32[32,10496]{1,0:T(8,128)S(1)} %get-tuple-element.28.part_ref, f32[8,128]{1,0:T(8,128)S(1)} %get-tuple-element.29.sums_ref), custom_call_target="tpu_custom_call" | custom-call | tf_op jit(solution)/shard_map/pallas_call | solution.py:488
  111.0 1.6 %shard_map.55 = (f32[32,8192]{1,0:T(8,128)}, f32[32,8192]{1,0:T(8,128)}) custom-call(f32[32,8192]{1,0:T(8,128)S(1)} %copy-done.2, f32[32,10496]{1,0:T(8,128)S(1)} %get-tuple-element.19.part_ref.image_ref, f32[32,2048]{1,0:T(8,128)S(1)} %get-tuple-element.21.left_ref, f32[32,10496]{1,0:T(8,128)S(1)} %get-tuple-element.28.part_ref, ...), custom_call_target="tpu_custom_call" | custom-call | tf_op jit(solution)/shard_map/pallas_call | solution.py:424
  (2 shorter events, 0.0 us)
Async XLA Ops:
  0.6 78.4 %copy-start.2 = (f32[32,8192]{1,0:T(8,128)S(1)}, f32[32,8192]{1,0:T(8,128)}, u32[]{:S(2)}) copy-start(f32[32,8192]{1,0:T(8,128)} %own_ref.7) | copy-start | bytes 3145732
  1.5 37.2 %collective-permute-start = (f32[3,2048]{1,0:T(4,128)S(1)}, f32[3,2048]{1,0:T(4,128)S(1)}, u32[]{:S(2)}, u32[]{:S(2)}) collective-permute-start(f32[3,2048]{1,0:T(4,128)S(1)} %get-tuple-element.57), channel_id=1, source_target_pairs={{1,0},{2,1},{3,2},{4,3},{5,4},{6,5},{7,6},{8,7},{9,8},{10,9},{11,1... | collective-permute-start | bytes 73736 | tf_op jit(solution)/shard_map/ppermute | solution.py:565
  5.8 34.6 %collective-permute-start.1 = (f32[32,2048]{1,0:T(8,128)S(1)}, f32[32,2048]{1,0:T(8,128)S(1)}, u32[]{:S(2)}, u32[]{:S(2)}) collective-permute-start(f32[32,2048]{1,0:T(8,128)S(1)} %slice.166), channel_id=1, source_target_pairs={{1,0},{2,1},{3,2},{4,3},{5,4},{6,5},{7,6},{8,7},{9,8},{10,9},{11,1... | collective-permute-start | bytes 786440 | tf_op jit(solution)/shard_map/ppermute | solution.py:566
  11.3 1.2 %copy-start = (f32[32,8192]{1,0:T(8,128)S(1)}, f32[32,8192]{1,0:T(8,128)}, u32[]{:S(2)}) copy-start(f32[32,8192]{1,0:T(8,128)} %own_ref.7) | copy-start | bytes 3145732
  12.5 0.8 copy-start.3
  40.4 1.2 %copy-start.1 = (f32[32,8192]{1,0:T(8,128)S(1)}, f32[32,8192]{1,0:T(8,128)}, u32[]{:S(2)}) copy-start(f32[32,8192]{1,0:T(8,128)} %own_ref.7) | copy-start | bytes 3145732

commit v4 on v3

--- a/solution.py
+++ b/solution.py
@@ -71,10 +71,10 @@
     high_ref[a] = jnp.concatenate([high, low], axis=0)
 
 
-def follower(span_ref, base, rows):
+def follower(span_ref, rows):
     def following(a, c):
-        last = c >= a + span_ref[a - base]
-        a_next = jnp.minimum(jnp.where(last, a + 1, a), base + rows - 1)
+        last = c >= a + span_ref[0, a]
+        a_next = jnp.minimum(jnp.where(last, a + 1, a), rows - 1)
         return a_next, jnp.where(last, a_next, c + 1)
 
     return following
@@ -104,12 +104,12 @@
     return jnp.concatenate(highs, axis=0), jnp.concatenate(lows, axis=0)
 
 
-def products(vals_ref, out_ref, base, a, c, high, low, valid):
+def products(vals_ref, out_ref, a, c, high, low, valid):
     high_ref, low_ref = vals_ref
-    front = dot(high_ref[c - base], high, 1)
-    front = front[:FRAMES] + front[FRAMES:] + dot(low_ref[c - base], low, 1)
-    back = dot(high_ref[a - base], high, 0)
-    back = back[:FRAMES] + back[FRAMES:] + dot(low_ref[a - base], low, 0)
+    front = dot(high_ref[c], high, 1)
+    front = front[:FRAMES] + front[FRAMES:] + dot(low_ref[c], low, 1)
+    back = dot(high_ref[a], high, 0)
+    back = back[:FRAMES] + back[FRAMES:] + dot(low_ref[a], low, 0)
     unused = out_ref.shape[1] // SUP - 1
     out_ref[:, lanes(jnp.where(valid, a, unused))] += front
     out_ref[:, lanes(jnp.where(valid & (a != c), c, unused))] += back
@@ -119,8 +119,8 @@
     return (total + BATCH - 1) // BATCH
 
 
-def moves(tiles, keep, g, save):
-    slot = lax.rem(g, 2)
+def moves(tiles, keep, g, slots, save):
+    slot = lax.rem(g, slots)
     stages, sems = tiles
     out = []
     for index in range(2):
@@ -130,10 +130,10 @@
     return out
 
 
-def sweep(span_ref, pos_ref, rows_ref, vals_ref, out_ref, base, rows, keep, tiles):
-    total = span_ref[rows]
+def sweep(span_ref, pos_ref, rows_ref, vals_ref, out_ref, rows, keep, tiles):
+    total = span_ref[0, rows]
     groups = group_count(total)
-    following = follower(span_ref, base, rows)
+    following = follower(span_ref, rows)
     highs, lows = tiles[0]
 
     def step(g, now):
@@ -141,64 +141,53 @@
 
         @pl.when(g >= 2)
         def _():
-            for copy in moves(tiles, keep, g - 2, True):
+            for copy in moves(tiles, keep, g - 2, 2, True):
                 copy.wait()
 
         for u in range(BATCH):
             a, c = now
-            high, low = kernel_tile(pos_ref, rows_ref, a - base, c - base, highs.at[slot, u], lows.at[slot, u])
-            products(vals_ref, out_ref, base, a, c, high, low, BATCH * g + u < total)
+            high, low = kernel_tile(pos_ref, rows_ref, a, c, highs.at[slot, u], lows.at[slot, u])
+            products(vals_ref, out_ref, a, c, high, low, BATCH * g + u < total)
             now = following(a, c)
-        for copy in moves(tiles, keep, g, True):
+        for copy in moves(tiles, keep, g, 2, True):
             copy.start()
         return now
 
-    lax.fori_loop(0, groups, step, (jnp.int32(base), jnp.int32(base)))
+    lax.fori_loop(0, groups, step, (jnp.int32(0), jnp.int32(0)))
     for k in (2, 1):
         @pl.when(groups >= k)
         def _():
-            for copy in moves(tiles, keep, groups - k, True):
+            for copy in moves(tiles, keep, groups - k, 2, True):
                 copy.wait()
 
 
-def fetch(keeps, counts, tiles, g, start):
-    for part, (first, end) in enumerate(((0, counts[0]), (counts[0], counts[0] + counts[1]))):
-        @pl.when((g >= first) & (g < end))
-        def _():
-            slot = lax.rem(g, AHEAD + 1)
-            for index in range(2):
-                src, dst = keeps[2 * part + index].at[g - first], tiles[0][index].at[slot]
-                sem = tiles[1].at[index, slot]
-                copy = pltpu.make_async_copy(src, dst, sem)
-                if start:
-                    copy.start()
-                else:
-                    copy.wait()
-
-
-def sweep_again(spans, bases, rows, vals_ref, out_ref, keeps, tiles):
-    totals = [span[n] for span, n in zip(spans, rows)]
-    counts = [group_count(total) for total in totals]
+def fetch(keep, groups, tiles, g, begin):
+    @pl.when(g < groups)
+    def _():
+        for copy in moves(tiles, keep, g, AHEAD + 1, False):
+            if begin:
+                copy.start()
+            else:
+                copy.wait()
+
+
+def sweep_again(span_ref, rows, vals_ref, out_ref, keep, tiles):
+    total = span_ref[0, rows]
+    groups = group_count(total)
+    following = follower(span_ref, rows)
     highs, lows = tiles[0]
-    first = 0
-    for part in range(2):
-        following = follower(spans[part], bases[part], rows[part])
-
-        def step(g, now, first=first, total=totals[part], following=following):
-            slot = lax.rem(g, AHEAD + 1)
-            fetch(keeps, counts, tiles, g + AHEAD, True)
-            fetch(keeps, counts, tiles, g, False)
-            for u in range(BATCH):
-                a, c = now
-                products(
-                    vals_ref, out_ref, 0, a, c, highs[slot, u], lows[slot, u], BATCH * (g - first) + u < total
-                )
-                now = following(a, c)
-            return now
-
-        start = jnp.int32(bases[part])
-        lax.fori_loop(first, first + counts[part], step, (start, start))
-        first = first + counts[part]
+
+    def step(g, now):
+        slot = lax.rem(g, AHEAD + 1)
+        fetch(keep, groups, tiles, g + AHEAD, True)
+        fetch(keep, groups, tiles, g, False)
+        for u in range(BATCH):
+            a, c = now
+            products(vals_ref, out_ref, a, c, highs[slot, u], lows[slot, u], BATCH * g + u < total)
+            now = following(a, c)
+        return now
+
+    lax.fori_loop(0, groups, step, (jnp.int32(0), jnp.int32(0)))
 
 
 def lane_totals(quantities):
@@ -240,85 +229,53 @@
     return jnp.maximum(peak, jnp.maximum(values[:, :128], values[:, 128:]))
 
 
-def inner_kernel(
-    span_ref, pos_ref, noise_ref, own_ref, out_ref, norm_ref, keep_high, keep_low, rows_ref, high_ref, low_ref, *stage
+def first_kernel(
+    span_ref, pos_ref, rows_ref, noise_ref, own_ref, halo_ref, out_ref, sums_ref, keep_high, keep_low, high_ref, low_ref, *stage
 ):
     rows = own_ref.shape[1] // SUP
     vals_ref, tiles = (high_ref, low_ref), (stage[:2], stage[2])
-    scale = scale_of(loop(0, rows, lambda a, peak: larger(peak, own_ref[:, lanes(a)]), zeros()))
-    spread_rows(pos_ref, rows_ref, rows - HALO)
-    clear(out_ref, 0, rows)
+    peak = loop(0, rows, lambda a, peak: larger(peak, own_ref[:, lanes(a)]), zeros())
+    scale = scale_of(loop(0, HALO, lambda a, peak: larger(peak, halo_ref[:, lanes(a)]), peak))
+    clear(out_ref, 0, rows + HALO)
 
     def begin(a, norm):
         values = own_ref[:, lanes(a)]
         hold(vals_ref, a, scale * values)
         return norm + fold(values * values)
 
-    norm_ref[...] = loop(0, rows, begin, zeros())
-    sweep(span_ref, pos_ref, rows_ref, vals_ref, out_ref, 0, rows - HALO, (keep_high, keep_low), tiles)
+    def begin_halo(a, _):
+        hold(vals_ref, rows + a, scale * halo_ref[:, lanes(a)])
+        return 0
+
+    norm = loop(0, rows, begin, zeros())
+    loop(0, HALO, begin_halo, 0)
+    sweep(span_ref, pos_ref, rows_ref, vals_ref, out_ref, rows, (keep_high, keep_low), tiles)
     inverse = 1.0 / (KERNEL * scale)
 
-    def finish(a, _):
+    def finish(a, curve):
         at = lanes(a)
-        out_ref[:, at] = out_ref[:, at] * inverse + noise_ref[:, at] * own_ref[:, at]
-        return 0
-
-    loop(0, rows, finish, 0)
-
-
-def outer_kernel(
-    span_ref, pos_ref, own_ref, halo_ref, norm_ref, begun_ref, out_ref, sums_ref, keep_high, keep_low,
-    rows_ref, high_ref, low_ref, *stage
-):
-    rows = own_ref.shape[1] // SUP
-    base = rows - HALO
-    vals_ref, tiles = (high_ref, low_ref), (stage[:2], stage[2])
-
-    def peaks(a, peak):
-        return larger(larger(peak, own_ref[:, lanes(base + a)]), halo_ref[:, lanes(a)])
-
-    scale = scale_of(loop(0, HALO, peaks, zeros()))
-    spread_rows(pos_ref, rows_ref, HALO)
-    clear(out_ref, base, 2 * HALO)
-
-    def begin(a, _):
-        hold(vals_ref, a, scale * own_ref[:, lanes(base + a)])
-        hold(vals_ref, HALO + a, scale * halo_ref[:, lanes(a)])
-        return 0
-
-    loop(0, HALO, begin, 0)
-    sweep(span_ref, pos_ref, rows_ref, vals_ref, out_ref, base, HALO, (keep_high, keep_low), tiles)
-    inverse = 1.0 / (KERNEL * scale)
-
-    def rest(a, curve):
-        at = lanes(a)
-        image = begun_ref[:, at]
+        image = out_ref[:, at] * inverse + noise_ref[:, at] * own_ref[:, at]
         out_ref[:, at] = image
         return curve + fold(own_ref[:, at] * image)
 
-    def edge(a, curve):
-        at = lanes(base + a)
-        image = begun_ref[:, at] + out_ref[:, at] * inverse
-        out_ref[:, at] = image
-        curve = curve + fold(own_ref[:, at] * image)
+    def finish_halo(a, curve):
         at = lanes(rows + a)
         image = out_ref[:, at] * inverse
         out_ref[:, at] = image
         return curve + fold(halo_ref[:, lanes(a)] * image)
 
-    curve = loop(0, HALO, edge, loop(0, base, rest, zeros()))
-    sums_ref[...] = lane_totals([norm_ref[...], curve])
+    curve = loop(0, HALO, finish_halo, loop(0, rows, finish, zeros()))
+    sums_ref[...] = lane_totals([norm, curve])
 
 
 def second_kernel(
-    span_ref, outer_ref, noise_ref, own_ref, halo_ref, image_ref, left_ref, right_ref, first_ref, *refs
+    span_ref, noise_ref, own_ref, halo_ref, image_ref, left_ref, right_ref, first_ref, keep_high, keep_low,
+    out_ref, sums_ref, high_ref, low_ref, resid_ref, *stage
 ):
-    keeps, (out_ref, sums_ref, high_ref, low_ref, resid_ref), stage = refs[:4], refs[4:9], refs[9:]
-    vals_ref, tiles = (high_ref, low_ref), (stage[:2], stage[2])
+    vals_ref, tiles, keep = (high_ref, low_ref), (stage[:2], stage[2]), (keep_high, keep_low)
     rows = own_ref.shape[1] // SUP
-    spans, bases, counts = (span_ref, outer_ref), (0, rows - HALO), (rows - HALO, HALO)
     for g in range(AHEAD):
-        fetch(keeps, [group_count(span[n]) for span, n in zip(spans, counts)], tiles, jnp.int32(g), True)
+        fetch(keep, group_count(span_ref[0, rows]), tiles, g, True)
     norm_before, curve_before = frame_columns(first_ref[0:1])[:2]
     alpha = wide(norm_before / curve_before)
 
@@ -352,7 +309,7 @@
 
     loop(0, rows + HALO, ready, 0)
     clear(out_ref, 0, rows + HALO)
-    sweep_again(spans, bases, counts, vals_ref, out_ref, keeps, tiles)
+    sweep_again(span_ref, rows, vals_ref, out_ref, keep, tiles)
     inverse = 1.0 / (KERNEL * scale)
 
     def finish(a, curve):
@@ -392,34 +349,25 @@
     return jax.ShapeDtypeStruct(shape, jnp.bfloat16), jax.ShapeDtypeStruct(shape, EIGHT)
 
 
-def first_pass(span, outer_span, positions, edge_pos, noise, right_side, halo):
-    rows = positions.shape[1] // SUP
-    inner = rows - HALO
-    field = f32((FRAMES, (rows + HALO + 1) * SUP))
-    spread = pltpu.VMEM((inner, 3, SUP, 128), jnp.float32)
-    image, norm, *keep = local_call(
-        inner_kernel, (span, padded(positions), noise, right_side), (field, f32((FRAMES, 128))) + kept(inner),
-        [spread] + vals_scratch(rows) + stage_scratch(2), 1, any_outs=2,
+def first_pass(span, pos, spread, noise, right_side, halo):
+    rows = right_side.shape[1] // SUP
+    return local_call(
+        first_kernel, (span, pos, spread, noise, right_side, halo),
+        (f32((FRAMES, (rows + HALO + 1) * SUP)), f32((8, 128))) + kept(rows),
+        vals_scratch(rows + HALO) + stage_scratch(2), 1, any_outs=2,
     )
-    outer_pos = padded(jnp.concatenate([positions[:, inner * SUP :], edge_pos], axis=1))
-    spread = pltpu.VMEM((HALO, 3, SUP, 128), jnp.float32)
-    image, sums, *keep_outer = local_call(
-        outer_kernel, (outer_span, outer_pos, right_side, halo, norm, image), (field, f32((8, 128))) + kept(HALO),
-        [spread] + vals_scratch(2 * HALO) + stage_scratch(2), 1, any_outs=2,
-    )
-    return image, sums, keep + keep_outer
-
-
-def second_pass(span, outer_span, noise, right_side, halo, image, left, right, first, keeps):
+
+
+def second_pass(span, noise, right_side, halo, image, left, right, first, keep):
     extent = right_side.shape[1] // SUP + HALO
     return local_call(
-        second_kernel, (span, outer_span, noise, right_side, halo, image, left, right, first, *keeps),
+        second_kernel, (span, noise, right_side, halo, image, left, right, first, *keep),
         (f32((FRAMES, (extent + 1) * SUP)), f32((8, 128))),
-        vals_scratch(extent) + [pltpu.VMEM((FRAMES, extent * SUP), jnp.float32)] + stage_scratch(AHEAD + 1), 2, anys=4,
+        vals_scratch(extent) + [pltpu.VMEM((FRAMES, extent * SUP), jnp.float32)] + stage_scratch(AHEAD + 1), 1, anys=2, mib=50,
     )
 
 
-def local_call(kernel, operands, out_shape, scratch, smalls, anys=0, any_outs=0):
+def local_call(kernel, operands, out_shape, scratch, smalls, anys=0, any_outs=0, mib=28):
     plain = len(operands) - smalls - anys
     return pl.pallas_call(
         kernel,
@@ -427,7 +375,7 @@
         in_specs=[SMEM] * smalls + [VMEM] * plain + [ANY] * anys,
         out_specs=(VMEM,) * (len(out_shape) - any_outs) + (ANY,) * any_outs,
         scratch_shapes=scratch,
-        compiler_params=pltpu.CompilerParams(vmem_limit_bytes=44 * 2**20),
+        compiler_params=pltpu.CompilerParams(vmem_limit_bytes=mib * 2**20),
     )(*operands)
 
 
@@ -538,39 +486,88 @@
         copy.wait()
 
 
-def spans(positions, rows, limit):
-    extent = positions.shape[1] // SUP
-    boxed = positions.reshape(3, extent, SUP)
-    low, high = jnp.min(boxed, axis=2), jnp.max(boxed, axis=2)
-    index = jnp.arange(rows, dtype=jnp.int32)
-    span = jnp.zeros((rows,), jnp.int32)
+def spans(boxes, rows, limit):
+    low, high = boxes
+    lane = lax.broadcasted_iota(jnp.int32, (1, 128), 1)
+    span = jnp.zeros((1, 128), jnp.int32)
     for k in range(1, HALO + 1):
-        ahead = slice(k, k + rows)
-        gap = jnp.maximum(jnp.maximum(low[:, ahead] - high[:, :rows], low[:, :rows] - high[:, ahead]), 0.0)
-        near = (jnp.sum(gap * gap, axis=0) < 1.0) & (index + k < limit)
+        low_k, high_k = pltpu.roll(low, 128 - k, 1), pltpu.roll(high, 128 - k, 1)
+        gap = jnp.maximum(jnp.maximum(low_k - high, low - high_k), 0.0)
+        near = (jnp.sum(gap * gap, axis=0, keepdims=True) < UNIT * UNIT) & (lane + k < limit)
         span = jnp.where(near, k, span)
-    return jnp.concatenate([span, jnp.sum(span + 1, keepdims=True)])
-
-
-def padded(positions):
-    return UNIT * jnp.concatenate([positions, jnp.zeros((5, positions.shape[1]), jnp.float32)], axis=0)
+    pairs = jnp.sum(jnp.where(lane < rows, span + 1, 0), axis=1, keepdims=True)
+    return jnp.broadcast_to(jnp.where(lane == rows, pairs, span), (8, 128))
+
+
+def start_kernel(positions_ref, own_ref, pos_ref, halo_ref, span_ref, rows_ref, edge_pos, edge, sems):
+    rows = own_ref.shape[1] // SUP
+    width = HALO * SUP
+    size = lax.axis_size("pts")
+    me = lax.axis_index("pts")
+    right, left = lax.rem(me + 1, size), lax.rem(me + size - 1, size)
+    barrier = pltpu.get_barrier_semaphore()
+    for peer in (left, right):
+        pl.semaphore_signal(barrier, inc=1, device_id=(peer,), device_id_type=MESH)
+    blank = jnp.zeros((5, width), jnp.float32)
+    for part in range(rows // HALO):
+        at = slice(part * width, (part + 1) * width)
+        pos_ref[:, at] = jnp.concatenate([UNIT * positions_ref[:, at], blank], axis=0)
+    pl.semaphore_wait(barrier, 2)
+    copies = []
+    for index, (src, dst) in enumerate(((pos_ref, edge_pos), (own_ref, edge))):
+        copies.append(
+            pltpu.make_async_remote_copy(
+                src_ref=src.at[:, pl.ds(0, width)], dst_ref=dst, send_sem=sems.at[0, index], recv_sem=sems.at[1, index],
+                device_id=(left,), device_id_type=MESH,
+            )
+        )
+        copies[-1].start()
+    lane = lax.broadcasted_iota(jnp.int32, (8, 128), 1)
+
+    def box(a, boxes):
+        points = pos_ref[:, lanes(a)]
+        low = jnp.min(jnp.minimum(points[:, :128], points[:, 128:]), axis=1, keepdims=True)
+        high = jnp.max(jnp.maximum(points[:, :128], points[:, 128:]), axis=1, keepdims=True)
+        return jnp.where(lane == a, low, boxes[0]), jnp.where(lane == a, high, boxes[1])
+
+    none = jnp.zeros((8, 128), jnp.float32)
+    boxes = loop(0, rows, box, (none, none))
+    spread_rows(pos_ref, rows_ref, rows)
+    for copy in copies:
+        copy.wait()
+    pos_ref[:, rows * SUP :] = edge_pos[...]
+    halo_ref[...] = edge[...]
+    boxes = loop(rows, rows + HALO, box, boxes)
+    span_ref[...] = spans(boxes, rows, jnp.where(me == size - 1, rows, rows + HALO))
+
+
+def start(positions, right_side, collective_id):
+    rows = right_side.shape[1] // SUP
+    width = HALO * SUP
+    return pl.pallas_call(
+        start_kernel,
+        out_shape=(
+            f32((8, (rows + HALO) * SUP)), f32((FRAMES, width)), jax.ShapeDtypeStruct((8, 128), jnp.int32),
+            f32((rows, 3, SUP, 128)),
+        ),
+        in_specs=[VMEM, VMEM],
+        out_specs=(VMEM,) * 4,
+        scratch_shapes=[
+            pltpu.VMEM((8, width), jnp.float32), pltpu.VMEM((FRAMES, width), jnp.float32), pltpu.SemaphoreType.DMA((2, 2)),
+        ],
+        compiler_params=pltpu.CompilerParams(
+            collective_id=collective_id, has_side_effects=True, vmem_limit_bytes=28 * 2**20
+        ),
+    )(positions, right_side)
 
 
 def body(positions, noise, right_side, pairs, counts):
     rows = positions.shape[1] // SUP
-    inner = rows - HALO
-    width = HALO * SUP
-    size = lax.axis_size("pts")
-    back = [(i + 1, i) for i in range(size - 1)]
-    edge_pos = lax.ppermute(positions[:, :width], "pts", back)
-    halo = lax.ppermute(right_side[:, :width], "pts", back)
     noise = noise.reshape(1, -1)
-    span = spans(positions, inner, rows)
-    outer_pos = jnp.concatenate([positions[:, inner * SUP :], edge_pos], axis=1)
-    outer_span = spans(outer_pos, HALO, jnp.where(lax.axis_index("pts") == size - 1, HALO, 2 * HALO))
-    image, sums, keeps = first_pass(span, outer_span, positions, edge_pos, noise, right_side, halo)
+    pos, halo, span, spread = start(positions, right_side, 2)
+    image, sums, *keep = first_pass(span, pos, spread, noise, right_side, halo)
     left, right, first = exchange(image, sums, rows, True, 0)
-    part, sums = second_pass(span, outer_span, noise, right_side, halo, image, left, right, first, keeps)
+    part, sums = second_pass(span, noise, right_side, halo, image, left, right, first, keep)
     left2, second = exchange(part, sums, rows, False, 1)
     parts = rows // HALO
     return local_call(

time: 113 us -> 93.4 us (0.83)
  Pallas kernels: 96.4 us -> 87.3 us
  starting transfers between devices: 5.25 us -> 0 us
  other arithmetic: 5.2 us -> 0 us
    pallas_call x4 -> x3, Pallas kernels: 53 us -> 43.5 us  [local_call(): pl.pallas_call(kernel, out_shape=out_shape, in_specs=[SMEM] * smalls + [V...]
    pallas_call x0 -> x1, Pallas kernels: none -> 7.87 us  [start(): pl.pallas_call(start_kernel, out_shape=(f32((8, (rows + HALO) * SUP)), f3...]
    pallas_call x2, Pallas kernels: 43.4 us -> 35.8 us  [exchange(): pl.pallas_call(functools.partial(exchange_kernel, both_ways, rows), out_s...]
    ppermute x2 -> x0, starting transfers between devices: 5.25 us -> none  [the longest x1 3.33 us: body(): edge_pos = lax.ppermute(positions[:, :width], 'pts', back)]
    unnamed x8 -> x16, local copies, waits for them, and re-layouts: 3.21 us -> 5.17 us
    slice x2 -> x0, local copies, waits for them, and re-layouts: 1.85 us -> none  [the longest x1 0.97 us: body(): halo = lax.ppermute(right_side[:, :width], 'pts', back)]
    reduce_sum x6 -> x0, other arithmetic: 1.69 us -> none  [the longest x2 1.29 us: spans(): return jnp.concatenate([span, jnp.sum(span + 1, keepdims=True)])]
    concatenate x3 -> x0, other arithmetic: 1.45 us -> none  [the longest x2 1.44 us: spans(): return jnp.concatenate([span, jnp.sum(span + 1, keepdims=True)])]
  transfers between devices with their start and end apart: 2 -> 0, of which waited for: 0 -> 0; matrix products, arithmetic and copies ran while one was open for 5% -> 0% of each run, Pallas kernels for 23% -> 0%
where the time goes in v4:
time: 93.4 us; the launch traced here: 93.1 us
  Pallas kernels  87.3 us (93%)
  local copies, waits for them, and re-layouts  5.17 us (6%)
    pallas_call x3, Pallas kernels, local_call(): pl.pallas_call(kernel, out_shape=out_shape, in_specs=[SMEM] * smalls + [V...  43.5 us
    pallas_call x2, Pallas kernels, exchange(): pl.pallas_call(functools.partial(exchange_kernel, both_ways, rows), out_s...  35.8 us
    pallas_call x1, Pallas kernels, start(): pl.pallas_call(start_kernel, out_shape=(f32((8, (rows + HALO) * SUP)), f3...  7.87 us
    unnamed x16, local copies, waits for them, and re-layouts  5.17 us

profile of v4, /device:TPU:1, one launch (start us, length us, event | category | flops | bytes accessed | tf_op | source)
XLA Modules:
  0.0 93.1 jit_solution(243100002937673830)
XLA Ops:
  0.6 0.0 copy-start
  0.6 1.2 %copy-done = f32[32,8192]{1,0:T(8,128)S(1)} copy-done((f32[32,8192]{1,0:T(8,128)S(1)}, f32[32,8192]{1,0:T(8,128)}, u32[]{:S(2)}) %copy-start) | copy-done | bytes 1048600
  1.9 0.0 copy-start.7
  1.9 0.9 copy-done.7
  2.8 0.0 copy-start.2
  2.8 0.0 copy-start.6
  2.8 7.9 %shard_map.50 = (f32[8,10240]{1,0:T(8,128)S(1)}, f32[32,2048]{1,0:T(8,128)S(1)}, s32[8,128]{1,0:T(8,128)S(1)}, f32[32,3,256,128]{3,2,1,0:T(8,128)S(1)}) custom-call(f32[3,8192]{1,0:T(4,128)S(1)} %copy-done.7, f32[32,8192]{1,0:T(8,128)S(1)} %copy-done), custom_call_target="tpu_custom_call" | custom-call | tf_op jit(solution)/shard_map/pallas_call | solution.py:547
  10.6 0.0 copy-start.1
  10.7 1.2 %copy-done.1 = f32[32,8192]{1,0:T(8,128)S(1)} copy-done((f32[32,8192]{1,0:T(8,128)S(1)}, f32[32,8192]{1,0:T(8,128)}, u32[]{:S(2)}) %copy-start.1) | copy-done | bytes 1048600
  11.9 0.0 copy-start.5
  11.9 0.8 copy-done.5
  12.6 26.8 %shard_map.51 = (f32[32,10496]{1,0:T(8,128)S(1)}, f32[8,128]{1,0:T(8,128)S(1)}, bf16[36,8,256,256]{3,2,1,0:T(8,128)(2,1)}, f8e4m3fn[36,8,256,256]{3,2,1,0:T(32,128)(4,1)}) custom-call(s32[8,128]{1,0:T(8,128)S(1)} %get-tuple-element.17.span_ref, f32[8,10240]{1,0:T(8,128)S(1)} %get-tuple-element.18.pos_ref, ...), custom_call_target="tpu_custom_call" | custom-call | tf_op jit(solution)/shard_map/pallas_call | solution.py:372
  39.4 21.3 %shard_map.52 = (f32[32,2048]{1,0:T(8,128)S(1)}, f32[32,2048]{1,0:T(8,128)S(1)}, f32[8,128]{1,0:T(8,128)S(1)}) custom-call(f32[32,10496]{1,0:T(8,128)S(1)} %get-tuple-element.21.part_ref.image_ref, f32[8,128]{1,0:T(8,128)S(1)} %get-tuple-element.22.sums_ref), custom_call_target="tpu_custom_call" | custom-call | tf_op jit(solution)/shard_map/pallas_call | solution.py:436
  60.8 0.0 copy-start.3
  60.8 1.1 %copy-done.3 = f32[32,10496]{1,0:T(8,128)} copy-done((f32[32,10496]{1,0:T(8,128)}, f32[32,10496]{1,0:T(8,128)S(1)}, u32[]{:S(2)}) %copy-start.3) | copy-done | bytes 1343512
  61.9 0.0 copy-done.2
  61.9 0.0 copy-done.6
  61.9 0.0 copy-start.4
  61.9 15.1 %shard_map.53 = (f32[32,10496]{1,0:T(8,128)S(1)}, f32[8,128]{1,0:T(8,128)S(1)}) custom-call(s32[8,128]{1,0:T(8,128)S(1)} %get-tuple-element.17.span_ref, f32[1,8192]{1,0:T(1,128)S(1)} %bitcast.2, f32[32,8192]{1,0:T(8,128)S(1)} %copy-done.2, f32[32,2048]{1,0:T(8,128)S(1)} %get-tuple-element.20.halo_ref, f32[32,10496]{1,0:T(8,128)} %copy-done.3, ...), custom_call_target="tpu_custom_call" | custom-call | tf_op jit(solution)/shard_map/pallas_call | solution.py:372
  77.0 14.5 %shard_map.54 = (f32[32,2048]{1,0:T(8,128)S(1)}, f32[8,128]{1,0:T(8,128)S(1)}) custom-call(f32[32,10496]{1,0:T(8,128)S(1)} %get-tuple-element.28.part_ref, f32[8,128]{1,0:T(8,128)S(1)} %get-tuple-element.29.sums_ref), custom_call_target="tpu_custom_call" | custom-call | tf_op jit(solution)/shard_map/pallas_call | solution.py:436
  91.5 0.0 copy-done.4
  91.5 1.6 %shard_map.55 = (f32[32,8192]{1,0:T(8,128)}, f32[32,8192]{1,0:T(8,128)}) custom-call(f32[32,8192]{1,0:T(8,128)S(1)} %copy-done.2, f32[32,10496]{1,0:T(8,128)S(1)} %copy-done.4, f32[32,2048]{1,0:T(8,128)S(1)} %get-tuple-element.23.left_ref, f32[32,10496]{1,0:T(8,128)S(1)} %get-tuple-element.28.part_ref, f32[32,2048]{1,0:T(8,128)S(1)} %get-tuple-element.30.left2_ref, ...), custom_call_target="tpu_custom_call" | custom-call | tf_op jit(solution)/shard_map/pallas_call | solution.py:372
Async XLA Ops:
  0.6 1.2 %copy-start = (f32[32,8192]{1,0:T(8,128)S(1)}, f32[32,8192]{1,0:T(8,128)}, u32[]{:S(2)}) copy-start(f32[32,8192]{1,0:T(8,128)} %own_ref.7) | copy-start | bytes 3145732
  1.9 0.9 copy-start.7
  2.8 59.1 %copy-start.2 = (f32[32,8192]{1,0:T(8,128)S(1)}, f32[32,8192]{1,0:T(8,128)}, u32[]{:S(2)}) copy-start(f32[32,8192]{1,0:T(8,128)} %own_ref.7) | copy-start | bytes 3145732
  2.8 59.1 %copy-start.6 = (f32[8192]{0:T(1024)S(1)}, f32[8192]{0:T(1024)}, u32[]{:S(2)}) copy-start(f32[8192]{0:T(1024)} %param.6) | copy-start | bytes 98308
  10.6 1.2 %copy-start.1 = (f32[32,8192]{1,0:T(8,128)S(1)}, f32[32,8192]{1,0:T(8,128)}, u32[]{:S(2)}) copy-start(f32[32,8192]{1,0:T(8,128)} %own_ref.7) | copy-start | bytes 3145732
  11.9 0.8 copy-start.5
  60.8 1.1 %copy-start.3 = (f32[32,10496]{1,0:T(8,128)}, f32[32,10496]{1,0:T(8,128)S(1)}, u32[]{:S(2)}) copy-start(f32[32,10496]{1,0:T(8,128)S(1)} %get-tuple-element.21.part_ref.image_ref) | copy-start | bytes 4030468
  61.9 29.6 %copy-start.4 = (f32[32,10496]{1,0:T(8,128)S(1)}, f32[32,10496]{1,0:T(8,128)}, u32[]{:S(2)}) copy-start(f32[32,10496]{1,0:T(8,128)} %copy-done.3) | copy-start | bytes 4030468

commit v5 on v4

--- a/solution.py
+++ b/solution.py
@@ -1,5 +1,3 @@
-import functools
-
 import jax
 import jax.numpy as jnp
 from jax import lax
@@ -154,6 +152,10 @@
         return now
 
     lax.fori_loop(0, groups, step, (jnp.int32(0), jnp.int32(0)))
+
+
+def settle(span_ref, rows, keep, tiles):
+    groups = group_count(span_ref[0, rows])
     for k in (2, 1):
         @pl.when(groups >= k)
         def _():
@@ -266,11 +268,12 @@
 
     curve = loop(0, HALO, finish_halo, loop(0, rows, finish, zeros()))
     sums_ref[...] = lane_totals([norm, curve])
+    settle(span_ref, rows, (keep_high, keep_low), tiles)
 
 
 def second_kernel(
     span_ref, noise_ref, own_ref, halo_ref, image_ref, left_ref, right_ref, first_ref, keep_high, keep_low,
-    out_ref, sums_ref, high_ref, low_ref, resid_ref, *stage
+    out_ref, resid_ref, inverse_ref, sums_ref, high_ref, low_ref, *stage
 ):
     vals_ref, tiles, keep = (high_ref, low_ref), (stage[:2], stage[2]), (keep_high, keep_low)
     rows = own_ref.shape[1] // SUP
@@ -310,22 +313,8 @@
     loop(0, rows + HALO, ready, 0)
     clear(out_ref, 0, rows + HALO)
     sweep_again(span_ref, rows, vals_ref, out_ref, keep, tiles)
-    inverse = 1.0 / (KERNEL * scale)
-
-    def finish(a, curve):
-        at = lanes(a)
-        image = out_ref[:, at] * inverse + noise_ref[:, at] * resid_ref[:, at]
-        out_ref[:, at] = image
-        return curve + fold(resid_ref[:, at] * image)
-
-    def finish_halo(a, curve):
-        at = lanes(rows + a)
-        image = out_ref[:, at] * inverse
-        out_ref[:, at] = image
-        return curve + fold(resid_ref[:, at] * image)
-
-    curve = loop(0, HALO, finish_halo, loop(0, rows, finish, zeros()))
-    sums_ref[...] = lane_totals([norm, curve, cross])
+    inverse_ref[...] = 1.0 / (KERNEL * scale)
+    sums_ref[0], sums_ref[1] = norm, cross
 
 
 def vals_scratch(count):
@@ -362,8 +351,8 @@
     extent = right_side.shape[1] // SUP + HALO
     return local_call(
         second_kernel, (span, noise, right_side, halo, image, left, right, first, *keep),
-        (f32((FRAMES, (extent + 1) * SUP)), f32((8, 128))),
-        vals_scratch(extent) + [pltpu.VMEM((FRAMES, extent * SUP), jnp.float32)] + stage_scratch(AHEAD + 1), 1, anys=2, mib=50,
+        (f32((FRAMES, (extent + 1) * SUP)), f32((FRAMES, extent * SUP)), f32((FRAMES, SUP)), f32((2, FRAMES, 128))),
+        vals_scratch(extent) + stage_scratch(AHEAD + 1), 1, anys=2, mib=44,
     )
 
 
@@ -379,78 +368,129 @@
     )(*operands)
 
 
-def exchange_kernel(both_ways, rows, part_ref, sums_ref, *refs):
-    if both_ways:
-        left_out, right_out, total_out, left_buf, right_buf, near, far, mine, edge_sems, near_sems, far_sems = refs
-    else:
-        left_out, total_out, left_buf, near, far, mine, edge_sems, near_sems, far_sems = refs
-    size = lax.axis_size("pts")
+def arrive(peers):
+    barrier = pltpu.get_barrier_semaphore()
+    for peer in peers:
+        pl.semaphore_signal(barrier, inc=1, device_id=(peer,), device_id_type=MESH)
+    return lambda: pl.semaphore_wait(barrier, len(peers))
+
+
+def send(src, dst, sems, index, peer):
+    copy = pltpu.make_async_remote_copy(
+        src_ref=src, dst_ref=dst, send_sem=sems.at[0, index], recv_sem=sems.at[1, index],
+        device_id=(peer,), device_id_type=MESH,
+    )
+    copy.start()
+    return copy
+
+
+def neighbours():
+    size, me = lax.axis_size("pts"), lax.axis_index("pts")
+    return lax.rem(me + size - 1, size), lax.rem(me + 1, size)
+
+
+def partners():
     me = lax.axis_index("pts")
-    groups = size // GROUP
+    groups = lax.axis_size("pts") // GROUP
     spot, group = lax.rem(me, GROUP), me // GROUP
-    right, left = lax.rem(me + 1, size), lax.rem(me + size - 1, size)
     near_peers = [group * GROUP + lax.rem(spot + k, GROUP) for k in range(1, GROUP)]
     far_peers = [lax.rem(group + k, groups) * GROUP + spot for k in range(1, groups)]
-    barrier = pltpu.get_barrier_semaphore()
-    peers = near_peers + far_peers + [left, right]
-    for peer in peers:
-        pl.semaphore_signal(barrier, inc=1, device_id=(peer,), device_id_type=MESH)
-    pl.semaphore_wait(barrier, len(peers))
-
-    def send(src, dst, sems, index, peer):
-        copy = pltpu.make_async_remote_copy(
-            src_ref=src, dst_ref=dst, send_sem=sems.at[0, index], recv_sem=sems.at[1, index],
-            device_id=(peer,), device_id_type=MESH,
-        )
-        copy.start()
-        return copy
-
-    near_copies = [send(sums_ref, near.at[k], near_sems, k, near_peers[k - 1]) for k in range(1, GROUP)]
-    width = HALO * SUP
-    edges = [send(part_ref.at[:, pl.ds(rows * SUP, width)], left_buf, edge_sems, 0, right)]
-    if both_ways:
-        edges.append(send(part_ref.at[:, pl.ds(0, width)], right_buf, edge_sems, 1, left))
-    for copy in near_copies:
-        copy.wait()
-    total = sums_ref[...]
-    for k in range(1, GROUP):
-        total = total + near[k]
-    mine[...] = total
-    far_copies = [send(mine, far.at[k], far_sems, k, far_peers[k - 1]) for k in range(1, groups)]
-    for copy in far_copies:
-        copy.wait()
-    for k in range(1, groups):
-        total = total + far[k]
-    total_out[...] = total
-    for copy in edges:
+    return near_peers, far_peers
+
+
+def sum_over_devices(total, mine, slots, sems, edges):
+    offset = 0
+    for stage, peers in enumerate(partners()):
+        mine[stage, 0:1] = total
+        copies = [
+            send(mine.at[stage, pl.ds(0, 1)], slots.at[offset + k, pl.ds(0, 1)], sems, offset + k, peer)
+            for k, peer in enumerate(peers)
+        ]
+        if stage == 0:
+            edges()
+        for copy in copies:
+            copy.wait()
+        for k in range(len(peers)):
+            total = total + slots[offset + k, 0:1]
+        offset += len(peers)
+    return total
+
+
+def exchange_kernel(
+    part_ref, sums_ref, left_out, right_out, total_out, left_buf, right_buf, slots, mine, edge_sems, sems
+):
+    near_peers, far_peers = partners()
+    left, right = neighbours()
+    arrive(near_peers + far_peers + [left, right])()
+    width = left_buf.shape[1]
+    first = part_ref.shape[1] - width - SUP
+    copies = []
+
+    def edges():
+        copies.append(send(part_ref.at[:, pl.ds(first, width)], left_buf, edge_sems, 0, right))
+        copies.append(send(part_ref.at[:, pl.ds(0, width)], right_buf, edge_sems, 1, left))
+
+    total = sum_over_devices(sums_ref[0:1], mine, slots, sems, edges)
+    total_out[...] = jnp.broadcast_to(total, (8, 128))
+    for copy in copies:
         copy.wait()
     left_out[...] = left_buf[...]
-    if both_ways:
-        right_out[...] = right_buf[...]
-
-
-def exchange(part, sums, rows, both_ways, collective_id):
-    edge = f32((FRAMES, HALO * SUP))
-    edges = 2 if both_ways else 1
-    groups = lax.axis_size("pts") // GROUP
+    right_out[...] = right_buf[...]
+
+
+def finish_kernel(
+    part_ref, resid_ref, inverse_ref, norms_ref, noise_ref, image_out, left_out, total_out,
+    edge, left_buf, slots, mine, edge_sems, sems
+):
+    near_peers, far_peers = partners()
+    left, right = neighbours()
+    arrived = arrive(near_peers + far_peers + [left, right])
+    rows = image_out.shape[1] // SUP
+    inverse = inverse_ref[...]
+
+    def finish(a, curve):
+        at = lanes(a)
+        image = part_ref[:, at] * inverse + noise_ref[:, at] * resid_ref[:, at]
+        image_out[:, at] = image
+        return curve + fold(resid_ref[:, at] * image)
+
+    def finish_halo(a, curve):
+        at = lanes(rows + a)
+        image = part_ref[:, at] * inverse
+        edge[:, lanes(a)] = image
+        return curve + fold(resid_ref[:, at] * image)
+
+    curve = loop(0, HALO, finish_halo, loop(0, rows, finish, zeros()))
+    total = lane_totals([norms_ref[0], curve, norms_ref[1]])[0:1]
+    arrived()
+    copies = []
+    total = sum_over_devices(
+        total, mine, slots, sems, lambda: copies.append(send(edge, left_buf, edge_sems, 0, right))
+    )
+    total_out[...] = jnp.broadcast_to(total, (8, 128))
+    for copy in copies:
+        copy.wait()
+    left_out[...] = left_buf[...]
+
+
+def remote_call(kernel, operands, out_shape, scratch, collective_id):
+    partners_count = GROUP - 1 + lax.axis_size("pts") // GROUP - 1
     return pl.pallas_call(
-        functools.partial(exchange_kernel, both_ways, rows),
-        out_shape=(edge,) * edges + (f32((8, 128)),),
-        in_specs=[VMEM, VMEM],
-        out_specs=(VMEM,) * (edges + 1),
-        scratch_shapes=[pltpu.VMEM(edge.shape, jnp.float32)] * edges
+        kernel,
+        out_shape=out_shape,
+        in_specs=[VMEM] * len(operands),
+        out_specs=(VMEM,) * len(out_shape),
+        scratch_shapes=scratch
         + [
-            pltpu.VMEM((GROUP, 8, 128), jnp.float32),
-            pltpu.VMEM((groups, 8, 128), jnp.float32),
-            pltpu.VMEM((8, 128), jnp.float32),
-            pltpu.SemaphoreType.DMA((2, edges)),
-            pltpu.SemaphoreType.DMA((2, GROUP)),
-            pltpu.SemaphoreType.DMA((2, groups)),
+            pltpu.VMEM((partners_count, 8, 128), jnp.float32),
+            pltpu.VMEM((2, 8, 128), jnp.float32),
+            pltpu.SemaphoreType.DMA((2, 2)),
+            pltpu.SemaphoreType.DMA((2, partners_count)),
         ],
         compiler_params=pltpu.CompilerParams(
             collective_id=collective_id, has_side_effects=True, vmem_limit_bytes=16 * 2**20
         ),
-    )(part, sums)
+    )(*operands)
 
 
 def last_kernel(
@@ -499,8 +539,10 @@
     return jnp.broadcast_to(jnp.where(lane == rows, pairs, span), (8, 128))
 
 
-def start_kernel(positions_ref, own_ref, pos_ref, halo_ref, span_ref, rows_ref, edge_pos, edge, sems):
-    rows = own_ref.shape[1] // SUP
+def start_kernel(
+    positions_any, own_any, pos_ref, halo_ref, span_ref, rows_ref, own_out, positions_ref, edge_pos, edge, local_sems, sems
+):
+    rows = own_any.shape[1] // SUP
     width = HALO * SUP
     size = lax.axis_size("pts")
     me = lax.axis_index("pts")
@@ -508,13 +550,13 @@
     barrier = pltpu.get_barrier_semaphore()
     for peer in (left, right):
         pl.semaphore_signal(barrier, inc=1, device_id=(peer,), device_id_type=MESH)
-    blank = jnp.zeros((5, width), jnp.float32)
-    for part in range(rows // HALO):
-        at = slice(part * width, (part + 1) * width)
-        pos_ref[:, at] = jnp.concatenate([UNIT * positions_ref[:, at], blank], axis=0)
+    bring = pltpu.make_async_copy(positions_any, positions_ref, local_sems.at[0])
+    bring.start()
+    pass_on = pltpu.make_async_copy(own_any, own_out, local_sems.at[1])
+    pass_on.start()
     pl.semaphore_wait(barrier, 2)
     copies = []
-    for index, (src, dst) in enumerate(((pos_ref, edge_pos), (own_ref, edge))):
+    for index, (src, dst) in enumerate(((positions_any, edge_pos), (own_any, edge))):
         copies.append(
             pltpu.make_async_remote_copy(
                 src_ref=src.at[:, pl.ds(0, width)], dst_ref=dst, send_sem=sems.at[0, index], recv_sem=sems.at[1, index],
@@ -522,6 +564,11 @@
             )
         )
         copies[-1].start()
+    bring.wait()
+    blank = jnp.zeros((5, width), jnp.float32)
+    for part in range(rows // HALO):
+        at = slice(part * width, (part + 1) * width)
+        pos_ref[:, at] = jnp.concatenate([UNIT * positions_ref[:, at], blank], axis=0)
     lane = lax.broadcasted_iota(jnp.int32, (8, 128), 1)
 
     def box(a, boxes):
@@ -535,7 +582,8 @@
     spread_rows(pos_ref, rows_ref, rows)
     for copy in copies:
         copy.wait()
-    pos_ref[:, rows * SUP :] = edge_pos[...]
+    pass_on.wait()
+    pos_ref[:, rows * SUP :] = jnp.concatenate([UNIT * edge_pos[...], blank], axis=0)
     halo_ref[...] = edge[...]
     boxes = loop(rows, rows + HALO, box, boxes)
     span_ref[...] = spans(boxes, rows, jnp.where(me == size - 1, rows, rows + HALO))
@@ -548,12 +596,16 @@
         start_kernel,
         out_shape=(
             f32((8, (rows + HALO) * SUP)), f32((FRAMES, width)), jax.ShapeDtypeStruct((8, 128), jnp.int32),
-            f32((rows, 3, SUP, 128)),
+            f32((rows, 3, SUP, 128)), f32(right_side.shape),
         ),
-        in_specs=[VMEM, VMEM],
-        out_specs=(VMEM,) * 4,
+        in_specs=[ANY, VMEM],
+        out_specs=(VMEM,) * 5,
         scratch_shapes=[
-            pltpu.VMEM((8, width), jnp.float32), pltpu.VMEM((FRAMES, width), jnp.float32), pltpu.SemaphoreType.DMA((2, 2)),
+            pltpu.VMEM(positions.shape, jnp.float32),
+            pltpu.VMEM((3, width), jnp.float32),
+            pltpu.VMEM((FRAMES, width), jnp.float32),
+            pltpu.SemaphoreType.DMA((2,)),
+            pltpu.SemaphoreType.DMA((2, 2)),
         ],
         compiler_params=pltpu.CompilerParams(
             collective_id=collective_id, has_side_effects=True, vmem_limit_bytes=28 * 2**20
@@ -564,11 +616,15 @@
 def body(positions, noise, right_side, pairs, counts):
     rows = positions.shape[1] // SUP
     noise = noise.reshape(1, -1)
-    pos, halo, span, spread = start(positions, right_side, 2)
+    pos, halo, span, spread, right_side = start(positions, right_side, 2)
     image, sums, *keep = first_pass(span, pos, spread, noise, right_side, halo)
-    left, right, first = exchange(image, sums, rows, True, 0)
-    part, sums = second_pass(span, noise, right_side, halo, image, left, right, first, keep)
-    left2, second = exchange(part, sums, rows, False, 1)
+    edge = f32(halo.shape)
+    held = pltpu.VMEM(halo.shape, jnp.float32)
+    left, right, first = remote_call(exchange_kernel, (image, sums), (edge, edge, f32((8, 128))), [held] * 2, 0)
+    part, resid, inverse, norms = second_pass(span, noise, right_side, halo, image, left, right, first, keep)
+    part, left2, second = remote_call(
+        finish_kernel, (part, resid, inverse, norms, noise), (f32(right_side.shape), edge, f32((8, 128))), [held] * 2, 1
+    )
     parts = rows // HALO
     return local_call(
         last_kernel, (right_side, image, left, part, left2, first, second),

time: 93.4 us -> 102 us (1.092)
  Pallas kernels: 87.3 us -> 98 us
  local copies, waits for them, and re-layouts: 5.17 us -> 2.88 us
    pallas_call x2, Pallas kernels: 35.8 us -> 45.7 us  [remote_call(): pl.pallas_call(kernel, out_shape=out_shape, in_specs=[VMEM] * len(operand...]
    unnamed x16 -> x8, local copies, waits for them, and re-layouts: 5.17 us -> 2.88 us
where the time goes in v5:
time: 102 us
  Pallas kernels  98 us (96%)
  local copies, waits for them, and re-layouts  2.88 us (3%)
    pallas_call x2, Pallas kernels, remote_call(): pl.pallas_call(kernel, out_shape=out_shape, in_specs=[VMEM] * len(operand...  45.7 us
    pallas_call x3, Pallas kernels, local_call(): pl.pallas_call(kernel, out_shape=out_shape, in_specs=[SMEM] * smalls + [V...  44.5 us
    pallas_call x1, Pallas kernels, start(): pl.pallas_call(start_kernel, out_shape=(f32((8, (rows + HALO) * SUP)), f3...  7.74 us
    unnamed x8, local copies, waits for them, and re-layouts  2.88 us

profile of v5, /device:TPU:1, one launch (start us, length us, event | category | flops | bytes accessed | tf_op | source)
XLA Modules:
  0.0 101.6 jit_solution(2254761827698175266)
XLA Ops:
  0.6 0.0 copy-start
  0.6 1.2 %copy-done = f32[32,8192]{1,0:T(8,128)S(1)} copy-done((f32[32,8192]{1,0:T(8,128)S(1)}, f32[32,8192]{1,0:T(8,128)}, u32[]{:S(2)}) %copy-start) | copy-done | bytes 1048600
  1.9 0.0 copy-start.3
  1.9 0.9 copy-done.3
  2.8 0.0 copy-start.2
  2.8 7.7 %shard_map.50 = (f32[8,10240]{1,0:T(8,128)S(1)}, f32[32,2048]{1,0:T(8,128)S(1)}, s32[8,128]{1,0:T(8,128)S(1)}, f32[32,3,256,128]{3,2,1,0:T(8,128)S(1)}, f32[32,8192]{1,0:T(8,128)S(1)}) custom-call(f32[3,8192]{1,0:T(4,128)S(1)} %copy-done.3, f32[32,8192]{1,0:T(8,128)S(1)} %copy-done), custom_call_target="tpu_custom_call" | custom-call | tf_op jit(solution)/shard_map/pallas_call | solution.py:595
  10.5 0.0 copy-start.1
  10.5 0.7 copy-done.1
  11.3 28.2 %shard_map.51 = (f32[32,10496]{1,0:T(8,128)S(1)}, f32[8,128]{1,0:T(8,128)S(1)}, bf16[36,8,256,256]{3,2,1,0:T(8,128)(2,1)}, f8e4m3fn[36,8,256,256]{3,2,1,0:T(32,128)(4,1)}) custom-call(s32[8,128]{1,0:T(8,128)S(1)} %get-tuple-element.22.span_ref, f32[8,10240]{1,0:T(8,128)S(1)} %get-tuple-element.23.pos_ref, ...), custom_call_target="tpu_custom_call" | custom-call | tf_op jit(solution)/shard_map/pallas_call | solution.py:361
  39.5 29.0 %shard_map.52 = (f32[32,2048]{1,0:T(8,128)S(1)}, f32[32,2048]{1,0:T(8,128)S(1)}, f32[8,128]{1,0:T(8,128)S(1)}) custom-call(f32[32,10496]{1,0:T(8,128)S(1)} %get-tuple-element.26.part_ref.image_ref, f32[8,128]{1,0:T(8,128)S(1)} %get-tuple-element.27.sums_ref), custom_call_target="tpu_custom_call" | custom-call | tf_op jit(solution)/shard_map/pallas_call | solution.py:478
  68.5 0.0 copy-done.2
  68.5 14.7 %shard_map.53 = (f32[32,10496]{1,0:T(8,128)S(1)}, f32[32,10240]{1,0:T(8,128)S(1)}, f32[32,256]{1,0:T(8,128)S(1)}, f32[2,32,128]{2,1,0:T(8,128)S(1)}) custom-call(s32[8,128]{1,0:T(8,128)S(1)} %get-tuple-element.22.span_ref, f32[1,8192]{1,0:T(1,128)S(1)} %bitcast.2, f32[32,8192]{1,0:T(8,128)S(1)} %get-tuple-element.21.own_ref, ...), custom_call_target="tpu_custom_call" | custom-call | tf_op jit(solution)/shard_map/pallas_call | solution.py:361
  83.2 16.8 %shard_map.54 = (f32[32,8192]{1,0:T(8,128)S(1)}, f32[32,2048]{1,0:T(8,128)S(1)}, f32[8,128]{1,0:T(8,128)S(1)}) custom-call(f32[32,10496]{1,0:T(8,128)S(1)} %get-tuple-element.33.part_ref, f32[32,10240]{1,0:T(8,128)S(1)} %get-tuple-element.34.resid_ref, f32[32,256]{1,0:T(8,128)S(1)} %get-tuple-element.35.inverse_ref, ...), custom_call_target="tpu_custom_call" | custom-call | tf_op jit(solution)/shard_map/pallas_call | solution.py:478
  99.9 1.6 %shard_map.55 = (f32[32,8192]{1,0:T(8,128)}, f32[32,8192]{1,0:T(8,128)}) custom-call(f32[32,8192]{1,0:T(8,128)S(1)} %get-tuple-element.21.own_ref, f32[32,10496]{1,0:T(8,128)S(1)} %get-tuple-element.26.part_ref.image_ref, f32[32,2048]{1,0:T(8,128)S(1)} %get-tuple-element.28.left_ref, f32[32,8192]{1,0:T(8,128)S(1)} %get-tuple-element.37.part_ref, ...), custom_call_target="tpu_custom_call" | custom-call | tf_op jit(solution)/shard_map/pallas_call | solution.py:361
Async XLA Ops:
  0.6 1.2 %copy-start = (f32[32,8192]{1,0:T(8,128)S(1)}, f32[32,8192]{1,0:T(8,128)}, u32[]{:S(2)}) copy-start(f32[32,8192]{1,0:T(8,128)} %own_any.1) | copy-start | bytes 3145732
  1.9 0.9 copy-start.3
  2.8 65.7 %copy-start.2 = (f32[8192]{0:T(1024)S(1)}, f32[8192]{0:T(1024)}, u32[]{:S(2)}) copy-start(f32[8192]{0:T(1024)} %param.6) | copy-start | bytes 98308
  10.5 0.8 copy-start.1

commit v6 on v5

--- a/solution.py
+++ b/solution.py
@@ -14,7 +14,7 @@
 ANY = pl.BlockSpec(memory_space=pl.ANY)
 SMEM = pl.BlockSpec(memory_space=pltpu.SMEM)
 AHEAD = 3
-BATCH = 8
+BATCH = 16
 EIGHT = jnp.float8_e4m3fn
 UNIT = 8.0
 KERNEL = UNIT**5 / 4
@@ -145,7 +145,7 @@
         for u in range(BATCH):
             a, c = now
             high, low = kernel_tile(pos_ref, rows_ref, a, c, highs.at[slot, u], lows.at[slot, u])
-            products(vals_ref, out_ref, a, c, high, low, BATCH * g + u < total)
+            products(vals_ref, out_ref, a, c, highs[slot, u], lows[slot, u], BATCH * g + u < total)
             now = following(a, c)
         for copy in moves(tiles, keep, g, 2, True):
             copy.start()
@@ -356,7 +356,7 @@
     )
 
 
-def local_call(kernel, operands, out_shape, scratch, smalls, anys=0, any_outs=0, mib=28):
+def local_call(kernel, operands, out_shape, scratch, smalls, anys=0, any_outs=0, mib=32):
     plain = len(operands) - smalls - anys
     return pl.pallas_call(
         kernel,
@@ -399,20 +399,19 @@
 
 
 def sum_over_devices(total, mine, slots, sems, edges):
-    offset = 0
     for stage, peers in enumerate(partners()):
         mine[stage, 0:1] = total
-        copies = [
-            send(mine.at[stage, pl.ds(0, 1)], slots.at[offset + k, pl.ds(0, 1)], sems, offset + k, peer)
-            for k, peer in enumerate(peers)
-        ]
+        for k, peer in enumerate(peers):
+            pltpu.make_async_remote_copy(
+                src_ref=mine.at[stage, pl.ds(0, 1)], dst_ref=slots.at[stage, pl.ds(k, 1)],
+                send_sem=sems.at[0, stage], recv_sem=sems.at[1, stage], device_id=(peer,), device_id_type=MESH,
+            ).start()
         if stage == 0:
             edges()
-        for copy in copies:
-            copy.wait()
-        for k in range(len(peers)):
-            total = total + slots[offset + k, 0:1]
-        offset += len(peers)
+        rows = slots.at[stage, pl.ds(0, len(peers))]
+        for side in range(2):
+            pltpu.make_async_copy(rows, rows, sems.at[side, stage]).wait()
+        total = total + jnp.sum(slots[stage, 0 : len(peers)], axis=0, keepdims=True)
     return total
 
 
@@ -474,7 +473,7 @@
 
 
 def remote_call(kernel, operands, out_shape, scratch, collective_id):
-    partners_count = GROUP - 1 + lax.axis_size("pts") // GROUP - 1
+    most = -(-lax.axis_size("pts") // GROUP // 8) * 8
     return pl.pallas_call(
         kernel,
         out_shape=out_shape,
@@ -482,10 +481,10 @@
         out_specs=(VMEM,) * len(out_shape),
         scratch_shapes=scratch
         + [
-            pltpu.VMEM((partners_count, 8, 128), jnp.float32),
+            pltpu.VMEM((2, most, 128), jnp.float32),
             pltpu.VMEM((2, 8, 128), jnp.float32),
             pltpu.SemaphoreType.DMA((2, 2)),
-            pltpu.SemaphoreType.DMA((2, partners_count)),
+            pltpu.SemaphoreType.DMA((2, 2)),
         ],
         compiler_params=pltpu.CompilerParams(
             collective_id=collective_id, has_side_effects=True, vmem_limit_bytes=16 * 2**20

time: 102 us -> 89.3 us (0.88)
  Pallas kernels: 98 us -> 85.4 us
    pallas_call x2, Pallas kernels: 45.7 us -> 37.1 us  [remote_call(): pl.pallas_call(kernel, out_shape=out_shape, in_specs=[VMEM] * len(operand...]
    pallas_call x3, Pallas kernels: 44.5 us -> 40.5 us  [local_call(): pl.pallas_call(kernel, out_shape=out_shape, in_specs=[SMEM] * smalls + [V...]
where the time goes in v6:
time: 89.3 us; the launch traced here: 88.9 us
  Pallas kernels  85.4 us (96%)
  local copies, waits for them, and re-layouts  2.88 us (3%)
    pallas_call x3, Pallas kernels, local_call(): pl.pallas_call(kernel, out_shape=out_shape, in_specs=[SMEM] * smalls + [V...  40.5 us
    pallas_call x2, Pallas kernels, remote_call(): pl.pallas_call(kernel, out_shape=out_shape, in_specs=[VMEM] * len(operand...  37.1 us
    pallas_call x1, Pallas kernels, start(): pl.pallas_call(start_kernel, out_shape=(f32((8, (rows + HALO) * SUP)), f3...  7.74 us
    unnamed x8, local copies, waits for them, and re-layouts  2.88 us

profile of v6, /device:TPU:1, one launch (start us, length us, event | category | flops | bytes accessed | tf_op | source)
XLA Modules:
  0.0 88.9 jit_solution(16572147215276830164)
XLA Ops:
  0.6 0.0 copy-start
  0.6 1.2 %copy-done = f32[32,8192]{1,0:T(8,128)S(1)} copy-done((f32[32,8192]{1,0:T(8,128)S(1)}, f32[32,8192]{1,0:T(8,128)}, u32[]{:S(2)}) %copy-start) | copy-done | bytes 1048600
  1.9 0.0 copy-start.3
  1.9 0.9 %copy-done.3 = f32[3,8192]{1,0:T(4,128)S(1)} copy-done((f32[3,8192]{1,0:T(4,128)S(1)}, f32[3,8192]{1,0:T(4,128)}, u32[]{:S(2)}) %copy-start.3) | copy-done | bytes 98328
  2.8 0.0 copy-start.2
  2.8 7.7 %shard_map.50 = (f32[8,10240]{1,0:T(8,128)S(1)}, f32[32,2048]{1,0:T(8,128)S(1)}, s32[8,128]{1,0:T(8,128)S(1)}, f32[32,3,256,128]{3,2,1,0:T(8,128)S(1)}, f32[32,8192]{1,0:T(8,128)S(1)}) custom-call(f32[3,8192]{1,0:T(4,128)S(1)} %copy-done.3, f32[32,8192]{1,0:T(8,128)S(1)} %copy-done), custom_call_target="tpu_custom_call" | custom-call | tf_op jit(solution)/shard_map/pallas_call | solution.py:594
  10.5 0.0 copy-start.1
  10.5 0.7 copy-done.1
  11.3 25.4 %shard_map.51 = (f32[32,10496]{1,0:T(8,128)S(1)}, f32[8,128]{1,0:T(8,128)S(1)}, bf16[18,16,256,256]{3,2,1,0:T(8,128)(2,1)}, f8e4m3fn[18,16,256,256]{3,2,1,0:T(32,128)(4,1)}) custom-call(s32[8,128]{1,0:T(8,128)S(1)} %get-tuple-element.22.span_ref, f32[8,10240]{1,0:T(8,128)S(1)} %get-tuple-element.23.pos_ref, ...), custom_call_target="tpu_custom_call" | custom-call | tf_op jit(solution)/shard_map/pallas_call | solution.py:361
  36.7 22.1 %shard_map.52 = (f32[32,2048]{1,0:T(8,128)S(1)}, f32[32,2048]{1,0:T(8,128)S(1)}, f32[8,128]{1,0:T(8,128)S(1)}) custom-call(f32[32,10496]{1,0:T(8,128)S(1)} %get-tuple-element.26.part_ref.image_ref, f32[8,128]{1,0:T(8,128)S(1)} %get-tuple-element.27.sums_ref), custom_call_target="tpu_custom_call" | custom-call | tf_op jit(solution)/shard_map/pallas_call | solution.py:477
  58.8 0.0 copy-done.2
  58.8 13.4 %shard_map.53 = (f32[32,10496]{1,0:T(8,128)S(1)}, f32[32,10240]{1,0:T(8,128)S(1)}, f32[32,256]{1,0:T(8,128)S(1)}, f32[2,32,128]{2,1,0:T(8,128)S(1)}) custom-call(s32[8,128]{1,0:T(8,128)S(1)} %get-tuple-element.22.span_ref, f32[1,8192]{1,0:T(1,128)S(1)} %bitcast.2, f32[32,8192]{1,0:T(8,128)S(1)} %get-tuple-element.21.own_ref, ...), custom_call_target="tpu_custom_call" | custom-call | tf_op jit(solution)/shard_map/pallas_call | solution.py:361
  72.2 15.1 %shard_map.54 = (f32[32,8192]{1,0:T(8,128)S(1)}, f32[32,2048]{1,0:T(8,128)S(1)}, f32[8,128]{1,0:T(8,128)S(1)}) custom-call(f32[32,10496]{1,0:T(8,128)S(1)} %get-tuple-element.33.part_ref, f32[32,10240]{1,0:T(8,128)S(1)} %get-tuple-element.34.resid_ref, f32[32,256]{1,0:T(8,128)S(1)} %get-tuple-element.35.inverse_ref, ...), custom_call_target="tpu_custom_call" | custom-call | tf_op jit(solution)/shard_map/pallas_call | solution.py:477
  87.3 1.6 %shard_map.55 = (f32[32,8192]{1,0:T(8,128)}, f32[32,8192]{1,0:T(8,128)}) custom-call(f32[32,8192]{1,0:T(8,128)S(1)} %get-tuple-element.21.own_ref, f32[32,10496]{1,0:T(8,128)S(1)} %get-tuple-element.26.part_ref.image_ref, f32[32,2048]{1,0:T(8,128)S(1)} %get-tuple-element.28.left_ref, f32[32,8192]{1,0:T(8,128)S(1)} %get-tuple-element.37.part_ref, ...), custom_call_target="tpu_custom_call" | custom-call | tf_op jit(solution)/shard_map/pallas_call | solution.py:361
Async XLA Ops:
  0.6 1.2 %copy-start = (f32[32,8192]{1,0:T(8,128)S(1)}, f32[32,8192]{1,0:T(8,128)}, u32[]{:S(2)}) copy-start(f32[32,8192]{1,0:T(8,128)} %own_any.1) | copy-start | bytes 3145732
  1.9 0.9 %copy-start.3 = (f32[3,8192]{1,0:T(4,128)S(1)}, f32[3,8192]{1,0:T(4,128)}, u32[]{:S(2)}) copy-start(f32[3,8192]{1,0:T(4,128)} %positions_any.1) | copy-start | bytes 294916
  2.8 56.0 %copy-start.2 = (f32[8192]{0:T(1024)S(1)}, f32[8192]{0:T(1024)}, u32[]{:S(2)}) copy-start(f32[8192]{0:T(1024)} %param.6) | copy-start | bytes 98308
  10.5 0.8 copy-start.1

commit v7 on v6

--- a/solution.py
+++ b/solution.py
@@ -69,52 +69,84 @@
     high_ref[a] = jnp.concatenate([high, low], axis=0)
 
 
-def follower(span_ref, rows):
-    def following(a, c):
-        last = c >= a + span_ref[0, a]
-        a_next = jnp.minimum(jnp.where(last, a + 1, a), rows - 1)
-        return a_next, jnp.where(last, a_next, c + 1)
-
-    return following
-
-
-def kernel_tile(pos_ref, rows_ref, a, c, high_ref, low_ref):
-    highs, lows = [], []
-    step = 32
-    for i in range(0, SUP, step):
-        pair = []
-        for h in range(2):
-            dist2 = None
-            for axis in range(3):
-                col = pos_ref[axis : axis + 1, pl.ds(pl.multiple_of(c * SUP + h * 128, 128), 128)]
-                diff = rows_ref[a, axis, i : i + step, :] - col
-                dist2 = diff * diff if axis == 0 else dist2 + diff * diff
-            dist2 = jnp.maximum(dist2, TINY)
-            reach = jnp.maximum(UNIT - dist2 * lax.rsqrt(dist2), 0.0)
-            square = reach * reach
-            kern = square * square * (1.25 * UNIT - reach)
-            high = kern.astype(jnp.bfloat16)
-            pair.append((high, (kern - high.astype(jnp.float32)).astype(EIGHT)))
-        highs.append(jnp.concatenate([p[0] for p in pair], axis=1))
-        lows.append(jnp.concatenate([p[1] for p in pair], axis=1))
-        high_ref[i : i + step, :] = highs[-1]
-        low_ref[i : i + step, :] = lows[-1]
-    return jnp.concatenate(highs, axis=0), jnp.concatenate(lows, axis=0)
-
-
-def products(vals_ref, out_ref, a, c, high, low, valid):
+def visited(span_ref, a, before):
+    return (span_ref[0, a] > 0) | jnp.logical_not(before)
+
+
+def pair_count(span_ref, rows):
+    def step(a, carry):
+        count, before = carry
+        here = visited(span_ref, a, before)
+        return count + jnp.where(here, jnp.maximum(span_ref[0, a], 1), 0), here
+
+    return lax.fori_loop(0, rows, step, (jnp.int32(0), True))[0]
+
+
+def first_pair(span_ref):
+    a = jnp.where(span_ref[0, 0] > 0, 0, 1)
+    return a, a + 1
+
+
+def following(span_ref, rows, a, c):
+    last = c >= a + span_ref[0, a]
+    after = jnp.minimum(jnp.where(span_ref[0, a + 1] > 0, a + 1, a + 2), rows - 1)
+    a_next = jnp.where(last, after, a)
+    return a_next, jnp.where(last, after, c) + 1
+
+
+def kernel_part(pos_ref, rows_ref, a, c, i, step, h):
+    dist2 = None
+    for axis in range(3):
+        col = pos_ref[axis : axis + 1, pl.ds(pl.multiple_of(c * SUP + h * 128, 128), 128)]
+        diff = rows_ref[a, axis, i : i + step, :] - col
+        dist2 = diff * diff if axis == 0 else dist2 + diff * diff
+    dist2 = jnp.maximum(dist2, TINY)
+    reach = jnp.maximum(UNIT - dist2 * lax.rsqrt(dist2), 0.0)
+    square = reach * reach
+    return square * square * (1.25 * UNIT - reach)
+
+
+def put(tile, i, step, kerns):
+    highs = [kern.astype(jnp.bfloat16) for kern in kerns]
+    lows = [(kern - high.astype(jnp.float32)).astype(EIGHT) for kern, high in zip(kerns, highs)]
+    tile[0][i : i + step, :] = jnp.concatenate(highs, axis=1)
+    tile[1][i : i + step, :] = jnp.concatenate(lows, axis=1)
+
+
+def pair_tile(pos_ref, rows_ref, a, c, tile):
+    for i in range(0, SUP, 32):
+        put(tile, i, 32, [kernel_part(pos_ref, rows_ref, a, c, i, 32, h) for h in range(2)])
+
+
+def own_tile(pos_ref, rows_ref, a, tile):
+    quarter = []
+    for i in range(0, 128, 32):
+        quarter.append(kernel_part(pos_ref, rows_ref, a, a, i, 32, 1))
+        put(tile, i, 32, [kernel_part(pos_ref, rows_ref, a, a, i, 32, 0), quarter[-1]])
+    turned = jnp.transpose(jnp.concatenate(quarter, axis=0))
+    for i in range(0, 128, 32):
+        put(tile, 128 + i, 32, [turned[i : i + 32], kernel_part(pos_ref, rows_ref, a, a, 128 + i, 32, 1)])
+
+
+def product(vals_ref, a, tile, dim):
     high_ref, low_ref = vals_ref
-    front = dot(high_ref[c], high, 1)
-    front = front[:FRAMES] + front[FRAMES:] + dot(low_ref[c], low, 1)
-    back = dot(high_ref[a], high, 0)
-    back = back[:FRAMES] + back[FRAMES:] + dot(low_ref[a], low, 0)
+    both = dot(high_ref[a], tile[0][...], dim)
+    return both[:FRAMES] + both[FRAMES:] + dot(low_ref[a], tile[1][...], dim)
+
+
+def pair_products(vals_ref, out_ref, a, c, tile, valid):
+    front, back = product(vals_ref, c, tile, 1), product(vals_ref, a, tile, 0)
     unused = out_ref.shape[1] // SUP - 1
     out_ref[:, lanes(jnp.where(valid, a, unused))] += front
-    out_ref[:, lanes(jnp.where(valid & (a != c), c, unused))] += back
-
-
-def group_count(total):
-    return (total + BATCH - 1) // BATCH
+    out_ref[:, lanes(jnp.where(valid, c, unused))] += back
+
+
+def own_products(vals_ref, out_ref, a, tile):
+    out_ref[:, lanes(a)] += product(vals_ref, a, tile, 0)
+
+
+def group_count(span_ref, rows):
+    return rows // BATCH + (pair_count(span_ref, rows) + BATCH - 1) // BATCH
 
 
 def moves(tiles, keep, g, slots, save):
@@ -128,34 +160,60 @@
     return out
 
 
+def each_tile(span_ref, rows, tiles, slots, groups, begin, own, pair, end):
+    highs, lows = tiles[0]
+    count = pair_count(span_ref, rows)
+
+    def tile(g, u):
+        slot = lax.rem(g, slots)
+        return highs.at[slot, u], lows.at[slot, u]
+
+    def own_step(g, _):
+        begin(g)
+        for u in range(BATCH):
+            own(g * BATCH + u, tile(g, u))
+        end(g)
+        return 0
+
+    lax.fori_loop(0, rows // BATCH, own_step, 0)
+
+    def pair_step(g, now):
+        begin(g)
+        for u in range(BATCH):
+            a, c = now
+            valid = ((g - rows // BATCH) * BATCH + u < count) & (c <= a + span_ref[0, a])
+            pair(a, c, tile(g, u), valid)
+            now = following(span_ref, rows, a, c)
+        end(g)
+        return now
+
+    lax.fori_loop(rows // BATCH, groups, pair_step, first_pair(span_ref))
+
+
 def sweep(span_ref, pos_ref, rows_ref, vals_ref, out_ref, rows, keep, tiles):
-    total = span_ref[0, rows]
-    groups = group_count(total)
-    following = follower(span_ref, rows)
-    highs, lows = tiles[0]
-
-    def step(g, now):
-        slot = lax.rem(g, 2)
-
+    def begin(g):
         @pl.when(g >= 2)
         def _():
             for copy in moves(tiles, keep, g - 2, 2, True):
                 copy.wait()
 
-        for u in range(BATCH):
-            a, c = now
-            high, low = kernel_tile(pos_ref, rows_ref, a, c, highs.at[slot, u], lows.at[slot, u])
-            products(vals_ref, out_ref, a, c, highs[slot, u], lows[slot, u], BATCH * g + u < total)
-            now = following(a, c)
+    def end(g):
         for copy in moves(tiles, keep, g, 2, True):
             copy.start()
-        return now
-
-    lax.fori_loop(0, groups, step, (jnp.int32(0), jnp.int32(0)))
+
+    def own(a, tile):
+        own_tile(pos_ref, rows_ref, a, tile)
+        own_products(vals_ref, out_ref, a, tile)
+
+    def pair(a, c, tile, valid):
+        pair_tile(pos_ref, rows_ref, a, c, tile)
+        pair_products(vals_ref, out_ref, a, c, tile, valid)
+
+    each_tile(span_ref, rows, tiles, 2, group_count(span_ref, rows), begin, own, pair, end)
 
 
 def settle(span_ref, rows, keep, tiles):
-    groups = group_count(span_ref[0, rows])
+    groups = group_count(span_ref, rows)
     for k in (2, 1):
         @pl.when(groups >= k)
         def _():
@@ -173,23 +231,18 @@
                 copy.wait()
 
 
-def sweep_again(span_ref, rows, vals_ref, out_ref, keep, tiles):
-    total = span_ref[0, rows]
-    groups = group_count(total)
-    following = follower(span_ref, rows)
-    highs, lows = tiles[0]
-
-    def step(g, now):
-        slot = lax.rem(g, AHEAD + 1)
+def sweep_again(span_ref, rows, groups, vals_ref, out_ref, keep, tiles):
+    def begin(g):
         fetch(keep, groups, tiles, g + AHEAD, True)
         fetch(keep, groups, tiles, g, False)
-        for u in range(BATCH):
-            a, c = now
-            products(vals_ref, out_ref, a, c, highs[slot, u], lows[slot, u], BATCH * g + u < total)
-            now = following(a, c)
-        return now
-
-    lax.fori_loop(0, groups, step, (jnp.int32(0), jnp.int32(0)))
+
+    def own(a, tile):
+        own_products(vals_ref, out_ref, a, tile)
+
+    def pair(a, c, tile, valid):
+        pair_products(vals_ref, out_ref, a, c, tile, valid)
+
+    each_tile(span_ref, rows, tiles, AHEAD + 1, groups, begin, own, pair, lambda g: None)
 
 
 def lane_totals(quantities):
@@ -277,8 +330,9 @@
 ):
     vals_ref, tiles, keep = (high_ref, low_ref), (stage[:2], stage[2]), (keep_high, keep_low)
     rows = own_ref.shape[1] // SUP
+    groups = group_count(span_ref, rows)
     for g in range(AHEAD):
-        fetch(keep, group_count(span_ref[0, rows]), tiles, g, True)
+        fetch(keep, groups, tiles, g, True)
     norm_before, curve_before = frame_columns(first_ref[0:1])[:2]
     alpha = wide(norm_before / curve_before)
 
@@ -312,7 +366,7 @@
 
     loop(0, rows + HALO, ready, 0)
     clear(out_ref, 0, rows + HALO)
-    sweep_again(span_ref, rows, vals_ref, out_ref, keep, tiles)
+    sweep_again(span_ref, rows, groups, vals_ref, out_ref, keep, tiles)
     inverse_ref[...] = 1.0 / (KERNEL * scale)
     sums_ref[0], sums_ref[1] = norm, cross
 
@@ -333,7 +387,7 @@
 
 
 def kept(rows):
-    steps = -(-rows * (HALO + 1) // BATCH)
+    steps = rows // BATCH - (-rows * HALO // BATCH)
     shape = (steps, BATCH, SUP, SUP)
     return jax.ShapeDtypeStruct(shape, jnp.bfloat16), jax.ShapeDtypeStruct(shape, EIGHT)
 
@@ -534,8 +588,7 @@
         gap = jnp.maximum(jnp.maximum(low_k - high, low - high_k), 0.0)
         near = (jnp.sum(gap * gap, axis=0, keepdims=True) < UNIT * UNIT) & (lane + k < limit)
         span = jnp.where(near, k, span)
-    pairs = jnp.sum(jnp.where(lane < rows, span + 1, 0), axis=1, keepdims=True)
-    return jnp.broadcast_to(jnp.where(lane == rows, pairs, span), (8, 128))
+    return jnp.broadcast_to(jnp.where(lane < rows, span, 0), (8, 128))
 
 
 def start_kernel(

time: 89.3 us -> 86.6 us (0.970)
  Pallas kernels: 85.4 us -> 82 us
    pallas_call x2, Pallas kernels: 37.1 us -> 31 us  [remote_call(): pl.pallas_call(kernel, out_shape=out_shape, in_specs=[VMEM] * len(operand...]
    pallas_call x3, Pallas kernels: 40.5 us -> 43.4 us  [local_call(): pl.pallas_call(kernel, out_shape=out_shape, in_specs=[SMEM] * smalls + [V...]
where the time goes in v7:
time: 86.6 us; the launch traced here: 85.6 us
  Pallas kernels  82 us (95%)
  local copies, waits for them, and re-layouts  2.88 us (3%)
    pallas_call x3, Pallas kernels, local_call(): pl.pallas_call(kernel, out_shape=out_shape, in_specs=[SMEM] * smalls + [V...  43.4 us
    pallas_call x2, Pallas kernels, remote_call(): pl.pallas_call(kernel, out_shape=out_shape, in_specs=[VMEM] * len(operand...  31 us
    pallas_call x1, Pallas kernels, start(): pl.pallas_call(start_kernel, out_shape=(f32((8, (rows + HALO) * SUP)), f3...  7.66 us
    unnamed x8, local copies, waits for them, and re-layouts  2.88 us

profile of v7, /device:TPU:1, one launch (start us, length us, event | category | flops | bytes accessed | tf_op | source)
XLA Modules:
  0.0 85.6 jit_solution(8005773537295261304)
XLA Ops:
  0.6 0.0 copy-start
  0.6 1.2 %copy-done = f32[32,8192]{1,0:T(8,128)S(1)} copy-done((f32[32,8192]{1,0:T(8,128)S(1)}, f32[32,8192]{1,0:T(8,128)}, u32[]{:S(2)}) %copy-start) | copy-done | bytes 1048600
  1.9 0.0 copy-start.3
  1.9 0.9 %copy-done.3 = f32[3,8192]{1,0:T(4,128)S(1)} copy-done((f32[3,8192]{1,0:T(4,128)S(1)}, f32[3,8192]{1,0:T(4,128)}, u32[]{:S(2)}) %copy-start.3) | copy-done | bytes 98328
  2.8 0.0 copy-start.2
  2.8 7.7 %shard_map.50 = (f32[8,10240]{1,0:T(8,128)S(1)}, f32[32,2048]{1,0:T(8,128)S(1)}, s32[8,128]{1,0:T(8,128)S(1)}, f32[32,3,256,128]{3,2,1,0:T(8,128)S(1)}, f32[32,8192]{1,0:T(8,128)S(1)}) custom-call(f32[3,8192]{1,0:T(4,128)S(1)} %copy-done.3, f32[32,8192]{1,0:T(8,128)S(1)} %copy-done), custom_call_target="tpu_custom_call" | custom-call | tf_op jit(solution)/shard_map/pallas_call | solution.py:647
  10.4 0.0 copy-start.1
  10.4 0.7 copy-done.1
  11.2 27.8 %shard_map.51 = (f32[32,10496]{1,0:T(8,128)S(1)}, f32[8,128]{1,0:T(8,128)S(1)}, bf16[18,16,256,256]{3,2,1,0:T(8,128)(2,1)}, f8e4m3fn[18,16,256,256]{3,2,1,0:T(32,128)(4,1)}) custom-call(s32[8,128]{1,0:T(8,128)S(1)} %get-tuple-element.22.span_ref, f32[8,10240]{1,0:T(8,128)S(1)} %get-tuple-element.23.pos_ref, ...), custom_call_target="tpu_custom_call" | custom-call | tf_op jit(solution)/shard_map/pallas_call | solution.py:415
  39.0 18.4 %shard_map.52 = (f32[32,2048]{1,0:T(8,128)S(1)}, f32[32,2048]{1,0:T(8,128)S(1)}, f32[8,128]{1,0:T(8,128)S(1)}) custom-call(f32[32,10496]{1,0:T(8,128)S(1)} %get-tuple-element.26.part_ref.image_ref, f32[8,128]{1,0:T(8,128)S(1)} %get-tuple-element.27.sums_ref), custom_call_target="tpu_custom_call" | custom-call | tf_op jit(solution)/shard_map/pallas_call | solution.py:531
  57.4 0.0 copy-done.2
  57.4 13.9 %shard_map.53 = (f32[32,10496]{1,0:T(8,128)S(1)}, f32[32,10240]{1,0:T(8,128)S(1)}, f32[32,256]{1,0:T(8,128)S(1)}, f32[2,32,128]{2,1,0:T(8,128)S(1)}) custom-call(s32[8,128]{1,0:T(8,128)S(1)} %get-tuple-element.22.span_ref, f32[1,8192]{1,0:T(1,128)S(1)} %bitcast.2, f32[32,8192]{1,0:T(8,128)S(1)} %get-tuple-element.21.own_ref, ...), custom_call_target="tpu_custom_call" | custom-call | tf_op jit(solution)/shard_map/pallas_call | solution.py:415
  71.4 12.6 %shard_map.54 = (f32[32,8192]{1,0:T(8,128)S(1)}, f32[32,2048]{1,0:T(8,128)S(1)}, f32[8,128]{1,0:T(8,128)S(1)}) custom-call(f32[32,10496]{1,0:T(8,128)S(1)} %get-tuple-element.33.part_ref, f32[32,10240]{1,0:T(8,128)S(1)} %get-tuple-element.34.resid_ref, f32[32,256]{1,0:T(8,128)S(1)} %get-tuple-element.35.inverse_ref, ...), custom_call_target="tpu_custom_call" | custom-call | tf_op jit(solution)/shard_map/pallas_call | solution.py:531
  84.0 1.6 %shard_map.55 = (f32[32,8192]{1,0:T(8,128)}, f32[32,8192]{1,0:T(8,128)}) custom-call(f32[32,8192]{1,0:T(8,128)S(1)} %get-tuple-element.21.own_ref, f32[32,10496]{1,0:T(8,128)S(1)} %get-tuple-element.26.part_ref.image_ref, f32[32,2048]{1,0:T(8,128)S(1)} %get-tuple-element.28.left_ref, f32[32,8192]{1,0:T(8,128)S(1)} %get-tuple-element.37.part_ref, ...), custom_call_target="tpu_custom_call" | custom-call | tf_op jit(solution)/shard_map/pallas_call | solution.py:415
Async XLA Ops:
  0.6 1.2 %copy-start = (f32[32,8192]{1,0:T(8,128)S(1)}, f32[32,8192]{1,0:T(8,128)}, u32[]{:S(2)}) copy-start(f32[32,8192]{1,0:T(8,128)} %own_any.1) | copy-start | bytes 3145732
  1.9 0.9 %copy-start.3 = (f32[3,8192]{1,0:T(4,128)S(1)}, f32[3,8192]{1,0:T(4,128)}, u32[]{:S(2)}) copy-start(f32[3,8192]{1,0:T(4,128)} %positions_any.1) | copy-start | bytes 294916
  2.8 54.7 %copy-start.2 = (f32[8192]{0:T(1024)S(1)}, f32[8192]{0:T(1024)}, u32[]{:S(2)}) copy-start(f32[8192]{0:T(1024)} %param.6) | copy-start | bytes 98308
  10.4 0.8 copy-start.1
